TPU v7x, 128 devices: a whole 4x4x4 slice. The times are simulated.
128 devices in a mesh: sec: 2 (over y_hi), gz: 16 (over y_lo, x, core), gx: 4 (over z).
Axes of the slice: x: 4, y: 4 (y_hi: 2, y_lo: 2; y = y_hi * 2 + y_lo), z: 4, core: 2. Of those that a mesh axis runs over, the one named last changes fastest.
Arguments:
- velocity: float32 [3, 32, 64, 2048], P(None, 'gx', 'sec', 'gz'), may hold values from -6 to 6
- test_fields: float32 [4, 3, 32, 64, 2048], P('sec', None, 'gx', None, 'gz'), may hold values from -6 to 6
Outputs:
- velocity_next: float32 [3, 32, 64, 2048], P(None, 'gx', 'sec', 'gz')
- test_next: float32 [4, 3, 32, 64, 2048], P('sec', None, 'gx', None, 'gz')
All inputs are finite; a program needn't handle non-finite values.
Results may differ from a plain program's by a relative error of at most 0.0001.
Values sent between devices are 32-bit elements; how exact they have to be, the bound alone decides.
No kernel may reach another device: no remote copies, remote signals or barrier semaphores. Data moves between devices by JAX's collectives and lax.ppermute only.
A program may use at most 128 MiB of HBM per device.

v0:
```python
import math

import jax
import jax.numpy as jnp
from jax import lax
from jax.sharding import PartitionSpec as P

ALPHA_LEFT = 1.0 / 3.0
COEF_NEAR = 14.0 / 9.0
COEF_FAR = 1.0 / 9.0
TIME_STEP = 0.2
VISCOSITY = 0.1
DIFFUSIVITY = 0.1
FORCE_AMPLITUDE = 1.0


def passed_along(block, axis, distance):
    devices = range(lax.axis_size(axis))
    route = [((i - distance) % len(devices), i) for i in devices]
    return lax.ppermute(block, axis, route)


def with_halo(cells, sides, width):
    for axis, dim in sides:
        count = lax.axis_size(axis)
        head = lax.slice_in_dim(cells, 0, width, axis=dim)
        tail = lax.slice_in_dim(cells, cells.shape[dim] - width, cells.shape[dim], axis=dim)
        cells = jnp.concatenate(
            [
                lax.ppermute(tail, axis, [(i, (i + 1) % count) for i in range(count)]),
                cells,
                lax.ppermute(head, axis, [((i + 1) % count, i) for i in range(count)]),
            ],
            axis=dim,
        )
    return cells


def green_table(length):
    rows = lax.broadcasted_iota(jnp.int32, (length, length), 0)
    columns = lax.broadcasted_iota(jnp.int32, (length, length), 1)
    radius = 1.0 - 4.0 * ALPHA_LEFT * ALPHA_LEFT
    decay = (1.0 - math.sqrt(radius)) / (2.0 * ALPHA_LEFT)

    def signed_power(exponent):
        parity = 1.0 - 2.0 * (exponent % 2).astype(jnp.float32)
        return parity * jnp.exp(exponent.astype(jnp.float32) * math.log(decay))

    return (
        signed_power(jnp.abs(rows - columns))
        - signed_power(rows + columns + 2)
        - signed_power(2 * length - rows - columns)
    ) / math.sqrt(radius)


def along(values, offset, axis_dim, length):
    return lax.slice_in_dim(values, 3 + offset, 3 + offset + length, axis=axis_dim)


def trimmed(values, axes_list):
    for axis_dim in axes_list:
        values = lax.slice_in_dim(values, 3, values.shape[axis_dim] - 3, axis=axis_dim)
    return values


def first_padded(values, axis_dim, length):

    def shifted(offset):
        return along(values, offset, axis_dim, length)

    return (
        45.0 * (shifted(1) - shifted(-1))
        - 9.0 * (shifted(2) - shifted(-2))
        + (shifted(3) - shifted(-3))
    ) / 60.0


def second_padded(values, axis_dim, length):

    def shifted(offset):
        return along(values, offset, axis_dim, length)

    return (
        2.0 * (shifted(3) + shifted(-3))
        - 27.0 * (shifted(2) + shifted(-2))
        + 270.0 * (shifted(1) + shifted(-1))
        - 490.0 * shifted(0)
    ) / 180.0


def first_rolled(values, axis_dim):

    def shifted(offset):
        return jnp.roll(values, -offset, axis=axis_dim)

    return (
        45.0 * (shifted(1) - shifted(-1))
        - 9.0 * (shifted(2) - shifted(-2))
        + (shifted(3) - shifted(-3))
    ) / 60.0


def second_rolled(values, axis_dim):

    def shifted(offset):
        return jnp.roll(values, -offset, axis=axis_dim)

    return (
        2.0 * (shifted(3) + shifted(-3))
        - 27.0 * (shifted(2) + shifted(-2))
        + 270.0 * (shifted(1) + shifted(-1))
        - 490.0 * values
    ) / 180.0


def compact_dz(padded, length):
    last_dim = padded.ndim - 1

    def shifted(offset):
        return along(padded, offset, last_dim, length)

    source = 0.5 * COEF_NEAR * (shifted(1) - shifted(-1)) + 0.25 * COEF_FAR * (
        shifted(2) - shifted(-2)
    )
    green = green_table(length)
    solved = jnp.dot(source, green.T, precision=lax.Precision.HIGHEST)
    head_corner = green[0, 0]
    tail_corner = green[length - 1, length - 1]
    head = solved[..., 0]
    tail = solved[..., length - 1]
    next_head = passed_along(head, "gz", -1)
    tail_value = (tail - ALPHA_LEFT * tail_corner * next_head) / (
        1.0 - ALPHA_LEFT * ALPHA_LEFT * head_corner * tail_corner
    )
    next_value = next_head - ALPHA_LEFT * head_corner * tail_value
    prior_tail = passed_along(tail_value, "gz", 1)
    return (
        solved
        - ALPHA_LEFT * prior_tail[..., None] * green[:, 0]
        - ALPHA_LEFT * next_value[..., None] * green[:, length - 1]
    )


def drive_field(x_index, y_index, cells_x, cells_y):
    phase_x = 2.0 * math.pi / cells_x * x_index.astype(jnp.float32)[:, None]
    phase_y = 2.0 * math.pi / cells_y * y_index.astype(jnp.float32)[None, :]
    stacked = jnp.stack(
        [
            jnp.sin(phase_x) * jnp.cos(phase_y),
            -jnp.cos(phase_x) * jnp.sin(phase_y),
            math.sqrt(2.0) * jnp.sin(phase_x) * jnp.sin(phase_y),
        ]
    )
    return FORCE_AMPLITUDE * stacked[..., None]


def mean_field(z_index, z_total, section):
    angle = 2.0 * math.pi / z_total * (z_index % z_total).astype(jnp.float32)
    waves = jnp.stack([jnp.cos(angle), jnp.sin(angle)])
    component_mask = (jnp.arange(3, dtype=jnp.int32) == section).astype(jnp.float32)
    return waves[:, None, None, None, :] * component_mask[None, :, None, None, None]


def cross_field(centred, total):
    return jnp.stack(
        [
            centred[1] * total[:, 2] - centred[2] * total[:, 1],
            centred[2] * total[:, 0] - centred[0] * total[:, 2],
            centred[0] * total[:, 1] - centred[1] * total[:, 0],
        ],
        axis=1,
    )


def shards(velocity, test_fields):
    x_cells = velocity.shape[1]
    half_cells = velocity.shape[2]
    z_cells = velocity.shape[3]
    section = lax.axis_index("sec")
    slab_index = lax.axis_index("gz")
    x_total = x_cells * lax.axis_size("gx")
    z_total = z_cells * lax.axis_size("gz")
    padded = with_halo(velocity, (("sec", 2), ("gz", 3), ("gx", 1)), 3)
    along_x = trimmed(padded, (2, 3))
    along_y = trimmed(padded, (1, 3))
    along_z = trimmed(padded, (1, 2))
    grad_x = first_padded(along_x, 1, x_cells)
    grad_y = first_padded(along_y, 2, half_cells)
    grad_z = compact_dz(along_z, z_cells)
    laplace = (
        second_padded(along_x, 1, x_cells)
        + second_padded(along_y, 2, half_cells)
        + second_padded(along_z, 3, z_cells)
    )
    advect = velocity[0:1] * grad_x + velocity[1:2] * grad_y + velocity[2:3] * grad_z
    x_index = lax.axis_index("gx") * x_cells + jnp.arange(x_cells, dtype=jnp.int32)
    y_index = section * half_cells + jnp.arange(half_cells, dtype=jnp.int32)
    drive = drive_field(x_index, y_index, x_total, half_cells * lax.axis_size("sec"))
    velocity_next = velocity + TIME_STEP * (VISCOSITY * laplace - advect + drive)
    old_whole, new_whole = (
        lax.all_gather(velocity, "sec", axis=2, tiled=True),
        lax.all_gather(velocity_next, "sec", axis=2, tiled=True),
    )
    centred = 0.5 * (old_whole + new_whole)
    z_index = slab_index * z_cells + jnp.arange(z_cells, dtype=jnp.int32)
    cross = cross_field(centred, test_fields + mean_field(z_index, z_total, section))
    cross_pad, tests_pad = (
        with_halo(cross, (("gz", 4), ("gx", 2)), 3),
        with_halo(test_fields, (("gz", 4), ("gx", 2)), 3),
    )
    cross_x = trimmed(cross_pad, (4,))
    cross_z = trimmed(cross_pad, (2,))
    cross_core = trimmed(cross_z, (4,))
    dx_cross = first_padded(cross_x[:, 1:3], 2, x_cells)
    dz_cross = compact_dz(cross_z[:, 0:2], z_cells)
    dy_cross = first_rolled(cross_core, 3)
    curl = jnp.stack(
        [
            dy_cross[:, 2] - dz_cross[:, 1],
            dz_cross[:, 0] - dx_cross[:, 1],
            dx_cross[:, 0] - dy_cross[:, 0],
        ],
        axis=1,
    )
    tests_x = trimmed(tests_pad, (4,))
    tests_z = trimmed(tests_pad, (2,))
    laplace_test = (
        second_padded(tests_x, 2, x_cells)
        + second_rolled(test_fields, 3)
        + second_padded(tests_z, 4, z_cells)
    )
    test_next = test_fields + TIME_STEP * (curl + DIFFUSIVITY * laplace_test)
    return (velocity_next, test_next)


def solution(mesh):
    placed = (P(None, "gx", "sec", "gz"), P("sec", None, "gx", None, "gz"))
    return jax.shard_map(
        shards,
        mesh=mesh,
        in_specs=placed,
        out_specs=(P(None, "gx", "sec", "gz"), P("sec", None, "gx", None, "gz")),
        check_vma=False,
    )
```

profile of v0, /device:TPU:0, one launch (start us, length us, event | category | flops | bytes accessed | tf_op | source)
XLA Modules:
  0.0 192.5 jit_solution(11116827213722034205)
XLA Ops:
  2.2 3.3 %collective-permute-start.1 = (f32[3,8,3,128]{3,2,1,0:T(4,128)}, f32[3,8,3,128]{3,2,1,0:T(4,128)}, u32[]{:S(2)}, u32[]{:S(2)}) collective-permute-start(f32[3,8,3,128]{3,2,1,0:T(4,128)} %get-tuple-element.57), channel_id=1, source_target_pairs={{64,0},{0,64},{65,1},{1,65},{66,2},{2,66},{67,3},{3,67},{68,4},{4,... | collective-permute-start | bytes 110600 | tf_op jit(solution)/shard_map/ppermute | solution.py:32
  5.8 2.5 %fusion.174 = (f32[2,3,8,64,3]{4,3,2,1,0:T(8,128)S(1)}, f32[2,3,8,64,3]{4,3,2,1,0:T(8,128)S(1)}) fusion(f32[2,3,8,64,128]{4,3,2,1,0:T(8,128)} %param.3), kind=kLoop, calls=%fused_computation.313 | loop fusion | bytes 147456 | tf_op jit(solution)/shard_map/slice | solution.py:26
  10.6 3.9 %collective-permute-start.15 = (f32[2,3,8,64,3]{3,2,4,1,0:T(8,128)}, f32[2,3,8,64,3]{3,2,4,1,0:T(8,128)}, u32[]{:S(2)}, u32[]{:S(2)}) collective-permute-start(f32[2,3,8,64,3]{3,2,4,1,0:T(8,128)} %copy.31), channel_id=1, source_target_pairs={{4,0},{8,4},{12,8},{16,12},{20,16},{24,20},{28,24},{32,28},{36,32}... | collective-permute-start | bytes 110600 | tf_op jit(solution)/shard_map/ppermute | solution.py:32
  16.0 11.1 %all_gather.6 = f32[3,8,64,128]{3,2,1,0:T(8,128)} all-gather(f32[3,8,32,128]{3,2,1,0:T(8,128)S(1)} %copy-done.4), channel_id=1, replica_groups=mesh['sec'=2,'gz'=16,'gx'=4] {'sec'}, dimensions={2}, use_global_device_ids=true | all-gather | bytes 1179648 | tf_op jit(solution)/shard_map/all_gather | solution.py:201
  27.2 2.1 %fusion.165 = (f32[2,3,8,63,128]{4,3,2,1,0:T(8,128)}, f32[2,3,8,63,128]{4,3,2,1,0:T(8,128)}) fusion(f32[2,3,8,64,128]{4,3,2,1,0:T(8,128)S(1)} %copy-done), kind=kLoop, calls=%fused_computation.304 | loop fusion | bytes 6193152 | tf_op jit(solution)/shard_map/jit(_roll_static)/slice | solution.py:106
  29.3 2.0 %fusion.167 = (f32[2,3,8,62,128]{4,3,2,1,0:T(8,128)}, f32[2,3,8,62,128]{4,3,2,1,0:T(8,128)}) fusion(f32[2,3,8,64,128]{4,3,2,1,0:T(8,128)S(1)} %copy-done), kind=kLoop, calls=%fused_computation.306 | loop fusion | bytes 6094848 | tf_op jit(solution)/shard_map/jit(_roll_static)/slice | solution.py:106
  31.3 2.0 %fusion.169 = (f32[2,3,8,61,128]{4,3,2,1,0:T(8,128)}, f32[2,3,8,61,128]{4,3,2,1,0:T(8,128)}) fusion(f32[2,3,8,64,128]{4,3,2,1,0:T(8,128)S(1)} %copy-done), kind=kLoop, calls=%fused_computation.308 | loop fusion | bytes 5996544 | tf_op jit(solution)/shard_map/jit(_roll_static)/slice | solution.py:106
  42.9 3.9 %collective-permute-start.3 = (f32[3,8,38,3]{3,2,1,0:T(8,128)}, f32[3,8,38,3]{3,2,1,0:T(8,128)}, u32[]{:S(2)}, u32[]{:S(2)}) collective-permute-start(f32[3,8,38,3]{3,2,1,0:T(8,128)} %get-tuple-element.51), channel_id=1, source_target_pairs={{4,0},{8,4},{12,8},{16,12},{20,16},{24,20},{28,24},{32,28},{36,32}... | collective-permute-start | bytes 32840 | tf_op jit(solution)/shard_map/ppermute | solution.py:32
  48.2 2.7 %copy.23 = f32[2,3,8,64,3]{4,3,2,1,0:T(8,128)} copy(f32[2,3,8,64,3]{3,2,4,1,0:T(8,128)} %collective-permute-done.15) | data formatting | bytes 73728 | tf_op jit(solution)/shard_map/ppermute | solution.py:32
  50.9 3.6 %pad_maximum_fusion.18 = (f32[2,3,3,64,134]{4,3,2,1,0:T(8,128)}, f32[2,3,3,64,134]{4,3,2,1,0:T(8,128)}) fusion(f32[2,3,8,64,3]{4,3,2,1,0:T(8,128)} %copy.23, f32[2,3,8,64,128]{4,3,2,1,0:T(8,128)S(1)} %copy-done, f32[2,3,8,64,3]{4,3,2,1,0:T(8,128)S(1)} %copy.22), kind=kLoop, calls=%fused_computation.78 | loop fusion | flops 617472 | bytes 2881536 | tf_op jit(solution)/shard_map/slice | solution.py:26
  54.5 4.0 %collective-permute-start.16 = (f32[2,3,3,64,134]{4,3,2,1,0:T(8,128)}, f32[2,3,3,64,134]{4,3,2,1,0:T(8,128)}, u32[]{:S(2)}, u32[]{:S(2)}) collective-permute-start(f32[2,3,3,64,134]{4,3,2,1,0:T(8,128)} %get-tuple-element.14), channel_id=1, source_target_pairs={{1,0},{2,1},{3,2},{0,3},{5,4},{6,5},{7,6},{4,7},{9,8},{10,9},{11,1... | collective-permute-start | bytes 1852424 | tf_op jit(solution)/shard_map/ppermute | solution.py:32
  58.6 1.7 pad_maximum_fusion.45
  64.8 3.3 %collective-permute-start.4 = (f32[3,3,38,134]{3,2,1,0:T(8,128)S(1)}, f32[3,3,38,134]{3,2,1,0:T(8,128)S(1)}, u32[]{:S(2)}, u32[]{:S(2)}) collective-permute-start(f32[3,3,38,134]{3,2,1,0:T(8,128)S(1)} %get-tuple-element.45), channel_id=1, source_target_pairs={{1,0},{2,1},{3,2},{0,3},{5,4},{6,5},{7,6},{4,7},{9,8},{10,9},{11,1... | collective-permute-start | bytes 549944 | tf_op jit(solution)/shard_map/ppermute | solution.py:32
  68.5 21.3 %collective-permute-done.4 = f32[3,3,38,134]{3,2,1,0:T(8,128)S(1)} collective-permute-done((f32[3,3,38,134]{3,2,1,0:T(8,128)S(1)}, f32[3,3,38,134]{3,2,1,0:T(8,128)S(1)}, u32[]{:S(2)}, u32[]{:S(2)}) %collective-permute-start.4) | collective-permute-done | bytes 183344 | tf_op jit(solution)/shard_map/ppermute | solution.py:32
  89.8 3.4 %collective-permute-done.5 = f32[3,3,38,134]{3,2,1,0:T(8,128)S(1)} collective-permute-done((f32[3,3,38,134]{3,2,1,0:T(8,128)S(1)}, f32[3,3,38,134]{3,2,1,0:T(8,128)S(1)}, u32[]{:S(2)}, u32[]{:S(2)}) %collective-permute-start.5) | collective-permute-done | bytes 183344 | tf_op jit(solution)/shard_map/ppermute | solution.py:30
  93.2 5.2 %fusion.85 = f32[3,8,32,128]{3,2,1,0:T(8,128)S(1)} fusion(f32[3,8,32,128]{3,2,1,0:T(8,128)S(1)} %copy-done.4, f32[3,8,38,131]{3,2,1,0:T(8,128)S(1)} %get-tuple-element.50, f32[3,8,38,131]{3,2,1,0:T(8,128)S(1)} %get-tuple-element.49, f32[3,8,32,128]{3,2,1,0:T(8,128)S(1)} %fusion.86, f32[3,8,3,128]{3,2,1,0:T(4,128)} %collective-permute-done, ...), kind=kLoop, calls=%fused_computation.163 | loop fusion | flops 8945664 | bytes 5584288 | tf_op jit(solution)/shard_map/add | solution.py:199
  98.5 10.1 %all_gather.7 = f32[3,8,64,128]{3,2,1,0:T(8,128)S(1)} all-gather(f32[3,8,32,128]{3,2,1,0:T(8,128)S(1)} %fusion.85), channel_id=1, replica_groups=mesh['sec'=2,'gz'=16,'gx'=4] {'sec'}, dimensions={2}, use_global_device_ids=true | all-gather | bytes 1179648 | tf_op jit(solution)/shard_map/all_gather | solution.py:202
  111.6 2.3 %fusion.170 = (f32[2,3,8,64,3]{4,3,2,1,0:T(8,128)}, f32[2,3,8,64,3]{4,3,2,1,0:T(8,128)}) fusion(f32[2,3,8,64,128]{4,3,2,1,0:T(8,128)S(1)} %pad_maximum_fusion.15), kind=kLoop, calls=%fused_computation.309 | loop fusion | bytes 147456 | tf_op jit(solution)/shard_map/slice | solution.py:27
  113.9 2.0 %fusion.171 = (f32[2,3,8,61,128]{4,3,2,1,0:T(8,128)}, f32[2,3,8,61,128]{4,3,2,1,0:T(8,128)}) fusion(f32[2,3,8,64,128]{4,3,2,1,0:T(8,128)S(1)} %pad_maximum_fusion.15), kind=kLoop, calls=%fused_computation.310 | loop fusion | bytes 5996544 | tf_op jit(solution)/shard_map/jit(_roll_static)/slice | solution.py:94
  115.9 1.9 fusion.172
  117.8 1.9 %copy.13 = f32[2,3,8,64,3]{3,2,4,1,0:T(8,128)S(1)} copy(f32[2,3,8,64,3]{4,3,2,1,0:T(8,128)} %get-tuple-element.35) | data formatting | bytes 73728 | tf_op jit(solution)/shard_map/slice | solution.py:26
  120.1 1.9 %copy.15 = f32[2,3,8,64,3]{3,2,4,1,0:T(8,128)S(1)} copy(f32[2,3,8,64,3]{4,3,2,1,0:T(8,128)} %get-tuple-element.34) | data formatting | bytes 73728 | tf_op jit(solution)/shard_map/slice | solution.py:27
  122.3 2.0 %fusion.173 = (f32[2,3,8,63,128]{4,3,2,1,0:T(8,128)}, f32[2,3,8,63,128]{4,3,2,1,0:T(8,128)}) fusion(f32[2,3,8,64,128]{4,3,2,1,0:T(8,128)S(1)} %pad_maximum_fusion.15), kind=kLoop, calls=%fused_computation.312 | loop fusion | bytes 6193152 | tf_op jit(solution)/shard_map/jit(_roll_static)/slice | solution.py:94
  124.8 3.1 %collective-permute-done.9 = f32[2,3,8,64,3]{3,2,4,1,0:T(8,128)S(1)} collective-permute-done((f32[2,3,8,64,3]{3,2,4,1,0:T(8,128)S(1)}, f32[2,3,8,64,3]{3,2,4,1,0:T(8,128)S(1)}, u32[]{:S(2)}, u32[]{:S(2)}) %collective-permute-start.9) | collective-permute-done | bytes 36896 | tf_op jit(solution)/shard_map/ppermute | solution.py:30
  127.9 1.7 copy.16
  129.7 7.0 %fusion.53 = f32[2,2,8,64,128]{4,3,2,1,0:T(8,128)S(1)} fusion(f32[2,3,8,64,3]{4,3,2,1,0:T(8,128)} %copy.16, f32[2,1,8,64,128]{4,3,2,1,0:T(8,128)} %copy-done.12, f32[2,1,8,64,128]{4,3,2,1,0:T(8,128)} %copy-done.10, f32[2,1,8,64,128]{4,3,2,1,0:T(8,128)} %copy-done.8, f32[2,3,8,64,3]{4,3,2,1,0:T(8,128)S(1)} %copy.14, s32[128]{0:T(128)S(1)} %copy-done.37), kind=kOutput, calls=%fused_computation.108 | convolution fusion | flops 408076288 | bytes 2695680 | tf_op jit(solution)/shard_map/dot_general | solution.py:126
  143.6 1.8 collective-permute-done.11
  146.1 6.8 %pad_maximum_fusion = (f32[2,3,11,64,134]{4,3,2,1,0:T(8,128)}, f32[2,3,11,64,134]{4,3,2,1,0:T(8,128)}) fusion(f32[2,3,3,64,134]{4,3,2,1,0:T(8,128)} %collective-permute-done.16, f32[2,3,8,64,3]{4,3,2,1,0:T(8,128)S(1)} %copy-done.3, f32[2,3,8,64,128]{4,3,2,1,0:T(8,128)S(1)} %copy-done, f32[2,3,8,64,3]{4,3,2,1,0:T(8,128)S(1)} %copy-done.2, ...), kind=kLoop, calls=%fused_computation | loop fusion | flops 3396096 | bytes 7409664 | tf_op jit(solution)/shard_map/concatenate | solution.py:28
  152.9 17.4 %collective-permute-done.12 = f32[2,3,3,64,134]{4,3,2,1,0:T(8,128)S(1)} collective-permute-done((f32[2,3,3,64,134]{4,3,2,1,0:T(8,128)S(1)}, f32[2,3,3,64,134]{4,3,2,1,0:T(8,128)S(1)}, u32[]{:S(2)}, u32[]{:S(2)}) %collective-permute-start.12) | collective-permute-done | bytes 617504 | tf_op jit(solution)/shard_map/ppermute | solution.py:32
  170.3 1.7 collective-permute-done.13
  172.0 2.2 %fusion.46 = f32[2,2,8,64,128]{4,3,2,1,0:T(8,128)S(1)} fusion(f32[2,3,3,64,134]{4,3,2,1,0:T(8,128)S(1)} %collective-permute-done.13, f32[2,3,8,64,3]{4,3,2,1,0:T(8,128)S(1)} %copy-done.6, f32[2,3,8,64,3]{4,3,2,1,0:T(8,128)S(1)} %copy-done.7, f32[2,1,8,64,128]{4,3,2,1,0:T(8,128)S(1)} %copy-done.13, f32[2,1,8,64,128]{4,3,2,1,0:T(8,128)S(1)} %copy-done.11, ...), kind=kLoop, calls=%fused_computation.87 | loop fusion | flops 9961472 | bytes 3930112 | tf_op jit(solution)/shard_map/div | solution.py:71
  175.6 16.7 %fusion.10 = f32[2,3,8,64,128]{4,3,2,1,0:T(8,128)} fusion(f32[2,3,8,64,128]{4,3,2,1,0:T(8,128)S(1)} %copy-done, f32[2,3,8,64,3]{4,3,2,1,0:T(8,128)S(1)} %copy-done.2, f32[2,3,8,64,3]{4,3,2,1,0:T(8,128)} %copy.23, f32[2,3,11,64,134]{4,3,2,1,0:T(8,128)} %get-tuple-element.13, f32[2,3,11,64,134]{4,3,2,1,0:T(8,128)} %get-tuple-element.12, ...), kind=kLoop, calls=%fused_computation.20 | loop fusion | flops 18874368 | bytes 23666688 | tf_op jit(solution)/shard_map/add | solution.py:232
  (145 shorter events, 32.1 us)
Async XLA Ops:
  2.2 38.6 %collective-permute-start.1 = (f32[3,8,3,128]{3,2,1,0:T(4,128)}, f32[3,8,3,128]{3,2,1,0:T(4,128)}, u32[]{:S(2)}, u32[]{:S(2)}) collective-permute-start(f32[3,8,3,128]{3,2,1,0:T(4,128)} %get-tuple-element.57), channel_id=1, source_target_pairs={{64,0},{0,64},{65,1},{1,65},{66,2},{2,66},{67,3},{3,67},{68,4},{4,... | collective-permute-start | bytes 110600 | tf_op jit(solution)/shard_map/ppermute | solution.py:32
  5.5 35.4 %collective-permute-start = (f32[3,8,3,128]{3,2,1,0:T(4,128)}, f32[3,8,3,128]{3,2,1,0:T(4,128)}, u32[]{:S(2)}, u32[]{:S(2)}) collective-permute-start(f32[3,8,3,128]{3,2,1,0:T(4,128)} %get-tuple-element.56), channel_id=1, source_target_pairs={{0,64},{64,0},{1,65},{65,1},{2,66},{66,2},{3,67},{67,3},{4,68},{68... | collective-permute-start | bytes 110600 | tf_op jit(solution)/shard_map/ppermute | solution.py:30
  9.4 37.4 %collective-permute-start.14 = (f32[2,3,8,64,3]{3,2,4,1,0:T(8,128)}, f32[2,3,8,64,3]{3,2,4,1,0:T(8,128)}, u32[]{:S(2)}, u32[]{:S(2)}) collective-permute-start(f32[2,3,8,64,3]{3,2,4,1,0:T(8,128)} %copy.30), channel_id=1, source_target_pairs={{0,4},{4,8},{8,12},{12,16},{16,20},{20,24},{24,28},{28,32},{32,36}... | collective-permute-start | bytes 110600 | tf_op jit(solution)/shard_map/ppermute | solution.py:30
  10.6 16.6 %copy-start = (f32[2,3,8,64,128]{4,3,2,1,0:T(8,128)S(1)}, f32[2,3,8,64,128]{4,3,2,1,0:T(8,128)}, u32[]{:S(2)}) copy-start(f32[2,3,8,64,128]{4,3,2,1,0:T(8,128)} %param.3) | copy-start | bytes 4718596
  10.6 37.7 %collective-permute-start.15 = (f32[2,3,8,64,3]{3,2,4,1,0:T(8,128)}, f32[2,3,8,64,3]{3,2,4,1,0:T(8,128)}, u32[]{:S(2)}, u32[]{:S(2)}) collective-permute-start(f32[2,3,8,64,3]{3,2,4,1,0:T(8,128)} %copy.31), channel_id=1, source_target_pairs={{4,0},{8,4},{12,8},{16,12},{20,16},{24,20},{28,24},{32,28},{36,32}... | collective-permute-start | bytes 110600 | tf_op jit(solution)/shard_map/ppermute | solution.py:32
  14.4 20.9 %copy-start.35 = (s32[128]{0:T(128)}, s32[128]{0:T(128)S(1)}, u32[]{:S(2)}) copy-start(s32[128]{0:T(128)S(1)} %iota_subtract_fusion.2) | copy-start | bytes 1540
  42.9 15.6 %collective-permute-start.2 = (f32[3,8,38,3]{3,2,1,0:T(8,128)}, f32[3,8,38,3]{3,2,1,0:T(8,128)}, u32[]{:S(2)}, u32[]{:S(2)}) collective-permute-start(f32[3,8,38,3]{3,2,1,0:T(8,128)} %get-tuple-element.52), channel_id=1, source_target_pairs={{0,4},{4,8},{8,12},{12,16},{16,20},{20,24},{24,28},{28,32},{32,36}... | collective-permute-start | bytes 32840 | tf_op jit(solution)/shard_map/ppermute | solution.py:30
  42.9 15.6 %collective-permute-start.3 = (f32[3,8,38,3]{3,2,1,0:T(8,128)}, f32[3,8,38,3]{3,2,1,0:T(8,128)}, u32[]{:S(2)}, u32[]{:S(2)}) collective-permute-start(f32[3,8,38,3]{3,2,1,0:T(8,128)} %get-tuple-element.51), channel_id=1, source_target_pairs={{4,0},{8,4},{12,8},{16,12},{20,16},{24,20},{28,24},{32,28},{36,32}... | collective-permute-start | bytes 32840 | tf_op jit(solution)/shard_map/ppermute | solution.py:32
  54.5 91.5 %collective-permute-start.16 = (f32[2,3,3,64,134]{4,3,2,1,0:T(8,128)}, f32[2,3,3,64,134]{4,3,2,1,0:T(8,128)}, u32[]{:S(2)}, u32[]{:S(2)}) collective-permute-start(f32[2,3,3,64,134]{4,3,2,1,0:T(8,128)} %get-tuple-element.14), channel_id=1, source_target_pairs={{1,0},{2,1},{3,2},{0,3},{5,4},{6,5},{7,6},{4,7},{9,8},{10,9},{11,1... | collective-permute-start | bytes 1852424 | tf_op jit(solution)/shard_map/ppermute | solution.py:32
  58.5 87.5 %collective-permute-start.17 = (f32[2,3,3,64,134]{4,3,2,1,0:T(8,128)}, f32[2,3,3,64,134]{4,3,2,1,0:T(8,128)}, u32[]{:S(2)}, u32[]{:S(2)}) collective-permute-start(f32[2,3,3,64,134]{4,3,2,1,0:T(8,128)} %get-tuple-element.15), channel_id=1, source_target_pairs={{0,1},{1,2},{2,3},{3,0},{4,5},{5,6},{6,7},{7,4},{8,9},{9,10},{10,1... | collective-permute-start | bytes 1852424 | tf_op jit(solution)/shard_map/ppermute | solution.py:30
  61.2 32.0 %copy-start.24 = (f32[8,32,128]{2,1,0:T(8,128)S(1)}, f32[8,32,128]{2,1,0:T(8,128)}, u32[]{:S(2)}) copy-start(f32[8,32,128]{2,1,0:T(8,128)} %get-tuple-element.53) | copy-start | bytes 393220
  61.2 32.0 %copy-start.25 = (f32[8,32,128]{2,1,0:T(8,128)S(1)}, f32[8,32,128]{2,1,0:T(8,128)}, u32[]{:S(2)}) copy-start(f32[8,32,128]{2,1,0:T(8,128)} %get-tuple-element.54) | copy-start | bytes 393220
  61.2 32.0 %copy-start.26 = (f32[8,32,128]{2,1,0:T(8,128)S(1)}, f32[8,32,128]{2,1,0:T(8,128)}, u32[]{:S(2)}) copy-start(f32[8,32,128]{2,1,0:T(8,128)} %get-tuple-element.55) | copy-start | bytes 393220
  61.3 32.0 %copy-start.33 = (f32[128]{0:T(128)S(1)}, f32[128]{0:T(128)}, u32[]{:S(2)}) copy-start(f32[128]{0:T(128)} %get-tuple-element.59) | copy-start | bytes 1540
  61.7 1.5 collective-permute-start.6
  63.2 5.3 %collective-permute-start.7 = (f32[3,8,32]{2,1,0:T(8,128)S(1)}, f32[3,8,32]{2,1,0:T(8,128)S(1)}, u32[]{:S(2)}, u32[]{:S(2)}) collective-permute-start(f32[3,8,32]{2,1,0:T(8,128)S(1)} %get-tuple-element.9), channel_id=1, source_target_pairs={{60,0},{0,4},{4,8},{8,12},{12,16},{16,20},{20,24},{24,28},{28,32},... | collective-permute-start | bytes 9224 | tf_op jit(solution)/shard_map/ppermute | solution.py:20
  64.8 24.9 %collective-permute-start.4 = (f32[3,3,38,134]{3,2,1,0:T(8,128)S(1)}, f32[3,3,38,134]{3,2,1,0:T(8,128)S(1)}, u32[]{:S(2)}, u32[]{:S(2)}) collective-permute-start(f32[3,3,38,134]{3,2,1,0:T(8,128)S(1)} %get-tuple-element.45), channel_id=1, source_target_pairs={{1,0},{2,1},{3,2},{0,3},{5,4},{6,5},{7,6},{4,7},{9,8},{10,9},{11,1... | collective-permute-start | bytes 549944 | tf_op jit(solution)/shard_map/ppermute | solution.py:32
  68.1 25.1 %collective-permute-start.5 = (f32[3,3,38,134]{3,2,1,0:T(8,128)S(1)}, f32[3,3,38,134]{3,2,1,0:T(8,128)S(1)}, u32[]{:S(2)}, u32[]{:S(2)}) collective-permute-start(f32[3,3,38,134]{3,2,1,0:T(8,128)S(1)} %get-tuple-element.44), channel_id=1, source_target_pairs={{0,1},{1,2},{2,3},{3,0},{4,5},{5,6},{6,7},{7,4},{8,9},{9,10},{10,1... | collective-permute-start | bytes 549944 | tf_op jit(solution)/shard_map/ppermute | solution.py:30
  98.4 10.3 %copy-start.23 = (f32[3,8,32,128]{3,2,1,0:T(8,128)}, f32[3,8,32,128]{3,2,1,0:T(8,128)S(1)}, u32[]{:S(2)}) copy-start(f32[3,8,32,128]{3,2,1,0:T(8,128)S(1)} %fusion.85) | copy-start | bytes 1179652
  98.5 10.1 %copy-start.22 = (f32[3,8,64,128]{3,2,1,0:T(8,128)S(1)}, f32[3,8,64,128]{3,2,1,0:T(8,128)}, u32[]{:S(2)}) copy-start(f32[3,8,64,128]{3,2,1,0:T(8,128)} %all_gather.6) | copy-start | bytes 2359300
  119.7 4.5 %collective-permute-start.8 = (f32[2,3,8,64,3]{3,2,4,1,0:T(8,128)S(1)}, f32[2,3,8,64,3]{3,2,4,1,0:T(8,128)S(1)}, u32[]{:S(2)}, u32[]{:S(2)}) collective-permute-start(f32[2,3,8,64,3]{3,2,4,1,0:T(8,128)S(1)} %copy.13), channel_id=1, source_target_pairs={{4,0},{8,4},{12,8},{16,12},{20,16},{24,20},{28,24},{32,28},{36,32}... | collective-permute-start | bytes 110600 | tf_op jit(solution)/shard_map/ppermute | solution.py:32
  122.0 5.9 %collective-permute-start.9 = (f32[2,3,8,64,3]{3,2,4,1,0:T(8,128)S(1)}, f32[2,3,8,64,3]{3,2,4,1,0:T(8,128)S(1)}, u32[]{:S(2)}, u32[]{:S(2)}) collective-permute-start(f32[2,3,8,64,3]{3,2,4,1,0:T(8,128)S(1)} %copy.15), channel_id=1, source_target_pairs={{0,4},{4,8},{8,12},{12,16},{16,20},{20,24},{24,28},{28,32},{32,36}... | collective-permute-start | bytes 110600 | tf_op jit(solution)/shard_map/ppermute | solution.py:30
  124.8 15.7 %copy-start.5 = (f32[2,3,8,64,3]{4,3,2,1,0:T(8,128)}, f32[2,3,8,64,3]{4,3,2,1,0:T(8,128)S(1)}, u32[]{:S(2)}) copy-start(f32[2,3,8,64,3]{4,3,2,1,0:T(8,128)S(1)} %copy.14) | copy-start | bytes 110596
  129.6 8.6 %copy-start.14 = (f32[2,3,8,61,128]{4,3,2,1,0:T(8,128)S(1)}, f32[2,3,8,61,128]{4,3,2,1,0:T(8,128)}, u32[]{:S(2)}) copy-start(f32[2,3,8,61,128]{4,3,2,1,0:T(8,128)} %get-tuple-element.36) | copy-start | bytes 4497412
  129.6 8.6 %copy-start.15 = (f32[2,3,8,61,128]{4,3,2,1,0:T(8,128)S(1)}, f32[2,3,8,61,128]{4,3,2,1,0:T(8,128)}, u32[]{:S(2)}) copy-start(f32[2,3,8,61,128]{4,3,2,1,0:T(8,128)} %get-tuple-element.37) | copy-start | bytes 4497412
  129.6 8.6 %copy-start.16 = (f32[2,3,8,62,128]{4,3,2,1,0:T(8,128)S(1)}, f32[2,3,8,62,128]{4,3,2,1,0:T(8,128)}, u32[]{:S(2)}) copy-start(f32[2,3,8,62,128]{4,3,2,1,0:T(8,128)} %get-tuple-element.38) | copy-start | bytes 4571140
  129.6 8.6 %copy-start.17 = (f32[2,3,8,62,128]{4,3,2,1,0:T(8,128)S(1)}, f32[2,3,8,62,128]{4,3,2,1,0:T(8,128)}, u32[]{:S(2)}) copy-start(f32[2,3,8,62,128]{4,3,2,1,0:T(8,128)} %get-tuple-element.39) | copy-start | bytes 4571140
  137.6 2.2 %collective-permute-start.10 = (f32[2,2,8,64]{3,2,1,0:T(8,128)S(1)}, f32[2,2,8,64]{3,2,1,0:T(8,128)S(1)}, u32[]{:S(2)}, u32[]{:S(2)}) collective-permute-start(f32[2,2,8,64]{3,2,1,0:T(8,128)S(1)} %get-tuple-element.3), channel_id=1, source_target_pairs={{4,0},{8,4},{12,8},{16,12},{20,16},{24,20},{28,24},{32,28},{36,32}... | collective-permute-start | bytes 24584 | tf_op jit(solution)/shard_map/ppermute | solution.py:20
  139.8 5.6 %collective-permute-start.11 = (f32[2,2,8,64]{3,2,1,0:T(8,128)S(1)}, f32[2,2,8,64]{3,2,1,0:T(8,128)S(1)}, u32[]{:S(2)}, u32[]{:S(2)}) collective-permute-start(f32[2,2,8,64]{3,2,1,0:T(8,128)S(1)} %get-tuple-element.7), channel_id=1, source_target_pairs={{60,0},{0,4},{4,8},{8,12},{12,16},{16,20},{20,24},{24,28},{28,32},... | collective-permute-start | bytes 24584 | tf_op jit(solution)/shard_map/ppermute | solution.py:20
  141.5 28.8 %collective-permute-start.12 = (f32[2,3,3,64,134]{4,3,2,1,0:T(8,128)S(1)}, f32[2,3,3,64,134]{4,3,2,1,0:T(8,128)S(1)}, u32[]{:S(2)}, u32[]{:S(2)}) collective-permute-start(f32[2,3,3,64,134]{4,3,2,1,0:T(8,128)S(1)} %get-tuple-element.10), channel_id=1, source_target_pairs={{1,0},{2,1},{3,2},{0,3},{5,4},{6,5},{7,6},{4,7},{9,8},{10,9},{11,1... | collective-permute-start | bytes 1852424 | tf_op jit(solution)/shard_map/ppermute | solution.py:32
  142.2 29.9 %collective-permute-start.13 = (f32[2,3,3,64,134]{4,3,2,1,0:T(8,128)S(1)}, f32[2,3,3,64,134]{4,3,2,1,0:T(8,128)S(1)}, u32[]{:S(2)}, u32[]{:S(2)}) collective-permute-start(f32[2,3,3,64,134]{4,3,2,1,0:T(8,128)S(1)} %get-tuple-element.11), channel_id=1, source_target_pairs={{0,1},{1,2},{2,3},{3,0},{4,5},{5,6},{6,7},{7,4},{8,9},{9,10},{10,1... | collective-permute-start | bytes 1852424 | tf_op jit(solution)/shard_map/ppermute | solution.py:30
  146.0 26.0 %copy-start.6 = (f32[2,3,8,64,3]{4,3,2,1,0:T(8,128)S(1)}, f32[2,3,8,64,3]{4,3,2,1,0:T(8,128)}, u32[]{:S(2)}) copy-start(f32[2,3,8,64,3]{4,3,2,1,0:T(8,128)} %copy-done.5) | copy-start | bytes 110596
  (24 other events, 73.3 us)
where the time goes:
time: 195 us; the launch traced here: 192 us
  waiting for transfers between devices  49.7 us (25%)
  other arithmetic  46.5 us (24%)
  local copies, waits for them, and re-layouts  40.6 us (21%)
  starting transfers between devices  22.6 us (12%)
  blocking collectives  21.2 us (11%)
  matrix products  7.9 us (4%)
  between operations  3.91 us (2%)
    ppermute x7, waiting for transfers between devices, with_halo(): lax.ppermute(head, axis, [((i + 1) % count, i) for i in range(count)])  38.7 us
    ppermute x7, starting transfers between devices, with_halo(): lax.ppermute(head, axis, [((i + 1) % count, i) for i in range(count)])  19.3 us
    add x1, other arithmetic, shards(): test_next = test_fields + TIME_STEP * (curl + DIFFUSIVITY * laplace_test)  16.7 us
    slice x9, local copies, waits for them, and re-layouts, shifted(): return jnp.roll(values, -offset, axis=axis_dim)  14 us
    all_gather x1, blocking collectives, shards(): lax.all_gather(velocity, 'sec', axis=2, tiled=True)  11.1 us
    concatenate x4, other arithmetic, with_halo(): jnp.concatenate([lax.ppermute(tail, axis, [(i, (i + 1) % count) for i in...  11 us
    all_gather x1, blocking collectives, shards(): lax.all_gather(velocity_next, 'sec', axis=2, tiled=True)  10.1 us
    ppermute x7, waiting for transfers between devices, with_halo(): lax.ppermute(tail, axis, [(i, (i + 1) % count) for i in range(count)])  8.25 us
  transfers between devices with their start and end apart: 18, of which 8 were waited for; matrix products, arithmetic and copies ran while one was open for 37% of the time, Pallas kernels for 0%

commit v1 on v0

v1 whole, which is shorter than its diff:
```python
import math

import jax
import jax.numpy as jnp
import numpy as np
from jax import lax
from jax.experimental import pallas as pl
from jax.experimental.pallas import tpu as pltpu
from jax.sharding import PartitionSpec as P

STEP = 0.2
VISC = 0.1
DIFF = 0.1
FIRST = (45.0 / 60.0, -9.0 / 60.0, 1.0 / 60.0)
SECOND = (270.0 / 180.0, -27.0 / 180.0, 2.0 / 180.0)
MID = -490.0 / 180.0
ROOT = math.sqrt(5.0 / 9.0)
DECAY = -(1.0 - ROOT) / (2.0 / 3.0)
HIGHEST = lax.Precision.HIGHEST
VMEM_LIMIT = 48 * 1024 * 1024


def compact_weight(distance):
    d = np.asarray(distance)

    def green(k):
        return DECAY ** np.abs(k) / ROOT

    return 7.0 / 9.0 * (green(d + 1) - green(d - 1)) + 1.0 / 36.0 * (green(d + 2) - green(d - 2))


def second_weight(distance):
    d = np.abs(distance)
    table = np.array([MID, *SECOND, 0.0])
    return table[np.minimum(d, 4)]


TAIL = float(compact_weight(2)) / DECAY**2
CORNER = float(compact_weight(1)) - TAIL * DECAY


def z_tables(n):
    j = np.arange(n)
    gap = j[None, :] - j[:, None]
    inner_first = compact_weight(gap)
    inner_second = second_weight(gap)
    pick = np.zeros((8, n))
    for k in range(3):
        pick[k, n - 1 - k] = 1.0
        pick[4 + k, k] = 1.0
    pick[3] = DECAY ** (n - 1 - j)
    pick[7] = DECAY**j
    spread_first = np.zeros((8, n))
    spread_second = np.zeros((8, n))
    for k in range(3):
        for z in range(3 - k):
            spread_second[k, z] = SECOND[z + k]
            spread_second[4 + k, n - 1 - z] = SECOND[z + k]
    spread_first[0, 0] = CORNER
    spread_first[4, n - 1] = -CORNER
    spread_first[3] = TAIL * DECAY ** (j + 1)
    spread_first[7] = -TAIL * DECAY ** (n - j)
    lay_test = np.zeros((8, n))
    lay_cross = np.zeros((8, n))
    for z in range(3):
        for k in range(3 - z):
            lay_test[z, n - 1 - k] = STEP * DIFF * SECOND[z + k]
            lay_test[4 + z, k] = STEP * DIFF * SECOND[z + k]
    lay_cross[0, n - 1] = STEP * CORNER
    lay_cross[4, 0] = -STEP * CORNER
    lay_cross[3] = STEP * DECAY ** (n - 1 - j)
    lay_cross[7] = STEP * DECAY**j
    land = np.zeros((8, n))
    for z in range(3):
        land[z, z] = 1.0
        land[4 + z, n - 1 - z] = 1.0
    land[3] = spread_first[3]
    land[7] = spread_first[7]
    f32 = np.float32
    return {
        "inner": np.concatenate([inner_first, inner_second], 1).astype(f32),
        "pick": pick.astype(f32),
        "spread": np.concatenate([spread_first, spread_second], 1).astype(f32),
        "lay": np.stack([lay_test, lay_cross]).astype(f32),
        "land": land.astype(f32),
        "first": (STEP * inner_first).astype(f32),
        "second": (STEP * DIFF * inner_second).astype(f32),
    }


def split(values):
    high = values.astype(jnp.bfloat16)
    low = (values - high.astype(jnp.float32)).astype(jnp.bfloat16)
    return high, low


def dot(a, b):
    return jnp.dot(a, b, preferred_element_type=jnp.float32)


def dot_nt(a, b):
    return lax.dot_general(
        a, b, (((1,), (1,)), ((), ())), precision=HIGHEST, preferred_element_type=jnp.float32
    )


def dot_tn(a, b):
    return lax.dot_general(
        a, b, (((0,), (0,)), ((), ())), precision=HIGHEST, preferred_element_type=jnp.float32
    )


def edges_kernel(v_ref, pick_ref, low_ref, high_ref, ends_ref, right_ref, left_ref):
    _, nx, ny, n = v_ref.shape
    low_ref[...] = v_ref[:, 0:3]
    high_ref[...] = v_ref[:, nx - 3 : nx]
    ends_ref[:, :, 0:4] = v_ref[:, :, 0:4]
    ends_ref[:, :, 4:8] = v_ref[:, :, ny - 4 : ny]
    picked = dot_nt(pick_ref[...], v_ref[...].reshape(-1, n))
    right_ref[...] = picked[0:4]
    left_ref[...] = picked[4:8]


def flow_kernel(
    places, v_ref, low_ref, high_ref, ends_ref, from_left, from_right, inner_ref, spread_ref,
    next_ref, centred_ref, padded, halo, along_z,
):
    _, nx, ny, n = v_ref.shape
    halo[0:4] = from_left[...]
    halo[4:8] = from_right[...]
    along_z[...] = jnp.dot(
        v_ref[...].reshape(-1, n), inner_ref[...], precision=HIGHEST, preferred_element_type=jnp.float32
    ) + dot_tn(halo[...], spread_ref[...])
    padded[:, :, 0:8] = ends_ref[...]
    padded[:, :, 8 : 8 + ny] = v_ref[...]
    padded[:, :, 8 + ny : 16 + ny] = ends_ref[...]
    section, column = places[0], places[1]
    rows_x = lax.broadcasted_iota(jnp.int32, (nx, n), 0) + column * nx
    rows_y = lax.broadcasted_iota(jnp.int32, (ny, n), 0) + section * ny
    phase_x = rows_x.astype(jnp.float32) * (2.0 * math.pi / 32)
    phase_y = rows_y.astype(jnp.float32) * (2.0 * math.pi / 64)
    sin_x, cos_x = jnp.sin(phase_x), jnp.cos(phase_x)
    sin_y, cos_y = jnp.sin(phase_y), jnp.cos(phase_y)
    for i in range(nx):
        drive = (
            sin_x[i : i + 1] * cos_y,
            -(cos_x[i : i + 1] * sin_y),
            math.sqrt(2.0) * (sin_x[i : i + 1] * sin_y),
        )
        own = [v_ref[c, i] for c in range(3)]
        for c in range(3):

            def at_x(k, c=c):
                if k < 0:
                    return low_ref[c, k + 3]
                if k >= nx:
                    return high_ref[c, k - nx]
                return v_ref[c, k]

            def at_y(k, c=c, i=i):
                return padded[c, i, 8 + k : 8 + k + ny]

            up_x = [at_x(i + k) for k in (1, 2, 3)]
            down_x = [at_x(i - k) for k in (1, 2, 3)]
            up_y = [at_y(k) for k in (1, 2, 3)]
            down_y = [at_y(-k) for k in (1, 2, 3)]
            grad_x = sum(w * (a - b) for w, a, b in zip(FIRST, up_x, down_x))
            grad_y = sum(w * (a - b) for w, a, b in zip(FIRST, up_y, down_y))
            lap = sum(
                w * ((a + b) + (d + e)) for w, a, b, d, e in zip(SECOND, up_x, down_x, up_y, down_y)
            )
            base = (c * nx + i) * ny
            grad_z = along_z[base : base + ny, 0:n]
            lap = lap + (2.0 * MID) * own[c] + along_z[base : base + ny, n : 2 * n]
            advect = own[0] * grad_x + own[1] * grad_y + own[2] * grad_z
            moved = own[c] + STEP * (VISC * lap - advect + drive[c])
            next_ref[c, i] = moved
            centred_ref[c, i] = 0.5 * (own[c] + moved)


def faces_kernel(tests_ref, low_ref, high_ref, sems):
    nx = tests_ref.shape[2]
    first = pltpu.make_async_copy(tests_ref.at[:, :, pl.ds(0, 3)], low_ref, sems.at[0])
    second = pltpu.make_async_copy(tests_ref.at[:, :, pl.ds(nx - 3, 3)], high_ref, sems.at[1])
    first.start()
    second.start()
    first.wait()
    second.wait()


def wave_of(problem, slab, n):
    z = lax.broadcasted_iota(jnp.int32, (8, n), 1) + slab * n
    angle = z.astype(jnp.float32) * (2.0 * math.pi / 2048)
    return jnp.where(problem == 0, jnp.cos(angle), jnp.sin(angle))[0:1]


def cross_kernel(
    places, tests_ref, own_ref, other_ref, lay_ref,
    cross_ref, low_ref, high_ref, right_ref, left_ref, whole,
):
    _, _, nx, ny, n = tests_ref.shape
    problem = pl.program_id(0)
    section = places[0]
    half = ny // 2

    @pl.when(problem == 0)
    def _():
        whole[:, :, pl.ds(pl.multiple_of(section * half, half), half)] = own_ref[...]
        whole[:, :, pl.ds(pl.multiple_of((1 - section) * half, half), half)] = other_ref[...]
        low_ref[...] = whole[:, 0:3]
        high_ref[...] = whole[:, nx - 3 : nx]

    wave = wave_of(problem, places[2], n)
    wave_x = jnp.where(section == 0, wave, 0.0)
    wave_y = jnp.where(section == 0, 0.0, wave)
    for i in range(nx):
        cx, cy, cz = whole[0, i], whole[1, i], whole[2, i]
        tx, ty, tz = tests_ref[0, 0, i] + wave_x, tests_ref[0, 1, i] + wave_y, tests_ref[0, 2, i]
        cross_ref[0, 0, i] = cx * tz - cz * tx
        cross_ref[0, 1, i] = cy * tz - cz * ty
        cross_ref[0, 2, i] = cx * ty - cy * tx
    sent = dot_nt(lay_ref[0], tests_ref[0].reshape(-1, n))
    lines = nx * ny
    first = dot_nt(lay_ref[1], cross_ref[0, 0:2].reshape(-1, n))
    sent_xy = sent[:, 0 : 2 * lines] + first
    right_ref[:, 0 : 2 * lines] = sent_xy[0:4]
    right_ref[:, 2 * lines :] = sent[0:4, 2 * lines :]
    left_ref[:, 0 : 2 * lines] = sent_xy[4:8]
    left_ref[:, 2 * lines :] = sent[4:8, 2 * lines :]


def local_kernel(tests_ref, cross_ref, first_ref, second_ref, out_ref, pad_t, pad_c):
    _, _, nx, ny, n = tests_ref.shape
    first_high, first_low = split(first_ref[...])
    second_high, second_low = split(second_ref[...])
    for c in range(3):
        t_high, t_low = split(tests_ref[0, c].reshape(-1, n))
        total = dot(t_high, second_high) + dot(t_low, second_high) + dot(t_high, second_low)
        if c < 2:
            c_high, c_low = split(cross_ref[0, c].reshape(-1, n))
            total = total + dot(c_high, first_high) + dot(c_low, first_high) + dot(c_high, first_low)
        out_ref[0, c] = total.reshape(nx, ny, n)
    for i in range(nx):
        for c in range(3):
            pad_t[c, 0:8] = tests_ref[0, c, i, ny - 8 : ny]
            pad_t[c, 8 : 8 + ny] = tests_ref[0, c, i]
            pad_t[c, 8 + ny : 16 + ny] = tests_ref[0, c, i, 0:8]
        for c in (1, 2):
            pad_c[c - 1, 0:8] = cross_ref[0, c, i, ny - 8 : ny]
            pad_c[c - 1, 8 : 8 + ny] = cross_ref[0, c, i]
            pad_c[c - 1, 8 + ny : 16 + ny] = cross_ref[0, c, i, 0:8]

        def first_y(c):
            return sum(
                (STEP * w) * (pad_c[c, 8 + k : 8 + k + ny] - pad_c[c, 8 - k : 8 - k + ny])
                for k, w in zip((1, 2, 3), FIRST)
            )

        def first_x(c, scale, i=i):
            total = None
            for k, w in zip((1, 2, 3), FIRST):
                for j, sign in ((i + k, scale), (i - k, -scale)):
                    if 0 <= j < nx:
                        term = (STEP * sign * w) * cross_ref[0, c, j]
                        total = term if total is None else total + term
            return total

        for c in range(3):
            value = out_ref[0, c, i] + (1.0 + STEP * DIFF * 2.0 * MID) * tests_ref[0, c, i]
            for k, w in zip((1, 2, 3), SECOND):
                near = pad_t[c, 8 + k : 8 + k + ny] + pad_t[c, 8 - k : 8 - k + ny]
                for j in (i + k, i - k):
                    if 0 <= j < nx:
                        near = near + tests_ref[0, c, j]
                value = value + (STEP * DIFF * w) * near
            if c == 0:
                value = value + first_y(1)
            elif c == 1:
                value = value + first_x(2, -1.0)
            else:
                value = value + first_x(0, -1.0) - first_y(0)
            out_ref[0, c, i] = value


def finish_kernel(
    places, part_ref, t_low_ref, t_high_ref, c_low_ref, c_high_ref, from_left, from_right, land_ref,
    out_ref, halo, cross,
):
    _, _, nx, ny, n = part_ref.shape
    problem = pl.program_id(0)
    section = places[0]
    halo[0:4] = from_left[...]
    halo[4:8] = from_right[...]
    out_ref[...] = part_ref[...] + dot_tn(halo[...], land_ref[...]).reshape(out_ref.shape)
    wave = wave_of(problem, places[2], n)
    wave_x = jnp.where(section == 0, wave, 0.0)
    wave_y = jnp.where(section == 0, 0.0, wave)
    for side, (t_ref, c_ref) in enumerate(((t_low_ref, c_low_ref), (t_high_ref, c_high_ref))):
        for h in range(3):
            cx, cy, cz = c_ref[0, h], c_ref[1, h], c_ref[2, h]
            tx, ty, tz = t_ref[0, 0, h] + wave_x, t_ref[0, 1, h] + wave_y, t_ref[0, 2, h]
            cross[0, h] = cz * tx - cx * tz
            cross[1, h] = cx * ty - cy * tx
        sign = -STEP if side == 0 else STEP
        for m in range(3):
            i = m if side == 0 else nx - 1 - m
            value = [out_ref[0, c, i] for c in range(3)]
            for d in range(m + 1, 4):
                h = 3 + m - d if side == 0 else d - 1 - m
                for c in range(3):
                    value[c] = value[c] + (STEP * DIFF * SECOND[d - 1]) * t_ref[0, c, h]
                value[1] = value[1] - (sign * FIRST[d - 1]) * cross[1, h]
                value[2] = value[2] + (sign * FIRST[d - 1]) * cross[0, h]
            for c in range(3):
                out_ref[0, c, i] = value[c]


def passed(block, axis, distance):
    count = lax.axis_size(axis)
    return lax.ppermute(block, axis, [(i, (i + distance) % count) for i in range(count)])


def shards(velocity, tests):
    _, nx, half, n = velocity.shape
    problems, _, _, ny, _ = tests.shape
    f32 = jnp.float32
    lines = nx * ny
    tables = {k: jnp.asarray(v) for k, v in z_tables(n).items()}
    places = jnp.stack([lax.axis_index(name) for name in ("sec", "gx", "gz")]).astype(jnp.int32)
    smem = pl.BlockSpec(memory_space=pltpu.SMEM)
    params = pltpu.CompilerParams(vmem_limit_bytes=VMEM_LIMIT)

    def shape(*dims):
        return jax.ShapeDtypeStruct(dims, f32)

    def cost(flops, moved):
        return pl.CostEstimate(flops=flops, bytes_accessed=moved, transcendentals=0)

    low, high, ends, to_right, to_left = pl.pallas_call(
        edges_kernel,
        out_shape=[
            shape(3, 3, half, n), shape(3, 3, half, n), shape(3, nx, 8, n),
            shape(4, 3 * nx * half), shape(4, 3 * nx * half),
        ],
        compiler_params=params,
        name="edges",
    )(velocity, tables["pick"])
    from_low = passed(high, "gx", 1)
    from_high = passed(low, "gx", -1)
    ends = passed(ends, "sec", 1)
    from_left = passed(to_right, "gz", 1)
    from_right = passed(to_left, "gz", -1)
    velocity_next, centred = pl.pallas_call(
        flow_kernel,
        in_specs=[smem] + [pl.BlockSpec(memory_space=pltpu.VMEM)] * 8,
        out_shape=[shape(3, nx, half, n)] * 2,
        scratch_shapes=[
            pltpu.VMEM((3, nx, half + 16, n), f32),
            pltpu.VMEM((8, 3 * nx * half), f32),
            pltpu.VMEM((3 * nx * half, 2 * n), f32),
        ],
        compiler_params=params,
        name="flow",
    )(places, velocity, from_low, from_high, ends, from_left, from_right, tables["inner"], tables["spread"])
    other = passed(centred, "sec", 1)
    tests_after, _ = lax.optimization_barrier((tests, centred))
    t_low, t_high = pl.pallas_call(
        faces_kernel,
        in_specs=[pl.BlockSpec(memory_space=pl.ANY)],
        out_specs=[pl.BlockSpec(memory_space=pl.ANY)] * 2,
        out_shape=[shape(problems, 3, 3, ny, n)] * 2,
        scratch_shapes=[pltpu.SemaphoreType.DMA((2,))],
        compiler_params=params,
        name="faces",
    )(tests_after)
    t_from_low = passed(t_high, "gx", 1)
    t_from_high = passed(t_low, "gx", -1)

    block = pl.BlockSpec((1, 3, nx, ny, n), lambda p: (p, 0, 0, 0, 0))
    face = pl.BlockSpec((1, 3, 3, ny, n), lambda p: (p, 0, 0, 0, 0))
    line = pl.BlockSpec((4, 3 * lines), lambda p: (0, p))

    def fixed(*dims):
        return pl.BlockSpec(dims, lambda p: (0,) * len(dims))

    cross, c_low, c_high, to_right, to_left = pl.pallas_call(
        cross_kernel,
        grid=(problems,),
        in_specs=[smem, block, fixed(3, nx, half, n), fixed(3, nx, half, n), fixed(2, 8, n)],
        out_specs=[block, fixed(3, 3, ny, n), fixed(3, 3, ny, n), line, line],
        out_shape=[
            shape(problems, 3, nx, ny, n), shape(3, 3, ny, n), shape(3, 3, ny, n),
            shape(4, problems * 3 * lines), shape(4, problems * 3 * lines),
        ],
        scratch_shapes=[pltpu.VMEM((3, nx, ny, n), f32)],
        compiler_params=params,
        name="cross",
    )(places, tests, centred, other, tables["lay"])
    c_from_low = passed(c_high, "gx", 1)
    c_from_high = passed(c_low, "gx", -1)
    from_left = passed(to_right, "gz", 1)
    from_right = passed(to_left, "gz", -1)
    part = pl.pallas_call(
        local_kernel,
        grid=(problems,),
        in_specs=[block, block, fixed(n, n), fixed(n, n)],
        out_specs=block,
        out_shape=shape(problems, 3, nx, ny, n),
        scratch_shapes=[pltpu.VMEM((3, ny + 16, n), f32), pltpu.VMEM((2, ny + 16, n), f32)],
        compiler_params=params,
        cost_estimate=cost(10**9, 6 * 10**6),
        name="local",
    )(tests, cross, tables["first"], tables["second"])
    test_next = pl.pallas_call(
        finish_kernel,
        grid=(problems,),
        in_specs=[smem, block, face, face, fixed(3, 3, ny, n), fixed(3, 3, ny, n), line, line, fixed(8, n)],
        out_specs=block,
        out_shape=shape(problems, 3, nx, ny, n),
        scratch_shapes=[pltpu.VMEM((8, 3 * lines), f32), pltpu.VMEM((2, 3, ny, n), f32)],
        compiler_params=params,
        name="finish",
    )(places, part, t_from_low, t_from_high, c_from_low, c_from_high, from_left, from_right, tables["land"])
    return velocity_next, test_next


def solution(mesh):
    placed = (P(None, "gx", "sec", "gz"), P("sec", None, "gx", None, "gz"))
    return jax.shard_map(shards, mesh=mesh, in_specs=placed, out_specs=placed, check_vma=False)
```

time: 195 us -> 52.4 us (0.27)
  the two profiles are of different devices: /device:TPU:0 before, /device:TPU:1 now
where the time goes in v1:
time: 52.4 us; the launch traced here: 52.1 us
  starting transfers between devices  28 us (53%)
  Pallas kernels  13.5 us (26%)
  local copies, waits for them, and re-layouts  5.7 us (11%)
  waiting for transfers between devices  4.1 us (8%)
  between operations  0.75 us (1%)
    ppermute x12, starting transfers between devices, passed(): lax.ppermute(block, axis, [(i, (i + distance) % count) for i in range(cou...  28 us
    unnamed x22, local copies, waits for them, and re-layouts  5.7 us
    ppermute x12, waiting for transfers between devices, passed(): lax.ppermute(block, axis, [(i, (i + distance) % count) for i in range(cou...  4.1 us
    pallas_call x1, Pallas kernels, shards(): pl.pallas_call(local_kernel, grid=(problems,), in_specs=[block, block, fi...  3.4 us
    pallas_call x1, Pallas kernels, shards(): pl.pallas_call(finish_kernel, grid=(problems,), in_specs=[smem, block, fa...  3.32 us
    pallas_call x1, Pallas kernels, shards(): pl.pallas_call(flow_kernel, in_specs=[smem] + [pl.BlockSpec(memory_space=...  3.2 us
    pallas_call x1, Pallas kernels, shards(): pl.pallas_call(cross_kernel, grid=(problems,), in_specs=[smem, block, fix...  3.03 us
  transfers between devices with their start and end apart: 12, of which 4 were waited for; matrix products, arithmetic and copies ran while one was open for 0% of the time, Pallas kernels for 13%

profile of v1, /device:TPU:1, one launch (start us, length us, event | category | flops | bytes accessed | tf_op | source)
XLA Modules:
  0.0 52.1 jit_solution(7097714362147541496)
XLA Ops:
  0.6 0.0 copy-start.2
  0.6 1.0 %copy-done.2 = f32[3,8,32,128]{3,2,1,0:T(8,128)S(1)} copy-done((f32[3,8,32,128]{3,2,1,0:T(8,128)S(1)}, f32[3,8,32,128]{3,2,1,0:T(8,128)}, u32[]{:S(2)}) %copy-start.2) | copy-done | bytes 393240
  1.6 0.7 %copy-done.10 = f32[8,128]{1,0:T(8,128)S(1)} copy-done((f32[8,128]{1,0:T(8,128)S(1)}, f32[8,128]{1,0:T(8,128)}, u32[]{:S(2)}) %copy-start.10) | copy-done | bytes 4120
  2.3 0.4 edges.1
  2.8 2.5 %collective-permute-start = (f32[3,3,32,128]{3,2,1,0:T(8,128)S(1)}, f32[3,3,32,128]{3,2,1,0:T(8,128)S(1)}, u32[]{:S(2)}, u32[]{:S(2)}) collective-permute-start(f32[3,3,32,128]{3,2,1,0:T(8,128)S(1)} %get-tuple-element.17), channel_id=1, source_target_pairs={{0,1},{1,2},{2,3},{3,0},{4,5},{5,6},{6,7},{7,4},{8,9},{9,10},{10,1... | collective-permute-start | bytes 442376 | tf_op jit(solution)/shard_map/ppermute | solution.py:320
  5.2 2.2 %collective-permute-start.1 = (f32[3,3,32,128]{3,2,1,0:T(8,128)S(1)}, f32[3,3,32,128]{3,2,1,0:T(8,128)S(1)}, u32[]{:S(2)}, u32[]{:S(2)}) collective-permute-start(f32[3,3,32,128]{3,2,1,0:T(8,128)S(1)} %get-tuple-element.18), channel_id=1, source_target_pairs={{0,3},{1,0},{2,1},{3,2},{4,7},{5,4},{6,5},{7,6},{8,11},{9,8},{10,9... | collective-permute-start | bytes 442376 | tf_op jit(solution)/shard_map/ppermute | solution.py:320
  7.4 2.1 %collective-permute-start.3 = (f32[4,768]{1,0:T(4,128)S(1)}, f32[4,768]{1,0:T(4,128)S(1)}, u32[]{:S(2)}, u32[]{:S(2)}) collective-permute-start(f32[4,768]{1,0:T(4,128)S(1)} %get-tuple-element.20), channel_id=1, source_target_pairs={{0,4},{4,8},{8,12},{12,16},{16,20},{20,24},{24,28},{28,32},{32,36}... | collective-permute-start | bytes 36872 | tf_op jit(solution)/shard_map/ppermute | solution.py:320
  9.4 0.0 collective-permute-start.4
  9.5 2.9 %collective-permute-start.2 = (f32[3,8,8,128]{3,2,1,0:T(8,128)S(1)}, f32[3,8,8,128]{3,2,1,0:T(8,128)S(1)}, u32[]{:S(2)}, u32[]{:S(2)}) collective-permute-start(f32[3,8,8,128]{3,2,1,0:T(8,128)S(1)} %get-tuple-element.19), channel_id=1, source_target_pairs={{0,64},{64,0},{1,65},{65,1},{2,66},{66,2},{3,67},{67,3},{4,68},{68... | collective-permute-start | bytes 294920 | tf_op jit(solution)/shard_map/ppermute | solution.py:320
  12.4 0.1 pad_add_fusion.places
  12.4 0.4 collective-permute-done.4.from_right
  12.9 1.6 %collective-permute-done.2.ends_ref = f32[3,8,8,128]{3,2,1,0:T(8,128)S(1)} collective-permute-done((f32[3,8,8,128]{3,2,1,0:T(8,128)S(1)}, f32[3,8,8,128]{3,2,1,0:T(8,128)S(1)}, u32[]{:S(2)}, u32[]{:S(2)}) %collective-permute-start.2) | collective-permute-done | bytes 98336 | tf_op jit(solution)/shard_map/ppermute | solution.py:320
  14.4 0.0 collective-permute-done.1.high_ref
  14.4 1.0 %copy-done.3 = f32[3,8,32,128]{3,2,1,0:T(8,128)S(1)} copy-done((f32[3,8,32,128]{3,2,1,0:T(8,128)S(1)}, f32[3,8,32,128]{3,2,1,0:T(8,128)}, u32[]{:S(2)}) %copy-start.3) | copy-done | bytes 393240
  15.4 0.9 %copy-done.4 = f32[128,256]{1,0:T(8,128)S(1)} copy-done((f32[128,256]{1,0:T(8,128)S(1)}, f32[128,256]{1,0:T(8,128)}, u32[]{:S(2)}) %copy-start.4) | copy-done | bytes 131096
  16.3 0.7 %copy-done.7 = f32[8,256]{1,0:T(8,128)S(1)} copy-done((f32[8,256]{1,0:T(8,128)S(1)}, f32[8,256]{1,0:T(8,128)}, u32[]{:S(2)}) %copy-start.7) | copy-done | bytes 8216
  17.0 3.2 %flow.1 = (f32[3,8,32,128]{3,2,1,0:T(8,128)}, f32[3,8,32,128]{3,2,1,0:T(8,128)S(1)}) custom-call(s32[3]{0:T(128)S(1)} %pad_add_fusion.places, f32[3,8,32,128]{3,2,1,0:T(8,128)S(1)} %copy-done.3, f32[3,3,32,128]{3,2,1,0:T(8,128)S(1)} %collective-permute-done.low_ref, f32[3,3,32,128]{3,2,1,0:T(8,128)S(1)} %collective-permute-done.1.high_ref, ...), custom_call_target="tpu_custom_call" | custom-call | tf_op jit(solution)/shard_map/flow/pallas_call | solution.py:353
  20.2 2.9 %collective-permute-start.5 = (f32[3,8,32,128]{3,2,1,0:T(8,128)S(1)}, f32[3,8,32,128]{3,2,1,0:T(8,128)S(1)}, u32[]{:S(2)}, u32[]{:S(2)}) collective-permute-start(f32[3,8,32,128]{3,2,1,0:T(8,128)S(1)} %get-tuple-element.23.own_ref), channel_id=1, source_target_pairs={{0,64},{64,0},{1,65},{65,1},{2,66},{66,2},{3,67},{67,3},{4,68},{68... | collective-permute-start | bytes 1179656 | tf_op jit(solution)/shard_map/ppermute | solution.py:320
  23.2 1.4 %copy-done = f32[2,3,8,64,128]{4,3,2,1,0:T(8,128)S(1)} copy-done((f32[2,3,8,64,128]{4,3,2,1,0:T(8,128)S(1)}, f32[2,3,8,64,128]{4,3,2,1,0:T(8,128)}, u32[]{:S(2)}) %copy-start) | copy-done | bytes 1572888
  24.6 0.1 faces.1
  24.7 0.0 copy-start.5
  24.7 0.0 copy-start.6
  24.7 0.1 collective-permute-start.6
  24.8 2.7 %collective-permute-start.7 = (f32[2,3,3,64,128]{4,3,2,1,0:T(8,128)S(1)}, f32[2,3,3,64,128]{4,3,2,1,0:T(8,128)S(1)}, u32[]{:S(2)}, u32[]{:S(2)}) collective-permute-start(f32[2,3,3,64,128]{4,3,2,1,0:T(8,128)S(1)} %get-tuple-element.27), channel_id=1, source_target_pairs={{0,3},{1,0},{2,1},{3,2},{4,7},{5,4},{6,5},{7,6},{8,11},{9,8},{10,9... | collective-permute-start | bytes 1769480 | tf_op jit(solution)/shard_map/ppermute | solution.py:320
  27.4 0.9 %collective-permute-done.5.other_ref = f32[3,8,32,128]{3,2,1,0:T(8,128)S(1)} collective-permute-done((f32[3,8,32,128]{3,2,1,0:T(8,128)S(1)}, f32[3,8,32,128]{3,2,1,0:T(8,128)S(1)}, u32[]{:S(2)}, u32[]{:S(2)}) %collective-permute-start.5) | collective-permute-done | bytes 393248 | tf_op jit(solution)/shard_map/ppermute | solution.py:320
  28.4 3.0 %cross.1 = (f32[2,3,8,64,128]{4,3,2,1,0:T(8,128)S(1)}, f32[3,3,64,128]{3,2,1,0:T(8,128)S(1)}, f32[3,3,64,128]{3,2,1,0:T(8,128)S(1)}, f32[4,3072]{1,0:T(4,128)S(1)}, f32[4,3072]{1,0:T(4,128)S(1)}) custom-call(s32[3]{0:T(128)S(1)} %pad_add_fusion.places, f32[2,3,8,64,128]{4,3,2,1,0:T(8,128)S(1)} %copy-done.1, f32[3,8,32,128]{3,2,1,0:T(8,128)S(1)} %get-tuple-element.23.own_ref, ...), custom_call_target="tpu_custom_call" | custom-call | tf_op jit(solution)/shard_map/cross/pallas_call | solution.py:386
  31.4 2.7 %collective-permute-start.9 = (f32[3,3,64,128]{3,2,1,0:T(8,128)S(1)}, f32[3,3,64,128]{3,2,1,0:T(8,128)S(1)}, u32[]{:S(2)}, u32[]{:S(2)}) collective-permute-start(f32[3,3,64,128]{3,2,1,0:T(8,128)S(1)} %get-tuple-element.29), channel_id=1, source_target_pairs={{0,3},{1,0},{2,1},{3,2},{4,7},{5,4},{6,5},{7,6},{8,11},{9,8},{10,9... | collective-permute-start | bytes 884744 | tf_op jit(solution)/shard_map/ppermute | solution.py:320
  34.1 6.6 %collective-permute-start.10 = (f32[4,3072]{1,0:T(4,128)S(1)}, f32[4,3072]{1,0:T(4,128)S(1)}, u32[]{:S(2)}, u32[]{:S(2)}) collective-permute-start(f32[4,3072]{1,0:T(4,128)S(1)} %get-tuple-element.30), channel_id=1, source_target_pairs={{0,4},{4,8},{8,12},{12,16},{16,20},{20,24},{24,28},{28,32},{32,36}... | collective-permute-start | bytes 147464 | tf_op jit(solution)/shard_map/ppermute | solution.py:320
  40.7 1.2 %collective-permute-done.10.from_left = f32[4,3072]{1,0:T(4,128)S(1)} collective-permute-done((f32[4,3072]{1,0:T(4,128)S(1)}, f32[4,3072]{1,0:T(4,128)S(1)}, u32[]{:S(2)}, u32[]{:S(2)}) %collective-permute-start.10) | collective-permute-done | bytes 49184 | tf_op jit(solution)/shard_map/ppermute | solution.py:320
  41.8 3.5 %collective-permute-start.11 = (f32[4,3072]{1,0:T(4,128)S(1)}, f32[4,3072]{1,0:T(4,128)S(1)}, u32[]{:S(2)}, u32[]{:S(2)}) collective-permute-start(f32[4,3072]{1,0:T(4,128)S(1)} %get-tuple-element.31), channel_id=1, source_target_pairs={{0,60},{4,0},{8,4},{12,8},{16,12},{20,16},{24,20},{28,24},{32,28},... | collective-permute-start | bytes 147464 | tf_op jit(solution)/shard_map/ppermute | solution.py:320
  45.3 3.4 %local.1.part_ref = f32[2,3,8,64,128]{4,3,2,1,0:T(8,128)S(1)} custom-call(f32[2,3,8,64,128]{4,3,2,1,0:T(8,128)S(1)} %copy-done.1, f32[2,3,8,64,128]{4,3,2,1,0:T(8,128)S(1)} %get-tuple-element.24.cross_ref, f32[128,128]{1,0:T(8,128)S(1)} %copy-done.6, f32[128,128]{1,0:T(8,128)S(1)} %copy-done.5), custom_call_target="tpu_custom_call" | custom-call | flops 1000000000 | bytes 6000000 | tf_op jit(solution)/shard_map/local/pallas_call | solution.py:403
  48.8 3.3 %finish.1 = f32[2,3,8,64,128]{4,3,2,1,0:T(8,128)} custom-call(s32[3]{0:T(128)S(1)} %pad_add_fusion.places, f32[2,3,8,64,128]{4,3,2,1,0:T(8,128)S(1)} %local.1.part_ref, f32[2,3,3,64,128]{4,3,2,1,0:T(8,128)S(1)} %collective-permute-done.6.t_low_ref, f32[2,3,3,64,128]{4,3,2,1,0:T(8,128)S(1)} %collective-permute-done.7.t_high_ref, ...), custom_call_target="tpu_custom_call" | custom-call | tf_op jit(solution)/shard_map/finish/pallas_call | solution.py:414
  (21 shorter events, 0.0 us)
Async XLA Ops:
  0.6 1.0 %copy-start.2 = (f32[3,8,32,128]{3,2,1,0:T(8,128)S(1)}, f32[3,8,32,128]{3,2,1,0:T(8,128)}, u32[]{:S(2)}) copy-start(f32[3,8,32,128]{3,2,1,0:T(8,128)} %v_ref.3) | copy-start | bytes 1179652
  1.6 0.7 %copy-start.10 = (f32[8,128]{1,0:T(8,128)S(1)}, f32[8,128]{1,0:T(8,128)}, u32[]{:S(2)}) copy-start(f32[8,128]{1,0:T(8,128)} %constant.30.clone.pick_ref) | copy-start | bytes 12292
  2.3 26.1 %copy-start.8 = (f32[2,8,128]{2,1,0:T(8,128)S(1)}, f32[2,8,128]{2,1,0:T(8,128)}, u32[]{:S(2)}) copy-start(f32[2,8,128]{2,1,0:T(8,128)} %constant.32.clone.lay_ref) | copy-start | bytes 24580
  2.8 11.7 %collective-permute-start = (f32[3,3,32,128]{3,2,1,0:T(8,128)S(1)}, f32[3,3,32,128]{3,2,1,0:T(8,128)S(1)}, u32[]{:S(2)}, u32[]{:S(2)}) collective-permute-start(f32[3,3,32,128]{3,2,1,0:T(8,128)S(1)} %get-tuple-element.17), channel_id=1, source_target_pairs={{0,1},{1,2},{2,3},{3,0},{4,5},{5,6},{6,7},{7,4},{8,9},{9,10},{10,1... | collective-permute-start | bytes 442376 | tf_op jit(solution)/shard_map/ppermute | solution.py:320
  5.2 9.2 %collective-permute-start.1 = (f32[3,3,32,128]{3,2,1,0:T(8,128)S(1)}, f32[3,3,32,128]{3,2,1,0:T(8,128)S(1)}, u32[]{:S(2)}, u32[]{:S(2)}) collective-permute-start(f32[3,3,32,128]{3,2,1,0:T(8,128)S(1)} %get-tuple-element.18), channel_id=1, source_target_pairs={{0,3},{1,0},{2,1},{3,2},{4,7},{5,4},{6,5},{7,6},{8,11},{9,8},{10,9... | collective-permute-start | bytes 442376 | tf_op jit(solution)/shard_map/ppermute | solution.py:320
  7.4 5.0 %collective-permute-start.3 = (f32[4,768]{1,0:T(4,128)S(1)}, f32[4,768]{1,0:T(4,128)S(1)}, u32[]{:S(2)}, u32[]{:S(2)}) collective-permute-start(f32[4,768]{1,0:T(4,128)S(1)} %get-tuple-element.20), channel_id=1, source_target_pairs={{0,4},{4,8},{8,12},{12,16},{16,20},{20,24},{24,28},{28,32},{32,36}... | collective-permute-start | bytes 36872 | tf_op jit(solution)/shard_map/ppermute | solution.py:320
  9.4 3.4 %collective-permute-start.4 = (f32[4,768]{1,0:T(4,128)S(1)}, f32[4,768]{1,0:T(4,128)S(1)}, u32[]{:S(2)}, u32[]{:S(2)}) collective-permute-start(f32[4,768]{1,0:T(4,128)S(1)} %get-tuple-element.21), channel_id=1, source_target_pairs={{0,60},{4,0},{8,4},{12,8},{16,12},{20,16},{24,20},{28,24},{32,28},... | collective-permute-start | bytes 36872 | tf_op jit(solution)/shard_map/ppermute | solution.py:320
  9.5 5.0 %collective-permute-start.2 = (f32[3,8,8,128]{3,2,1,0:T(8,128)S(1)}, f32[3,8,8,128]{3,2,1,0:T(8,128)S(1)}, u32[]{:S(2)}, u32[]{:S(2)}) collective-permute-start(f32[3,8,8,128]{3,2,1,0:T(8,128)S(1)} %get-tuple-element.19), channel_id=1, source_target_pairs={{0,64},{64,0},{1,65},{65,1},{2,66},{66,2},{3,67},{67,3},{4,68},{68... | collective-permute-start | bytes 294920 | tf_op jit(solution)/shard_map/ppermute | solution.py:320
  14.4 1.0 %copy-start.3 = (f32[3,8,32,128]{3,2,1,0:T(8,128)S(1)}, f32[3,8,32,128]{3,2,1,0:T(8,128)}, u32[]{:S(2)}) copy-start(f32[3,8,32,128]{3,2,1,0:T(8,128)} %v_ref.3) | copy-start | bytes 1179652
  15.4 0.9 %copy-start.4 = (f32[128,256]{1,0:T(8,128)S(1)}, f32[128,256]{1,0:T(8,128)}, u32[]{:S(2)}) copy-start(f32[128,256]{1,0:T(8,128)} %constant.29.clone.inner_ref) | copy-start | bytes 393220
  16.3 0.7 %copy-start.7 = (f32[8,256]{1,0:T(8,128)S(1)}, f32[8,256]{1,0:T(8,128)}, u32[]{:S(2)}) copy-start(f32[8,256]{1,0:T(8,128)} %constant.31.clone.spread_ref) | copy-start | bytes 24580
  20.2 8.1 %collective-permute-start.5 = (f32[3,8,32,128]{3,2,1,0:T(8,128)S(1)}, f32[3,8,32,128]{3,2,1,0:T(8,128)S(1)}, u32[]{:S(2)}, u32[]{:S(2)}) collective-permute-start(f32[3,8,32,128]{3,2,1,0:T(8,128)S(1)} %get-tuple-element.23.own_ref), channel_id=1, source_target_pairs={{0,64},{64,0},{1,65},{65,1},{2,66},{66,2},{3,67},{67,3},{4,68},{68... | collective-permute-start | bytes 1179656 | tf_op jit(solution)/shard_map/ppermute | solution.py:320
  23.2 1.4 %copy-start = (f32[2,3,8,64,128]{4,3,2,1,0:T(8,128)S(1)}, f32[2,3,8,64,128]{4,3,2,1,0:T(8,128)}, u32[]{:S(2)}) copy-start(f32[2,3,8,64,128]{4,3,2,1,0:T(8,128)} %tests_ref.4) | copy-start | bytes 4718596
  24.6 3.8 %copy-start.1 = (f32[2,3,8,64,128]{4,3,2,1,0:T(8,128)S(1)}, f32[2,3,8,64,128]{4,3,2,1,0:T(8,128)}, u32[]{:S(2)}) copy-start(f32[2,3,8,64,128]{4,3,2,1,0:T(8,128)} %tests_ref.4) | copy-start | bytes 4718596
  24.7 20.7 %copy-start.5 = (f32[128,128]{1,0:T(8,128)S(1)}, f32[128,128]{1,0:T(8,128)}, u32[]{:S(2)}) copy-start(f32[128,128]{1,0:T(8,128)} %constant.35.clone.second_ref) | copy-start | bytes 196612
  24.7 20.7 %copy-start.6 = (f32[128,128]{1,0:T(8,128)S(1)}, f32[128,128]{1,0:T(8,128)}, u32[]{:S(2)}) copy-start(f32[128,128]{1,0:T(8,128)} %constant.34.clone.first_ref) | copy-start | bytes 196612
  24.7 24.1 %collective-permute-start.6 = (f32[2,3,3,64,128]{4,3,2,1,0:T(8,128)S(1)}, f32[2,3,3,64,128]{4,3,2,1,0:T(8,128)S(1)}, u32[]{:S(2)}, u32[]{:S(2)}) collective-permute-start(f32[2,3,3,64,128]{4,3,2,1,0:T(8,128)S(1)} %get-tuple-element.26), channel_id=1, source_target_pairs={{0,1},{1,2},{2,3},{3,0},{4,5},{5,6},{6,7},{7,4},{8,9},{9,10},{10,1... | collective-permute-start | bytes 1769480 | tf_op jit(solution)/shard_map/ppermute | solution.py:320
  24.8 24.0 %collective-permute-start.7 = (f32[2,3,3,64,128]{4,3,2,1,0:T(8,128)S(1)}, f32[2,3,3,64,128]{4,3,2,1,0:T(8,128)S(1)}, u32[]{:S(2)}, u32[]{:S(2)}) collective-permute-start(f32[2,3,3,64,128]{4,3,2,1,0:T(8,128)S(1)} %get-tuple-element.27), channel_id=1, source_target_pairs={{0,3},{1,0},{2,1},{3,2},{4,7},{5,4},{6,5},{7,6},{8,11},{9,8},{10,9... | collective-permute-start | bytes 1769480 | tf_op jit(solution)/shard_map/ppermute | solution.py:320
  31.4 17.4 %collective-permute-start.8 = (f32[3,3,64,128]{3,2,1,0:T(8,128)S(1)}, f32[3,3,64,128]{3,2,1,0:T(8,128)S(1)}, u32[]{:S(2)}, u32[]{:S(2)}) collective-permute-start(f32[3,3,64,128]{3,2,1,0:T(8,128)S(1)} %get-tuple-element.28), channel_id=1, source_target_pairs={{0,1},{1,2},{2,3},{3,0},{4,5},{5,6},{6,7},{7,4},{8,9},{9,10},{10,1... | collective-permute-start | bytes 884744 | tf_op jit(solution)/shard_map/ppermute | solution.py:320
  31.4 17.4 %collective-permute-start.9 = (f32[3,3,64,128]{3,2,1,0:T(8,128)S(1)}, f32[3,3,64,128]{3,2,1,0:T(8,128)S(1)}, u32[]{:S(2)}, u32[]{:S(2)}) collective-permute-start(f32[3,3,64,128]{3,2,1,0:T(8,128)S(1)} %get-tuple-element.29), channel_id=1, source_target_pairs={{0,3},{1,0},{2,1},{3,2},{4,7},{5,4},{6,5},{7,6},{8,11},{9,8},{10,9... | collective-permute-start | bytes 884744 | tf_op jit(solution)/shard_map/ppermute | solution.py:320
  34.1 7.7 %collective-permute-start.10 = (f32[4,3072]{1,0:T(4,128)S(1)}, f32[4,3072]{1,0:T(4,128)S(1)}, u32[]{:S(2)}, u32[]{:S(2)}) collective-permute-start(f32[4,3072]{1,0:T(4,128)S(1)} %get-tuple-element.30), channel_id=1, source_target_pairs={{0,4},{4,8},{8,12},{12,16},{16,20},{20,24},{24,28},{28,32},{32,36}... | collective-permute-start | bytes 147464 | tf_op jit(solution)/shard_map/ppermute | solution.py:320
  41.8 6.9 %collective-permute-start.11 = (f32[4,3072]{1,0:T(4,128)S(1)}, f32[4,3072]{1,0:T(4,128)S(1)}, u32[]{:S(2)}, u32[]{:S(2)}) collective-permute-start(f32[4,3072]{1,0:T(4,128)S(1)} %get-tuple-element.31), channel_id=1, source_target_pairs={{0,60},{4,0},{8,4},{12,8},{16,12},{20,16},{24,20},{28,24},{32,28},... | collective-permute-start | bytes 147464 | tf_op jit(solution)/shard_map/ppermute | solution.py:320
  45.3 3.5 %copy-start.9 = (f32[8,128]{1,0:T(8,128)S(1)}, f32[8,128]{1,0:T(8,128)}, u32[]{:S(2)}) copy-start(f32[8,128]{1,0:T(8,128)} %constant.33.clone.land_ref) | copy-start | bytes 12292

commit v2 on v0

v2 whole, which is shorter than its diff:
```python
import math

import jax
import jax.numpy as jnp
import numpy as np
from jax import lax
from jax.experimental import pallas as pl
from jax.experimental.pallas import tpu as pltpu
from jax.sharding import PartitionSpec as P

STEP = 0.2
VISC = 0.1
DIFF = 0.1
FIRST = (45.0 / 60.0, -9.0 / 60.0, 1.0 / 60.0)
SECOND = (270.0 / 180.0, -27.0 / 180.0, 2.0 / 180.0)
MID = -490.0 / 180.0
ROOT = math.sqrt(5.0 / 9.0)
DECAY = -(1.0 - ROOT) / (2.0 / 3.0)
VMEM_LIMIT = 48 * 1024 * 1024
F32 = jnp.float32
BF16 = jnp.bfloat16


def compact_weight(distance):
    d = np.asarray(distance)

    def green(k):
        return DECAY ** np.abs(k) / ROOT

    return 7.0 / 9.0 * (green(d + 1) - green(d - 1)) + 1.0 / 36.0 * (green(d + 2) - green(d - 2))


def second_weight(distance):
    table = np.array([MID, *SECOND, 0.0])
    return table[np.minimum(np.abs(distance), 4)]


TAIL = float(compact_weight(2)) / DECAY**2
CORNER = float(compact_weight(1)) - TAIL * DECAY


def halves(table):
    table = np.asarray(table, np.float32)
    high = np.asarray(np.asarray(table, jnp.bfloat16), np.float32)
    low = np.asarray(np.asarray(table - high, jnp.bfloat16), np.float32)
    return high, low


def make_tables(n, x_total, y_total, z_total):
    j = np.arange(n)
    gap = j[None, :] - j[:, None]
    inner_first = compact_weight(gap)
    inner_second = second_weight(gap)
    pick = np.zeros((8, n))
    for k in range(3):
        pick[k, n - 1 - k] = 1.0
        pick[4 + k, k] = 1.0
    pick[3] = DECAY ** (n - 1 - j)
    pick[7] = DECAY**j
    spread_first = np.zeros((8, n))
    spread_second = np.zeros((8, n))
    for k in range(3):
        for z in range(3 - k):
            spread_second[k, z] = SECOND[z + k]
            spread_second[4 + k, n - 1 - z] = SECOND[z + k]
    spread_first[0, 0] = CORNER
    spread_first[4, n - 1] = -CORNER
    spread_first[3] = TAIL * DECAY ** (j + 1)
    spread_first[7] = -TAIL * DECAY ** (n - j)
    lay_test = np.zeros((8, n))
    lay_cross = np.zeros((8, n))
    for z in range(3):
        for k in range(3 - z):
            lay_test[z, n - 1 - k] = STEP * DIFF * SECOND[z + k]
            lay_test[4 + z, k] = STEP * DIFF * SECOND[z + k]
    lay_cross[0, n - 1] = STEP * CORNER
    lay_cross[4, 0] = -STEP * CORNER
    lay_cross[3] = STEP * DECAY ** (n - 1 - j)
    lay_cross[7] = STEP * DECAY**j
    land = np.zeros((8, n))
    for z in range(3):
        land[z, z] = 1.0
        land[4 + z, n - 1 - z] = 1.0
    land[3] = spread_first[3]
    land[7] = spread_first[7]

    def stacked(table):
        high, low = halves(table)
        return np.concatenate([high, high, low, np.zeros_like(high)])

    def wide(column):
        return np.broadcast_to(np.asarray(column)[:, None], (len(column), n))

    phase_x = 2.0 * math.pi / x_total * np.arange(x_total)
    phase_y = 2.0 * math.pi / y_total * np.arange(y_total)
    angle = 2.0 * math.pi / z_total * np.arange(z_total)
    parts = {
        "pick": np.concatenate(halves(pick)),
        "lay_test": np.concatenate(halves(lay_test)),
        "lay_cross": np.concatenate(halves(lay_cross)),
        "spread_first": stacked(spread_first),
        "spread_second": stacked(spread_second),
        "land": stacked(land),
        "flow_first": np.concatenate(halves(inner_first)),
        "flow_second": np.concatenate(halves(inner_second)),
        "test_first": np.concatenate(halves(STEP * inner_first)),
        "test_second": np.concatenate(halves(STEP * DIFF * inner_second)),
        "sin_x": wide(np.sin(phase_x)),
        "cos_x": wide(np.cos(phase_x)),
        "sin_y": wide(np.sin(phase_y)),
        "cos_y": wide(np.cos(phase_y)),
        "wave": np.concatenate([np.cos(angle), np.sin(angle)]).reshape(-1, n),
    }
    places, rows = {}, 0
    for name, part in parts.items():
        places[name] = (rows, len(part))
        rows += len(part)
    return np.concatenate(list(parts.values())).astype(np.float32), places


def split(values):
    high = values.astype(BF16)
    low = (values - high.astype(F32)).astype(BF16)
    return high, low


def dot(a, b):
    return jnp.dot(a, b, preferred_element_type=F32)


def three(values, high, low):
    a, b = split(values)
    return dot(a, high) + dot(b, high) + dot(a, low)


def lines_out(values, both):
    a, b = split(values)
    nt = (((1,), (1,)), ((), ()))
    main = lax.dot_general(both, a, nt, preferred_element_type=F32)
    rest = lax.dot_general(both, b, nt, preferred_element_type=F32)
    return main[0:8] + main[8:16] + rest[0:8]


def lines_in(raw, tables):
    high = raw.astype(BF16).astype(F32)
    low = raw - high
    packed = jnp.concatenate([high, low, high, jnp.zeros_like(high)], 0).astype(BF16)
    return lax.dot_general(packed, tables, (((0,), (0,)), ((), ())), preferred_element_type=F32)


class Tables:
    def __init__(self, ref, places):
        self.ref = ref
        self.places = places

    def get(self, name):
        start, rows = self.places[name]
        return self.ref[start : start + rows]

    def pair(self, name):
        start, rows = self.places[name]
        half = rows // 2
        return self.ref[start : start + half].astype(BF16), self.ref[start + half : start + rows].astype(BF16)

    def row(self, name, index):
        return self.ref[pl.ds(self.places[name][0] + index, 1)]


def in_chip():
    return lax.rem(lax.axis_index("gz"), 2) == 0


def hand_out(sent, inner_ref, outer_ref):
    even = in_chip()
    inner_ref[...] = jnp.where(even, sent[0:4], sent[4:8])
    outer_ref[...] = jnp.where(even, sent[4:8], sent[0:4])


def taken_in(inner_ref, outer_ref):
    even = in_chip()
    left = jnp.where(even, outer_ref[...], inner_ref[...])
    right = jnp.where(even, inner_ref[...], outer_ref[...])
    return jnp.concatenate([left, right], 0)


def wave_parts(tables, problem, slabs):
    wave = tables.row("wave", problem * slabs + lax.axis_index("gz"))
    first = lax.axis_index("sec") == 0
    return jnp.where(first, wave, 0.0), jnp.where(first, 0.0, wave)


def wrap(pad, k, values):
    ny = values.shape[0]
    pad[k, 0:8] = values[ny - 8 : ny]
    pad[k, 8 : 8 + ny] = values
    pad[k, 8 + ny : 16 + ny] = values[0:8]


def tables_kernel(source, out):
    out[...] = source[...]


def faces_kernel(tests_ref, low_ref, high_ref):
    nx = tests_ref.shape[2]
    low_ref[...] = tests_ref[:, :, 0:3]
    high_ref[...] = tests_ref[:, :, nx - 3 : nx]


def spread_kernel(places, tests_ref, tables_ref, out_ref, sent_ref, pad):
    problems, _, nx, ny, n = tests_ref.shape
    tables = Tables(tables_ref, places)
    high, low = tables.pair("test_second")
    lay = tables.get("lay_test").astype(BF16)
    lines = nx * ny
    for p in range(problems):
        for c in range(3):
            flat = tests_ref[p, c].reshape(lines, n)
            out_ref[p, c] = three(flat, high, low).reshape(nx, ny, n)
            at = (3 * p + c) * lines
            sent_ref[:, at : at + lines] = lines_out(flat, lay)
        for i in range(nx):
            for c in range(3):
                wrap(pad, c, tests_ref[p, c, i])
            for c in range(3):
                value = out_ref[p, c, i] + (1.0 + STEP * DIFF * 2.0 * MID) * tests_ref[p, c, i]
                for k, w in zip((1, 2, 3), SECOND):
                    near = pad[c, 8 + k : 8 + k + ny] + pad[c, 8 - k : 8 - k + ny]
                    for j in (i + k, i - k):
                        if 0 <= j < nx:
                            near = near + tests_ref[p, c, j]
                    value = value + (STEP * DIFF * w) * near
                out_ref[p, c, i] = value


def whole_kernel(places, own_ref, other_ref, tables_ref, whole_ref, low_ref, high_ref, inner_ref, outer_ref):
    _, nx, half, n = own_ref.shape
    section = lax.axis_index("sec")
    whole_ref[:, :, pl.ds(pl.multiple_of(section * half, half), half)] = own_ref[...]
    whole_ref[:, :, pl.ds(pl.multiple_of((1 - section) * half, half), half)] = other_ref[...]
    low_ref[...] = whole_ref[:, 0:3]
    high_ref[...] = whole_ref[:, nx - 3 : nx]
    pick = Tables(tables_ref, places).get("pick").astype(BF16)
    hand_out(lines_out(whole_ref[...].reshape(-1, n), pick), inner_ref, outer_ref)


def flow_kernel(places, whole_ref, tables_ref, acc_ref, pad, grad_z, lap_z):
    _, nx, ny, n = whole_ref.shape
    tables = Tables(tables_ref, places)
    flat = whole_ref[...].reshape(-1, n)
    grad_z[...] = three(flat, *tables.pair("flow_first")).reshape(grad_z.shape)
    lap_z[...] = three(flat, *tables.pair("flow_second")).reshape(lap_z.shape)
    sin_y, cos_y = tables.get("sin_y"), tables.get("cos_y")
    column = lax.axis_index("gx") * nx
    for i in range(nx):
        sin_x, cos_x = tables.row("sin_x", column + i), tables.row("cos_x", column + i)
        drive = (sin_x * cos_y, -(cos_x * sin_y), math.sqrt(2.0) * (sin_x * sin_y))
        for c in range(3):
            wrap(pad, c, whole_ref[c, i])
        own = [whole_ref[c, i] for c in range(3)]
        for c in range(3):
            grad_x = grad_y = None
            lap = lap_z[c, i] + (2.0 * MID) * own[c]
            for k, first, second in zip((1, 2, 3), FIRST, SECOND):
                up, down = pad[c, 8 + k : 8 + k + ny], pad[c, 8 - k : 8 - k + ny]
                term = first * (up - down)
                grad_y = term if grad_y is None else grad_y + term
                near = up + down
                for j, sign in ((i + k, first), (i - k, -first)):
                    if 0 <= j < nx:
                        value = whole_ref[c, j]
                        near = near + value
                        grad_x = sign * value if grad_x is None else grad_x + sign * value
                lap = lap + second * near
            advect = own[0] * grad_x + own[1] * grad_y + own[2] * grad_z[c, i]
            acc_ref[c, i] = own[c] + STEP * (VISC * lap - advect + drive[c])


def step_kernel(
    places, whole_ref, acc_ref, low_ref, high_ref, inner_in, outer_in, tests_ref, sent_ref, tables_ref,
    next_ref, cross_ref, low_out, high_out, inner_out, outer_out, moved_ref, grad_z, lap_z,
):
    _, nx, ny, n = whole_ref.shape
    half = ny // 2
    problems = tests_ref.shape[0]
    tables = Tables(tables_ref, places)
    raw = taken_in(inner_in, outer_in)
    grad_z[...] = lines_in(raw, tables.get("spread_first").astype(BF16)).reshape(grad_z.shape)
    lap_z[...] = lines_in(raw, tables.get("spread_second").astype(BF16)).reshape(lap_z.shape)
    mine = pl.ds(pl.multiple_of(lax.axis_index("sec") * half, half), half)
    waves = [wave_parts(tables, p, places["wave"][1] // 2) for p in range(problems)]
    for i in range(nx):
        own = [whole_ref[c, i] for c in range(3)]
        centred = []
        for c in range(3):
            lap, grad_x = lap_z[c, i], None
            for k, first, second in zip((1, 2, 3), FIRST, SECOND):
                for j, sign in ((i + k, first), (i - k, -first)):
                    if not 0 <= j < nx:
                        value = low_ref[c, j + 3] if j < 0 else high_ref[c, j - nx]
                        lap = lap + second * value
                        grad_x = sign * value if grad_x is None else grad_x + sign * value
            advect = own[2] * grad_z[c, i]
            if grad_x is not None:
                advect = advect + own[0] * grad_x
            moved = acc_ref[c, i] + STEP * (VISC * lap - advect)
            moved_ref[c, i] = moved
            next_ref[c, i] = moved_ref[c, i, mine]
            centred.append(0.5 * (own[c] + moved))
            if i < 3:
                low_out[c, i] = centred[c]
            if i >= nx - 3:
                high_out[c, i - nx + 3] = centred[c]
        cx, cy, cz = centred
        for p in range(problems):
            tx, ty, tz = tests_ref[p, 0, i] + waves[p][0], tests_ref[p, 1, i] + waves[p][1], tests_ref[p, 2, i]
            cross_ref[p, 0, i] = cx * tz - cz * tx
            cross_ref[p, 1, i] = cy * tz - cz * ty
            cross_ref[p, 2, i] = cx * ty - cy * tx
    lay = tables.get("lay_cross").astype(BF16)
    lines = nx * ny
    even = in_chip()
    for p in range(problems):
        at = 3 * p * lines
        added = lines_out(cross_ref[p, 0:2].reshape(-1, n), lay)
        for start, stop, sent in (
            (at, at + 2 * lines, sent_ref[:, at : at + 2 * lines] + added),
            (at + 2 * lines, at + 3 * lines, sent_ref[:, at + 2 * lines : at + 3 * lines]),
        ):
            inner_out[:, start:stop] = jnp.where(even, sent[0:4], sent[4:8])
            outer_out[:, start:stop] = jnp.where(even, sent[4:8], sent[0:4])


def curl_kernel(places, part_ref, cross_ref, low_ref, high_ref, tables_ref, out_ref, pad):
    problems, _, nx, ny, n = part_ref.shape
    tables = Tables(tables_ref, places)
    high, low = tables.pair("test_first")
    for p in range(problems):
        for c in range(2):
            total = three(cross_ref[p, c].reshape(-1, n), high, low)
            out_ref[p, c] = part_ref[p, c] + total.reshape(nx, ny, n)
        for i in range(nx):
            wrap(pad, 0, cross_ref[p, 1, i])
            wrap(pad, 1, cross_ref[p, 2, i])
            value = [out_ref[p, 0, i], out_ref[p, 1, i], part_ref[p, 2, i]]
            for k, first, second in zip((1, 2, 3), FIRST, SECOND):
                w = STEP * first
                value[0] = value[0] + w * (pad[1, 8 + k : 8 + k + ny] - pad[1, 8 - k : 8 - k + ny])
                value[2] = value[2] - w * (pad[0, 8 + k : 8 + k + ny] - pad[0, 8 - k : 8 - k + ny])
                for j, sign in ((i + k, w), (i - k, -w)):
                    if 0 <= j < nx:
                        value[1] = value[1] - sign * cross_ref[p, 2, j]
                        value[2] = value[2] - sign * cross_ref[p, 0, j]
                    else:
                        face, h = (low_ref, j + 3) if j < 0 else (high_ref, j - nx)
                        for c in range(3):
                            value[c] = value[c] + (STEP * DIFF * second) * face[p, c, h]
            for c in range(3):
                out_ref[p, c, i] = value[c]


def finish_kernel(
    places, part_ref, t_low_ref, t_high_ref, c_low_ref, c_high_ref, inner_in, outer_in, tables_ref,
    out_ref, held, cross, sems,
):
    problems, _, nx, ny, n = part_ref.shape
    tables = Tables(tables_ref, places)
    land = tables.get("land").astype(BF16)
    raw = taken_in(inner_in, outer_in)
    lines = nx * ny
    copies = []
    for p in range(problems):
        wave_x, wave_y = wave_parts(tables, p, places["wave"][1] // 2)
        for c in range(3):
            at = (3 * p + c) * lines
            held[p, c] = part_ref[p, c] + lines_in(raw[:, at : at + lines], land).reshape(nx, ny, n)
            if c == 0:
                copies.append(pltpu.make_async_copy(held.at[p, c], out_ref.at[p, c], sems.at[3 * p + c]))
                copies[-1].start()
        for side, (t_ref, c_ref) in enumerate(((t_low_ref, c_low_ref), (t_high_ref, c_high_ref))):
            for h in range(3):
                cx, cy, cz = c_ref[0, h], c_ref[1, h], c_ref[2, h]
                tx, ty, tz = t_ref[p, 0, h] + wave_x, t_ref[p, 1, h] + wave_y, t_ref[p, 2, h]
                cross[0, h] = cz * tx - cx * tz
                cross[1, h] = cx * ty - cy * tx
            sign = -STEP if side == 0 else STEP
            for m in range(3):
                i = m if side == 0 else nx - 1 - m
                second, third = held[p, 1, i], held[p, 2, i]
                for d in range(m + 1, 4):
                    h = 3 + m - d if side == 0 else d - 1 - m
                    second = second - (sign * FIRST[d - 1]) * cross[1, h]
                    third = third + (sign * FIRST[d - 1]) * cross[0, h]
                held[p, 1, i] = second
                held[p, 2, i] = third
        for c in (1, 2):
            copies.append(pltpu.make_async_copy(held.at[p, c], out_ref.at[p, c], sems.at[3 * p + c]))
            copies[-1].start()
    for copy in copies:
        copy.wait()


def shifted(block, axis, distance):
    count = lax.axis_size(axis)
    return lax.ppermute(block, axis, [(i, (i + distance) % count) for i in range(count)])


def swapped(block, axis, first):
    count = lax.axis_size(axis)
    pairs = [(i % count, (i + 1) % count) for i in range(first, count + first, 2)]
    return lax.ppermute(block, axis, pairs + [(b, a) for a, b in pairs])


def shards(velocity, tests):
    _, nx, half, n = velocity.shape
    problems, _, _, ny, _ = tests.shape
    lines = nx * ny
    constants, places = make_tables(n, nx * lax.axis_size("gx"), ny, n * lax.axis_size("gz"))
    params = pltpu.CompilerParams(vmem_limit_bytes=VMEM_LIMIT)
    vmem = pl.BlockSpec(memory_space=pltpu.VMEM)

    def shape(*dims):
        return jax.ShapeDtypeStruct(dims, F32)

    def run(kernel, name, args, outs, scratch=(), flops=10**8, out_specs=None, bind=True):
        body = kernel if not bind else (lambda *refs: kernel(places, *refs))
        moved = 4 * sum(math.prod(a.shape) for a in (*args, *outs))
        return pl.pallas_call(
            body,
            in_specs=[vmem] * len(args),
            out_specs=[vmem] * len(outs) if out_specs is None else out_specs,
            out_shape=list(outs),
            scratch_shapes=list(scratch),
            compiler_params=params,
            cost_estimate=pl.CostEstimate(flops=flops, bytes_accessed=moved, transcendentals=0),
            name=name,
        )(*args)

    whole_shape = (3, nx, ny, n)
    tests_shape = (problems, 3, nx, ny, n)
    other = shifted(velocity, "sec", 1)
    (tables,) = run(tables_kernel, "tables", [jnp.asarray(constants)], [shape(*constants.shape)], bind=False)
    t_low, t_high = run(faces_kernel, "faces", [tests], [shape(problems, 3, 3, ny, n)] * 2, bind=False)
    t_from_low = shifted(t_high, "gx", 1)
    t_from_high = shifted(t_low, "gx", -1)
    part, sent = run(
        spread_kernel, "spread", [tests, tables],
        [shape(*tests_shape), shape(8, problems * 3 * lines)],
        [pltpu.VMEM((3, ny + 16, n), F32)], flops=10**9,
    )
    whole, low, high, inner, outer = run(
        whole_kernel, "whole", [velocity, other, tables],
        [shape(*whole_shape), shape(3, 3, ny, n), shape(3, 3, ny, n), shape(4, 3 * lines), shape(4, 3 * lines)],
    )
    from_low = shifted(high, "gx", 1)
    from_high = shifted(low, "gx", -1)
    outer = swapped(outer, "gz", 1)
    inner = swapped(inner, "gz", 0)
    (acc,) = run(
        flow_kernel, "flow", [whole, tables], [shape(*whole_shape)],
        [pltpu.VMEM((3, ny + 16, n), F32), pltpu.VMEM(whole_shape, F32), pltpu.VMEM(whole_shape, F32)],
        flops=10**9,
    )
    velocity_next, cross, low, high, inner, outer = run(
        step_kernel, "step", [whole, acc, from_low, from_high, inner, outer, tests, sent, tables],
        [
            shape(3, nx, half, n), shape(*tests_shape), shape(3, 3, ny, n), shape(3, 3, ny, n),
            shape(4, problems * 3 * lines), shape(4, problems * 3 * lines),
        ],
        [pltpu.VMEM(whole_shape, F32)] * 3, flops=10**9,
    )
    from_low = shifted(high, "gx", 1)
    from_high = shifted(low, "gx", -1)
    outer = swapped(outer, "gz", 1)
    inner = swapped(inner, "gz", 0)
    (part,) = run(
        curl_kernel, "curl", [part, cross, t_from_low, t_from_high, tables], [shape(*tests_shape)],
        [pltpu.VMEM((2, ny + 16, n), F32)], flops=10**9,
    )
    (test_next,) = run(
        finish_kernel, "finish",
        [part, t_from_low, t_from_high, from_low, from_high, inner, outer, tables],
        [shape(*tests_shape)],
        [
            pltpu.VMEM(tests_shape, F32), pltpu.VMEM((2, 3, ny, n), F32),
            pltpu.SemaphoreType.DMA((3 * problems,)),
        ],
        flops=10**9, out_specs=[pl.BlockSpec(memory_space=pl.ANY)],
    )
    return velocity_next, test_next


def solution(mesh):
    placed = (P(None, "gx", "sec", "gz"), P("sec", None, "gx", None, "gz"))
    return jax.shard_map(shards, mesh=mesh, in_specs=placed, out_specs=placed, check_vma=False)
```

time: 195 us -> 44 us (0.23); the launches traced: 192 us -> 43.8 us
  other arithmetic: 46.5 us -> 0 us
  waiting for transfers between devices: 49.7 us -> 8.35 us
  local copies, waits for them, and re-layouts: 40.6 us -> 2.56 us
  blocking collectives: 21.2 us -> 0 us
  Pallas kernels: 0 us -> 11.6 us
  matrix products: 7.9 us -> 0 us
  between operations: 3.91 us -> 0.7 us
  starting transfers between devices: 22.6 us -> 20.6 us
    ppermute x18 -> x11, waiting for transfers between devices: 49.7 us -> 8.35 us  [the longest x7 7.2 us: shifted(): lax.ppermute(block, axis, [(i, (i + distance) % count) for i in range(cou...]
    slice x18 -> x0, local copies, waits for them, and re-layouts: 27.3 us -> none  [the longest x9 14 us: shifted(): return jnp.roll(values, -offset, axis=axis_dim)]
    add x3 -> x0, other arithmetic: 23.3 us -> none  [the longest x1 16.7 us: shards(): test_next = test_fields + TIME_STEP * (curl + DIFFUSIVITY * laplace_test)]
    all_gather x2 -> x0, blocking collectives: 21.2 us -> none  [the longest x1 11.1 us: shards(): lax.all_gather(velocity, 'sec', axis=2, tiled=True)]
    pallas_call x0 -> x8, Pallas kernels: none -> 11.6 us  [run(): pl.pallas_call(body, in_specs=[vmem] * len(args), out_specs=[vmem] * len(...]
    concatenate x4 -> x0, other arithmetic: 11 us -> none  [with_halo(): jnp.concatenate([lax.ppermute(tail, axis, [(i, (i + 1) % count) for i in...]
    dot_general x2 -> x0, matrix products: 7.9 us -> none  [compact_dz(): solved = jnp.dot(source, green.T, precision=lax.Precision.HIGHEST)]
    ppermute x4 -> x0, local copies, waits for them, and re-layouts: 6.33 us -> none  [the longest x2 3.21 us: with_halo(): lax.ppermute(head, axis, [((i + 1) % count, i) for i in range(count)])]
  transfers between devices with their start and end apart: 18 -> 11, of which waited for: 8 -> 4; matrix products, arithmetic and copies ran while one was open for 37% -> 0% of each run, Pallas kernels for 0% -> 23%
where the time goes in v2:
time: 44 us; the launch traced here: 43.8 us
  starting transfers between devices  20.6 us (47%)
  Pallas kernels  11.6 us (26%)
  waiting for transfers between devices  8.35 us (19%)
  local copies, waits for them, and re-layouts  2.56 us (6%)
  between operations  0.7 us (2%)
    ppermute x7, starting transfers between devices, shifted(): lax.ppermute(block, axis, [(i, (i + distance) % count) for i in range(cou...  15 us
    pallas_call x8, Pallas kernels, run(): pl.pallas_call(body, in_specs=[vmem] * len(args), out_specs=[vmem] * len(...  11.6 us
    ppermute x7, waiting for transfers between devices, shifted(): lax.ppermute(block, axis, [(i, (i + distance) % count) for i in range(cou...  7.2 us
    ppermute x4, starting transfers between devices, swapped(): return lax.ppermute(block, axis, pairs + [(b, a) for a, b in pairs])  5.57 us
    unnamed x10, local copies, waits for them, and re-layouts  2.56 us
    ppermute x4, waiting for transfers between devices, swapped(): return lax.ppermute(block, axis, pairs + [(b, a) for a, b in pairs])  1.15 us
  transfers between devices with their start and end apart: 11, of which 4 were waited for; matrix products, arithmetic and copies ran while one was open for 0% of the time, Pallas kernels for 23%

profile of v2, /device:TPU:0, one launch (start us, length us, event | category | flops | bytes accessed | tf_op | source)
XLA Modules:
  0.0 43.8 jit_solution(12003935816081768724)
XLA Ops:
  0.6 3.4 %collective-permute-start = (f32[3,8,32,128]{3,2,1,0:T(8,128)}, f32[3,8,32,128]{3,2,1,0:T(8,128)S(1)}, u32[]{:S(2)}, u32[]{:S(2)}) collective-permute-start(f32[3,8,32,128]{3,2,1,0:T(8,128)} %refs_0_.2), channel_id=1, source_target_pairs={{0,64},{64,0},{1,65},{65,1},{2,66},{66,2},{3,67},{67,3},{4,68},{68... | collective-permute-start | bytes 1179656 | tf_op jit(solution)/shard_map/ppermute | solution.py:404
  4.0 1.4 %copy-done = f32[2,3,8,64,128]{4,3,2,1,0:T(8,128)S(1)} copy-done((f32[2,3,8,64,128]{4,3,2,1,0:T(8,128)S(1)}, f32[2,3,8,64,128]{4,3,2,1,0:T(8,128)}, u32[]{:S(2)}) %copy-start) | copy-done | bytes 1572888
  5.4 0.1 faces.1
  5.5 0.0 copy-start.1
  5.5 2.0 %collective-permute-start.5 = (f32[2,3,3,64,128]{4,3,2,1,0:T(8,128)S(1)}, f32[2,3,3,64,128]{4,3,2,1,0:T(8,128)S(1)}, u32[]{:S(2)}, u32[]{:S(2)}) collective-permute-start(f32[2,3,3,64,128]{4,3,2,1,0:T(8,128)S(1)} %get-tuple-element.26), channel_id=1, source_target_pairs={{0,1},{1,2},{2,3},{3,0},{4,5},{5,6},{6,7},{7,4},{8,9},{9,10},{10,1... | collective-permute-start | bytes 1769480 | tf_op jit(solution)/shard_map/ppermute | solution.py:404
  7.5 2.2 %collective-permute-start.6 = (f32[2,3,3,64,128]{4,3,2,1,0:T(8,128)S(1)}, f32[2,3,3,64,128]{4,3,2,1,0:T(8,128)S(1)}, u32[]{:S(2)}, u32[]{:S(2)}) collective-permute-start(f32[2,3,3,64,128]{4,3,2,1,0:T(8,128)S(1)} %get-tuple-element.27), channel_id=1, source_target_pairs={{0,3},{1,0},{2,1},{3,2},{4,7},{5,4},{6,5},{7,6},{8,11},{9,8},{10,9... | collective-permute-start | bytes 1769480 | tf_op jit(solution)/shard_map/ppermute | solution.py:404
  9.7 3.6 %collective-permute-done.refs_1_ = f32[3,8,32,128]{3,2,1,0:T(8,128)S(1)} collective-permute-done((f32[3,8,32,128]{3,2,1,0:T(8,128)}, f32[3,8,32,128]{3,2,1,0:T(8,128)S(1)}, u32[]{:S(2)}, u32[]{:S(2)}) %collective-permute-start) | collective-permute-done | bytes 393248 | tf_op jit(solution)/shard_map/ppermute | solution.py:404
  13.3 0.4 whole.1
  13.7 2.0 %collective-permute-start.1 = (f32[3,3,64,128]{3,2,1,0:T(8,128)S(1)}, f32[3,3,64,128]{3,2,1,0:T(8,128)S(1)}, u32[]{:S(2)}, u32[]{:S(2)}) collective-permute-start(f32[3,3,64,128]{3,2,1,0:T(8,128)S(1)} %get-tuple-element.18), channel_id=1, source_target_pairs={{0,1},{1,2},{2,3},{3,0},{4,5},{5,6},{6,7},{7,4},{8,9},{9,10},{10,1... | collective-permute-start | bytes 884744 | tf_op jit(solution)/shard_map/ppermute | solution.py:404
  15.8 2.2 %collective-permute-start.2 = (f32[3,3,64,128]{3,2,1,0:T(8,128)S(1)}, f32[3,3,64,128]{3,2,1,0:T(8,128)S(1)}, u32[]{:S(2)}, u32[]{:S(2)}) collective-permute-start(f32[3,3,64,128]{3,2,1,0:T(8,128)S(1)} %get-tuple-element.19), channel_id=1, source_target_pairs={{0,3},{1,0},{2,1},{3,2},{4,7},{5,4},{6,5},{7,6},{8,11},{9,8},{10,9... | collective-permute-start | bytes 884744 | tf_op jit(solution)/shard_map/ppermute | solution.py:404
  18.0 0.0 collective-permute-start.3
  18.0 1.8 %spread.1 = (f32[2,3,8,64,128]{4,3,2,1,0:T(8,128)S(1)}, f32[8,3072]{1,0:T(8,128)S(1)}) custom-call(f32[2,3,8,64,128]{4,3,2,1,0:T(8,128)S(1)} %copy-done.1, f32[1392,128]{1,0:T(8,128)S(1)} %tables.1.refs_2_.refs_1_.refs_8_.refs_4_.refs_7_), custom_call_target="tpu_custom_call" | custom-call | flops 1000000000 | bytes 3956736 | tf_op jit(solution)/shard_map/spread/pallas_call | solution.py:427
  19.8 0.0 collective-permute-done.3.refs_4_
  19.8 4.0 %collective-permute-start.4 = (f32[4,1536]{1,0:T(4,128)S(1)}, f32[4,1536]{1,0:T(4,128)S(1)}, u32[]{:S(2)}, u32[]{:S(2)}) collective-permute-start(f32[4,1536]{1,0:T(4,128)S(1)} %get-tuple-element.21), channel_id=1, source_target_pairs={{4,8},{12,16},{20,24},{28,32},{36,40},{44,48},{52,56},{60,0},{8,4}... | collective-permute-start | bytes 73736 | tf_op jit(solution)/shard_map/ppermute | solution.py:410
  23.8 1.8 %flow.1.refs_1_ = f32[3,8,64,128]{3,2,1,0:T(8,128)S(1)} custom-call(f32[3,8,64,128]{3,2,1,0:T(8,128)S(1)} %get-tuple-element.17.refs_0_, f32[1392,128]{1,0:T(8,128)S(1)} %tables.1.refs_2_.refs_1_.refs_8_.refs_4_.refs_7_), custom_call_target="tpu_custom_call" | custom-call | flops 1000000000 | bytes 2285568 | tf_op jit(solution)/shard_map/flow/pallas_call | solution.py:427
  25.6 0.0 collective-permute-done.4.refs_5_
  25.6 3.4 %collective-permute-done.1.refs_2_ = f32[3,3,64,128]{3,2,1,0:T(8,128)S(1)} collective-permute-done((f32[3,3,64,128]{3,2,1,0:T(8,128)S(1)}, f32[3,3,64,128]{3,2,1,0:T(8,128)S(1)}, u32[]{:S(2)}, u32[]{:S(2)}) %collective-permute-start.1) | collective-permute-done | bytes 294944 | tf_op jit(solution)/shard_map/ppermute | solution.py:404
  29.0 0.0 collective-permute-done.2.refs_3_
  29.0 3.1 %step.1 = (f32[3,8,32,128]{3,2,1,0:T(8,128)}, f32[2,3,8,64,128]{4,3,2,1,0:T(8,128)S(1)}, f32[3,3,64,128]{3,2,1,0:T(8,128)S(1)}, f32[3,3,64,128]{3,2,1,0:T(8,128)...) custom-call(f32[3,8,64,128]{3,2,1,0:T(8,128)S(1)} %get-tuple-element.17.refs_0_, f32[3,8,64,128]{3,2,1,0:T(8,128)S(1)} %flow.1.refs_1_, ...), custom_call_target="tpu_custom_call" | custom-call | flops 1000000000 | bytes 7249920 | tf_op jit(solution)/shard_map/step/pallas_call | solution.py:427
  32.0 1.1 %copy-done.2 = f32[2,3,8,64,128]{4,3,2,1,0:T(8,128)} copy-done((f32[2,3,8,64,128]{4,3,2,1,0:T(8,128)}, f32[2,3,8,64,128]{4,3,2,1,0:T(8,128)S(1)}, u32[]{:S(2)}) %copy-start.2) | copy-done | bytes 1572888
  33.2 1.3 %collective-permute-start.7 = (f32[3,3,64,128]{3,2,1,0:T(8,128)S(1)}, f32[3,3,64,128]{3,2,1,0:T(8,128)S(1)}, u32[]{:S(2)}, u32[]{:S(2)}) collective-permute-start(f32[3,3,64,128]{3,2,1,0:T(8,128)S(1)} %get-tuple-element.28), channel_id=1, source_target_pairs={{0,1},{1,2},{2,3},{3,0},{4,5},{5,6},{6,7},{7,4},{8,9},{9,10},{10,1... | collective-permute-start | bytes 884744 | tf_op jit(solution)/shard_map/ppermute | solution.py:404
  34.4 2.0 %collective-permute-start.8 = (f32[3,3,64,128]{3,2,1,0:T(8,128)S(1)}, f32[3,3,64,128]{3,2,1,0:T(8,128)S(1)}, u32[]{:S(2)}, u32[]{:S(2)}) collective-permute-start(f32[3,3,64,128]{3,2,1,0:T(8,128)S(1)} %get-tuple-element.29), channel_id=1, source_target_pairs={{0,3},{1,0},{2,1},{3,2},{4,7},{5,4},{6,5},{7,6},{8,11},{9,8},{10,9... | collective-permute-start | bytes 884744 | tf_op jit(solution)/shard_map/ppermute | solution.py:404
  36.4 0.9 %collective-permute-start.10 = (f32[4,3072]{1,0:T(4,128)S(1)}, f32[4,3072]{1,0:T(4,128)S(1)}, u32[]{:S(2)}, u32[]{:S(2)}) collective-permute-start(f32[4,3072]{1,0:T(4,128)S(1)} %get-tuple-element.31), channel_id=1, source_target_pairs={{4,8},{12,16},{20,24},{28,32},{36,40},{44,48},{52,56},{60,0},{8,4}... | collective-permute-start | bytes 147464 | tf_op jit(solution)/shard_map/ppermute | solution.py:410
  37.3 0.0 collective-permute-done.5.refs_2_.refs_1_
  37.3 0.7 %collective-permute-start.9 = (f32[4,3072]{1,0:T(4,128)S(1)}, f32[4,3072]{1,0:T(4,128)S(1)}, u32[]{:S(2)}, u32[]{:S(2)}) collective-permute-start(f32[4,3072]{1,0:T(4,128)S(1)} %get-tuple-element.30), channel_id=1, source_target_pairs={{0,4},{8,12},{16,20},{24,28},{32,36},{40,44},{48,52},{56,60},{4,0}... | collective-permute-start | bytes 147464 | tf_op jit(solution)/shard_map/ppermute | solution.py:410
  38.0 0.0 collective-permute-done.6.refs_3_.refs_2_
  38.0 2.9 %curl.1.refs_0_ = f32[2,3,8,64,128]{4,3,2,1,0:T(8,128)S(1)} custom-call(f32[2,3,8,64,128]{4,3,2,1,0:T(8,128)S(1)} %get-tuple-element.24.refs_0_, f32[2,3,8,64,128]{4,3,2,1,0:T(8,128)} %copy-done.2, f32[2,3,3,64,128]{4,3,2,1,0:T(8,128)S(1)} %collective-permute-done.5.refs_2_.refs_1_, f32[2,3,3,64,128]{4,3,2,1,0:T(8,128)S(1)} %collective-permute-done.6.refs_3_.refs_2_, ...), custom_call_target="tpu_custom_call" | custom-call | flops 1000000000 | bytes 6610944 | tf_op jit(solution)/shard_map/curl/pallas_call | solution.py:427
  40.9 1.1 %collective-permute-done.10.refs_6_ = f32[4,3072]{1,0:T(4,128)S(1)} collective-permute-done((f32[4,3072]{1,0:T(4,128)S(1)}, f32[4,3072]{1,0:T(4,128)S(1)}, u32[]{:S(2)}, u32[]{:S(2)}) %collective-permute-start.10) | collective-permute-done | bytes 49184 | tf_op jit(solution)/shard_map/ppermute | solution.py:410
  42.0 0.0 collective-permute-done.9.refs_5_
  42.0 0.2 collective-permute-done.7.refs_3_
  42.3 0.0 collective-permute-done.8.refs_4_
  42.3 1.6 %finish.1 = f32[2,3,8,64,128]{4,3,2,1,0:T(8,128)} custom-call(f32[2,3,8,64,128]{4,3,2,1,0:T(8,128)S(1)} %curl.1.refs_0_, f32[2,3,3,64,128]{4,3,2,1,0:T(8,128)S(1)} %collective-permute-done.5.refs_2_.refs_1_, f32[2,3,3,64,128]{4,3,2,1,0:T(8,128)S(1)} %collective-permute-done.6.refs_3_.refs_2_, f32[3,3,64,128]{3,2,1,0:T(8,128)S(1)} %collective-permute-done.7.refs_3_, ...), custom_call_target="tpu_custom_call" | custom-call | flops 1000000000 | bytes 5726208 | tf_op jit(solution)/shard_map/finish/pallas_call | solution.py:427
  (8 shorter events, 0.1 us)
Async XLA Ops:
  0.6 12.7 %collective-permute-start = (f32[3,8,32,128]{3,2,1,0:T(8,128)}, f32[3,8,32,128]{3,2,1,0:T(8,128)S(1)}, u32[]{:S(2)}, u32[]{:S(2)}) collective-permute-start(f32[3,8,32,128]{3,2,1,0:T(8,128)} %refs_0_.2), channel_id=1, source_target_pairs={{0,64},{64,0},{1,65},{65,1},{2,66},{66,2},{3,67},{67,3},{4,68},{68... | collective-permute-start | bytes 1179656 | tf_op jit(solution)/shard_map/ppermute | solution.py:404
  4.0 1.4 %copy-start = (f32[2,3,8,64,128]{4,3,2,1,0:T(8,128)S(1)}, f32[2,3,8,64,128]{4,3,2,1,0:T(8,128)}, u32[]{:S(2)}) copy-start(f32[2,3,8,64,128]{4,3,2,1,0:T(8,128)} %tests_ref.1) | copy-start | bytes 4718596
  5.4 4.3 %copy-start.3 = (f32[1392,128]{1,0:T(8,128)S(1)}, f32[1392,128]{1,0:T(8,128)}, u32[]{:S(2)}) copy-start(f32[1392,128]{1,0:T(8,128)} %constant.2.clone.source) | copy-start | bytes 2138116
  5.4 7.9 %copy-start.4 = (f32[3,8,32,128]{3,2,1,0:T(8,128)S(1)}, f32[3,8,32,128]{3,2,1,0:T(8,128)}, u32[]{:S(2)}) copy-start(f32[3,8,32,128]{3,2,1,0:T(8,128)} %refs_0_.2) | copy-start | bytes 1179652
  5.5 12.5 %copy-start.1 = (f32[2,3,8,64,128]{4,3,2,1,0:T(8,128)S(1)}, f32[2,3,8,64,128]{4,3,2,1,0:T(8,128)}, u32[]{:S(2)}) copy-start(f32[2,3,8,64,128]{4,3,2,1,0:T(8,128)} %tests_ref.1) | copy-start | bytes 4718596
  5.5 31.8 %collective-permute-start.5 = (f32[2,3,3,64,128]{4,3,2,1,0:T(8,128)S(1)}, f32[2,3,3,64,128]{4,3,2,1,0:T(8,128)S(1)}, u32[]{:S(2)}, u32[]{:S(2)}) collective-permute-start(f32[2,3,3,64,128]{4,3,2,1,0:T(8,128)S(1)} %get-tuple-element.26), channel_id=1, source_target_pairs={{0,1},{1,2},{2,3},{3,0},{4,5},{5,6},{6,7},{7,4},{8,9},{9,10},{10,1... | collective-permute-start | bytes 1769480 | tf_op jit(solution)/shard_map/ppermute | solution.py:404
  7.5 30.5 %collective-permute-start.6 = (f32[2,3,3,64,128]{4,3,2,1,0:T(8,128)S(1)}, f32[2,3,3,64,128]{4,3,2,1,0:T(8,128)S(1)}, u32[]{:S(2)}, u32[]{:S(2)}) collective-permute-start(f32[2,3,3,64,128]{4,3,2,1,0:T(8,128)S(1)} %get-tuple-element.27), channel_id=1, source_target_pairs={{0,3},{1,0},{2,1},{3,2},{4,7},{5,4},{6,5},{7,6},{8,11},{9,8},{10,9... | collective-permute-start | bytes 1769480 | tf_op jit(solution)/shard_map/ppermute | solution.py:404
  13.7 15.2 %collective-permute-start.1 = (f32[3,3,64,128]{3,2,1,0:T(8,128)S(1)}, f32[3,3,64,128]{3,2,1,0:T(8,128)S(1)}, u32[]{:S(2)}, u32[]{:S(2)}) collective-permute-start(f32[3,3,64,128]{3,2,1,0:T(8,128)S(1)} %get-tuple-element.18), channel_id=1, source_target_pairs={{0,1},{1,2},{2,3},{3,0},{4,5},{5,6},{6,7},{7,4},{8,9},{9,10},{10,1... | collective-permute-start | bytes 884744 | tf_op jit(solution)/shard_map/ppermute | solution.py:404
  15.8 13.2 %collective-permute-start.2 = (f32[3,3,64,128]{3,2,1,0:T(8,128)S(1)}, f32[3,3,64,128]{3,2,1,0:T(8,128)S(1)}, u32[]{:S(2)}, u32[]{:S(2)}) collective-permute-start(f32[3,3,64,128]{3,2,1,0:T(8,128)S(1)} %get-tuple-element.19), channel_id=1, source_target_pairs={{0,3},{1,0},{2,1},{3,2},{4,7},{5,4},{6,5},{7,6},{8,11},{9,8},{10,9... | collective-permute-start | bytes 884744 | tf_op jit(solution)/shard_map/ppermute | solution.py:404
  18.0 1.8 %collective-permute-start.3 = (f32[4,1536]{1,0:T(4,128)S(1)}, f32[4,1536]{1,0:T(4,128)S(1)}, u32[]{:S(2)}, u32[]{:S(2)}) collective-permute-start(f32[4,1536]{1,0:T(4,128)S(1)} %get-tuple-element.20), channel_id=1, source_target_pairs={{0,4},{8,12},{16,20},{24,28},{32,36},{40,44},{48,52},{56,60},{4,0}... | collective-permute-start | bytes 73736 | tf_op jit(solution)/shard_map/ppermute | solution.py:410
  19.8 5.8 %collective-permute-start.4 = (f32[4,1536]{1,0:T(4,128)S(1)}, f32[4,1536]{1,0:T(4,128)S(1)}, u32[]{:S(2)}, u32[]{:S(2)}) collective-permute-start(f32[4,1536]{1,0:T(4,128)S(1)} %get-tuple-element.21), channel_id=1, source_target_pairs={{4,8},{12,16},{20,24},{28,32},{36,40},{44,48},{52,56},{60,0},{8,4}... | collective-permute-start | bytes 73736 | tf_op jit(solution)/shard_map/ppermute | solution.py:410
  32.0 1.1 %copy-start.2 = (f32[2,3,8,64,128]{4,3,2,1,0:T(8,128)}, f32[2,3,8,64,128]{4,3,2,1,0:T(8,128)S(1)}, u32[]{:S(2)}) copy-start(f32[2,3,8,64,128]{4,3,2,1,0:T(8,128)S(1)} %get-tuple-element.25.refs_1_) | copy-start | bytes 4718596
  33.2 9.1 %collective-permute-start.7 = (f32[3,3,64,128]{3,2,1,0:T(8,128)S(1)}, f32[3,3,64,128]{3,2,1,0:T(8,128)S(1)}, u32[]{:S(2)}, u32[]{:S(2)}) collective-permute-start(f32[3,3,64,128]{3,2,1,0:T(8,128)S(1)} %get-tuple-element.28), channel_id=1, source_target_pairs={{0,1},{1,2},{2,3},{3,0},{4,5},{5,6},{6,7},{7,4},{8,9},{9,10},{10,1... | collective-permute-start | bytes 884744 | tf_op jit(solution)/shard_map/ppermute | solution.py:404
  34.4 7.8 %collective-permute-start.8 = (f32[3,3,64,128]{3,2,1,0:T(8,128)S(1)}, f32[3,3,64,128]{3,2,1,0:T(8,128)S(1)}, u32[]{:S(2)}, u32[]{:S(2)}) collective-permute-start(f32[3,3,64,128]{3,2,1,0:T(8,128)S(1)} %get-tuple-element.29), channel_id=1, source_target_pairs={{0,3},{1,0},{2,1},{3,2},{4,7},{5,4},{6,5},{7,6},{8,11},{9,8},{10,9... | collective-permute-start | bytes 884744 | tf_op jit(solution)/shard_map/ppermute | solution.py:404
  36.4 5.6 %collective-permute-start.10 = (f32[4,3072]{1,0:T(4,128)S(1)}, f32[4,3072]{1,0:T(4,128)S(1)}, u32[]{:S(2)}, u32[]{:S(2)}) collective-permute-start(f32[4,3072]{1,0:T(4,128)S(1)} %get-tuple-element.31), channel_id=1, source_target_pairs={{4,8},{12,16},{20,24},{28,32},{36,40},{44,48},{52,56},{60,0},{8,4}... | collective-permute-start | bytes 147464 | tf_op jit(solution)/shard_map/ppermute | solution.py:410
  37.3 4.7 %collective-permute-start.9 = (f32[4,3072]{1,0:T(4,128)S(1)}, f32[4,3072]{1,0:T(4,128)S(1)}, u32[]{:S(2)}, u32[]{:S(2)}) collective-permute-start(f32[4,3072]{1,0:T(4,128)S(1)} %get-tuple-element.30), channel_id=1, source_target_pairs={{0,4},{8,12},{16,20},{24,28},{32,36},{40,44},{48,52},{56,60},{4,0}... | collective-permute-start | bytes 147464 | tf_op jit(solution)/shard_map/ppermute | solution.py:410

commit v3 on v2

--- a/solution.py
+++ b/solution.py
@@ -16,7 +16,7 @@
 MID = -490.0 / 180.0
 ROOT = math.sqrt(5.0 / 9.0)
 DECAY = -(1.0 - ROOT) / (2.0 / 3.0)
-VMEM_LIMIT = 48 * 1024 * 1024
+VMEM_LIMIT = 12 * 1024 * 1024
 F32 = jnp.float32
 BF16 = jnp.bfloat16
 
@@ -200,10 +200,23 @@
     out[...] = source[...]
 
 
-def faces_kernel(tests_ref, low_ref, high_ref):
-    nx = tests_ref.shape[2]
-    low_ref[...] = tests_ref[:, :, 0:3]
-    high_ref[...] = tests_ref[:, :, nx - 3 : nx]
+def early_rows(shape, half):
+    problems, _, _, ny, _ = shape
+    tests = {(p, h): (p * 3 + h) * ny for p in range(problems) for h in range(3)}
+    first = problems * 3 * ny
+    flow = {(c, h): first + (c * 3 + h) * half for c in range(3) for h in range(3)}
+    return tests, flow, first + 9 * half
+
+
+def faces_kernel(tests_ref, own_ref, low_ref, high_ref):
+    nx, ny = tests_ref.shape[2:4]
+    half = own_ref.shape[2]
+    tests, flow, _ = early_rows(tests_ref.shape, half)
+    for out, start in ((low_ref, 0), (high_ref, nx - 3)):
+        for (p, h), at in tests.items():
+            out[at : at + ny] = tests_ref[p, 0, start + h]
+        for (c, h), at in flow.items():
+            out[at : at + half] = own_ref[c, start + h]
 
 
 def spread_kernel(places, tests_ref, tables_ref, out_ref, sent_ref, pad):
@@ -237,8 +250,8 @@
     section = lax.axis_index("sec")
     whole_ref[:, :, pl.ds(pl.multiple_of(section * half, half), half)] = own_ref[...]
     whole_ref[:, :, pl.ds(pl.multiple_of((1 - section) * half, half), half)] = other_ref[...]
-    low_ref[...] = whole_ref[:, 0:3]
-    high_ref[...] = whole_ref[:, nx - 3 : nx]
+    low_ref[...] = other_ref[:, 0:3]
+    high_ref[...] = other_ref[:, nx - 3 : nx]
     pick = Tables(tables_ref, places).get("pick").astype(BF16)
     hand_out(lines_out(whole_ref[...].reshape(-1, n), pick), inner_ref, outer_ref)
 
@@ -276,17 +289,23 @@
 
 
 def step_kernel(
-    places, whole_ref, acc_ref, low_ref, high_ref, inner_in, outer_in, tests_ref, sent_ref, tables_ref,
-    next_ref, cross_ref, low_out, high_out, inner_out, outer_out, moved_ref, grad_z, lap_z,
+    places, whole_ref, acc_ref, low_early, high_early, low_other, high_other, inner_in, outer_in, tests_ref, sent_ref,
+    tables_ref, next_ref, cross_ref, low_out, high_out, inner_out, outer_out, moved_ref, grad_z, lap_z, low_ref, high_ref,
 ):
     _, nx, ny, n = whole_ref.shape
     half = ny // 2
     problems = tests_ref.shape[0]
+    section = lax.axis_index("sec")
+    mine = pl.ds(pl.multiple_of(section * half, half), half)
+    theirs = pl.ds(pl.multiple_of((1 - section) * half, half), half)
+    for face, early, other in ((low_ref, low_early, low_other), (high_ref, high_early, high_other)):
+        for (c, h), at in early_rows(tests_ref.shape, half)[1].items():
+            face[c, h, mine] = early[at : at + half]
+            face[c, h, theirs] = other[c, h]
     tables = Tables(tables_ref, places)
     raw = taken_in(inner_in, outer_in)
     grad_z[...] = lines_in(raw, tables.get("spread_first").astype(BF16)).reshape(grad_z.shape)
     lap_z[...] = lines_in(raw, tables.get("spread_second").astype(BF16)).reshape(lap_z.shape)
-    mine = pl.ds(pl.multiple_of(lax.axis_index("sec") * half, half), half)
     waves = [wave_parts(tables, p, places["wave"][1] // 2) for p in range(problems)]
     for i in range(nx):
         own = [whole_ref[c, i] for c in range(3)]
@@ -306,16 +325,23 @@
             moved_ref[c, i] = moved
             next_ref[c, i] = moved_ref[c, i, mine]
             centred.append(0.5 * (own[c] + moved))
-            if i < 3:
-                low_out[c, i] = centred[c]
-            if i >= nx - 3:
-                high_out[c, i - nx + 3] = centred[c]
         cx, cy, cz = centred
         for p in range(problems):
             tx, ty, tz = tests_ref[p, 0, i] + waves[p][0], tests_ref[p, 1, i] + waves[p][1], tests_ref[p, 2, i]
             cross_ref[p, 0, i] = cx * tz - cz * tx
             cross_ref[p, 1, i] = cy * tz - cz * ty
             cross_ref[p, 2, i] = cx * ty - cy * tx
+    for p in range(problems):
+        for out, sign in ((low_out, 1.0), (high_out, -1.0)):
+            for m in range(3):
+                second = third = 0.0
+                for d in range(m + 1, 4):
+                    j = d - 1 - m if sign > 0 else nx + m - d
+                    slope, bend = sign * STEP * FIRST[d - 1], STEP * DIFF * SECOND[d - 1]
+                    second = second + (bend * tests_ref[p, 1, j] - slope * cross_ref[p, 2, j])
+                    third = third + (bend * tests_ref[p, 2, j] - slope * cross_ref[p, 0, j])
+                out[p, 0, m] = second
+                out[p, 1, m] = third
     lay = tables.get("lay_cross").astype(BF16)
     lines = nx * ny
     even = in_chip()
@@ -334,6 +360,7 @@
     problems, _, nx, ny, n = part_ref.shape
     tables = Tables(tables_ref, places)
     high, low = tables.pair("test_first")
+    early = early_rows(part_ref.shape, ny // 2)[0]
     for p in range(problems):
         for c in range(2):
             total = three(cross_ref[p, c].reshape(-1, n), high, low)
@@ -352,47 +379,26 @@
                         value[2] = value[2] - sign * cross_ref[p, 0, j]
                     else:
                         face, h = (low_ref, j + 3) if j < 0 else (high_ref, j - nx)
-                        for c in range(3):
-                            value[c] = value[c] + (STEP * DIFF * second) * face[p, c, h]
+                        at = early[p, h]
+                        value[0] = value[0] + (STEP * DIFF * second) * face[at : at + ny]
             for c in range(3):
                 out_ref[p, c, i] = value[c]
 
 
-def finish_kernel(
-    places, part_ref, t_low_ref, t_high_ref, c_low_ref, c_high_ref, inner_in, outer_in, tables_ref,
-    out_ref, held, cross, sems,
-):
+def finish_kernel(places, part_ref, low_ref, high_ref, inner_in, outer_in, tables_ref, out_ref, held, sems):
     problems, _, nx, ny, n = part_ref.shape
-    tables = Tables(tables_ref, places)
-    land = tables.get("land").astype(BF16)
+    land = Tables(tables_ref, places).get("land").astype(BF16)
     raw = taken_in(inner_in, outer_in)
     lines = nx * ny
     copies = []
     for p in range(problems):
-        wave_x, wave_y = wave_parts(tables, p, places["wave"][1] // 2)
         for c in range(3):
             at = (3 * p + c) * lines
             held[p, c] = part_ref[p, c] + lines_in(raw[:, at : at + lines], land).reshape(nx, ny, n)
-            if c == 0:
-                copies.append(pltpu.make_async_copy(held.at[p, c], out_ref.at[p, c], sems.at[3 * p + c]))
-                copies[-1].start()
-        for side, (t_ref, c_ref) in enumerate(((t_low_ref, c_low_ref), (t_high_ref, c_high_ref))):
-            for h in range(3):
-                cx, cy, cz = c_ref[0, h], c_ref[1, h], c_ref[2, h]
-                tx, ty, tz = t_ref[p, 0, h] + wave_x, t_ref[p, 1, h] + wave_y, t_ref[p, 2, h]
-                cross[0, h] = cz * tx - cx * tz
-                cross[1, h] = cx * ty - cy * tx
-            sign = -STEP if side == 0 else STEP
-            for m in range(3):
-                i = m if side == 0 else nx - 1 - m
-                second, third = held[p, 1, i], held[p, 2, i]
-                for d in range(m + 1, 4):
-                    h = 3 + m - d if side == 0 else d - 1 - m
-                    second = second - (sign * FIRST[d - 1]) * cross[1, h]
-                    third = third + (sign * FIRST[d - 1]) * cross[0, h]
-                held[p, 1, i] = second
-                held[p, 2, i] = third
-        for c in (1, 2):
+            if c > 0:
+                held[p, c, 0:3] += low_ref[p, c - 1]
+                for m in range(3):
+                    held[p, c, nx - 1 - m] += high_ref[p, c - 1, m]
             copies.append(pltpu.make_async_copy(held.at[p, c], out_ref.at[p, c], sems.at[3 * p + c]))
             copies[-1].start()
     for copy in copies:
@@ -439,9 +445,9 @@
     tests_shape = (problems, 3, nx, ny, n)
     other = shifted(velocity, "sec", 1)
     (tables,) = run(tables_kernel, "tables", [jnp.asarray(constants)], [shape(*constants.shape)], bind=False)
-    t_low, t_high = run(faces_kernel, "faces", [tests], [shape(problems, 3, 3, ny, n)] * 2, bind=False)
-    t_from_low = shifted(t_high, "gx", 1)
-    t_from_high = shifted(t_low, "gx", -1)
+    rows = early_rows(tests_shape, half)[2]
+    low, high = run(faces_kernel, "faces", [tests, velocity], [shape(rows, n)] * 2, bind=False)
+    early = [shifted(high, "gx", 1), shifted(low, "gx", -1)]
     part, sent = run(
         spread_kernel, "spread", [tests, tables],
         [shape(*tests_shape), shape(8, problems * 3 * lines)],
@@ -449,7 +455,7 @@
     )
     whole, low, high, inner, outer = run(
         whole_kernel, "whole", [velocity, other, tables],
-        [shape(*whole_shape), shape(3, 3, ny, n), shape(3, 3, ny, n), shape(4, 3 * lines), shape(4, 3 * lines)],
+        [shape(*whole_shape)] + [shape(3, 3, half, n)] * 2 + [shape(4, 3 * lines)] * 2,
     )
     from_low = shifted(high, "gx", 1)
     from_high = shifted(low, "gx", -1)
@@ -461,29 +467,26 @@
         flops=10**9,
     )
     velocity_next, cross, low, high, inner, outer = run(
-        step_kernel, "step", [whole, acc, from_low, from_high, inner, outer, tests, sent, tables],
+        step_kernel, "step", [whole, acc, *early, from_low, from_high, inner, outer, tests, sent, tables],
         [
-            shape(3, nx, half, n), shape(*tests_shape), shape(3, 3, ny, n), shape(3, 3, ny, n),
+            shape(3, nx, half, n), shape(*tests_shape), shape(problems, 2, 3, ny, n), shape(problems, 2, 3, ny, n),
             shape(4, problems * 3 * lines), shape(4, problems * 3 * lines),
         ],
-        [pltpu.VMEM(whole_shape, F32)] * 3, flops=10**9,
+        [pltpu.VMEM(whole_shape, F32)] * 3 + [pltpu.VMEM((3, 3, ny, n), F32)] * 2, flops=10**9,
     )
     from_low = shifted(high, "gx", 1)
     from_high = shifted(low, "gx", -1)
     outer = swapped(outer, "gz", 1)
     inner = swapped(inner, "gz", 0)
     (part,) = run(
-        curl_kernel, "curl", [part, cross, t_from_low, t_from_high, tables], [shape(*tests_shape)],
+        curl_kernel, "curl", [part, cross, *early, tables], [shape(*tests_shape)],
         [pltpu.VMEM((2, ny + 16, n), F32)], flops=10**9,
     )
     (test_next,) = run(
         finish_kernel, "finish",
-        [part, t_from_low, t_from_high, from_low, from_high, inner, outer, tables],
+        [part, from_low, from_high, inner, outer, tables],
         [shape(*tests_shape)],
-        [
-            pltpu.VMEM(tests_shape, F32), pltpu.VMEM((2, 3, ny, n), F32),
-            pltpu.SemaphoreType.DMA((3 * problems,)),
-        ],
+        [pltpu.VMEM(tests_shape, F32), pltpu.SemaphoreType.DMA((3 * problems,))],
         flops=10**9, out_specs=[pl.BlockSpec(memory_space=pl.ANY)],
     )
     return velocity_next, test_next

time: 44 us -> 40 us (0.909); the launches traced: 43.8 us -> 39.3 us
  waiting for transfers between devices: 8.35 us -> 5.25 us
  Pallas kernels: 11.6 us -> 8.97 us
  starting transfers between devices: 20.6 us -> 21.9 us
    ppermute x7, waiting for transfers between devices: 7.2 us -> 4.04 us  [shifted(): lax.ppermute(block, axis, [(i, (i + distance) % count) for i in range(cou...]
    pallas_call x8, Pallas kernels: 11.6 us -> 8.97 us  [run(): pl.pallas_call(body, in_specs=[vmem] * len(args), out_specs=[vmem] * len(...]
    ppermute x4, starting transfers between devices: 5.57 us -> 6.91 us  [swapped(): return lax.ppermute(block, axis, pairs + [(b, a) for a, b in pairs])]
  transfers between devices with their start and end apart: 11 -> 11, of which waited for: 4 -> 3; matrix products, arithmetic and copies ran while one was open for 0% -> 0% of each run, Pallas kernels for 23% -> 14%
where the time goes in v3:
time: 40 us; the launch traced here: 39.3 us
  starting transfers between devices  21.9 us (55%)
  Pallas kernels  8.97 us (22%)
  waiting for transfers between devices  5.25 us (13%)
  local copies, waits for them, and re-layouts  2.42 us (6%)
  between operations  0.74 us (2%)
    ppermute x7, starting transfers between devices, shifted(): lax.ppermute(block, axis, [(i, (i + distance) % count) for i in range(cou...  15 us
    pallas_call x8, Pallas kernels, run(): pl.pallas_call(body, in_specs=[vmem] * len(args), out_specs=[vmem] * len(...  8.97 us
    ppermute x4, starting transfers between devices, swapped(): return lax.ppermute(block, axis, pairs + [(b, a) for a, b in pairs])  6.91 us
    ppermute x7, waiting for transfers between devices, shifted(): lax.ppermute(block, axis, [(i, (i + distance) % count) for i in range(cou...  4.04 us
    unnamed x10, local copies, waits for them, and re-layouts  2.42 us
    ppermute x4, waiting for transfers between devices, swapped(): return lax.ppermute(block, axis, pairs + [(b, a) for a, b in pairs])  1.22 us
  transfers between devices with their start and end apart: 11, of which 3 were waited for; matrix products, arithmetic and copies ran while one was open for 0% of the time, Pallas kernels for 14%

profile of v3, /device:TPU:0, one launch (start us, length us, event | category | flops | bytes accessed | tf_op | source)
XLA Modules:
  0.0 39.3 jit_solution(8254711783974068791)
XLA Ops:
  0.6 3.4 %collective-permute-start = (f32[3,8,32,128]{3,2,1,0:T(8,128)}, f32[3,8,32,128]{3,2,1,0:T(8,128)S(1)}, u32[]{:S(2)}, u32[]{:S(2)}) collective-permute-start(f32[3,8,32,128]{3,2,1,0:T(8,128)} %own_ref.1), channel_id=1, source_target_pairs={{0,64},{64,0},{1,65},{65,1},{2,66},{66,2},{3,67},{67,3},{4,68},{68... | collective-permute-start | bytes 1179656 | tf_op jit(solution)/shard_map/ppermute | solution.py:410
  4.0 1.4 %copy-done = f32[2,3,8,64,128]{4,3,2,1,0:T(8,128)S(1)} copy-done((f32[2,3,8,64,128]{4,3,2,1,0:T(8,128)S(1)}, f32[2,3,8,64,128]{4,3,2,1,0:T(8,128)}, u32[]{:S(2)}) %copy-start) | copy-done | bytes 1572888
  5.4 1.0 %copy-done.2 = f32[3,8,32,128]{3,2,1,0:T(8,128)S(1)} copy-done((f32[3,8,32,128]{3,2,1,0:T(8,128)S(1)}, f32[3,8,32,128]{3,2,1,0:T(8,128)}, u32[]{:S(2)}) %copy-start.2) | copy-done | bytes 393240
  6.4 0.0 copy-start.1
  6.5 2.0 %collective-permute-start.1 = (f32[672,128]{1,0:T(8,128)S(1)}, f32[672,128]{1,0:T(8,128)S(1)}, u32[]{:S(2)}, u32[]{:S(2)}) collective-permute-start(f32[672,128]{1,0:T(8,128)S(1)} %get-tuple-element.18), channel_id=1, source_target_pairs={{0,1},{1,2},{2,3},{3,0},{4,5},{5,6},{6,7},{7,4},{8,9},{9,10},{10,1... | collective-permute-start | bytes 1032200 | tf_op jit(solution)/shard_map/ppermute | solution.py:410
  8.4 2.2 %collective-permute-start.2 = (f32[672,128]{1,0:T(8,128)S(1)}, f32[672,128]{1,0:T(8,128)S(1)}, u32[]{:S(2)}, u32[]{:S(2)}) collective-permute-start(f32[672,128]{1,0:T(8,128)S(1)} %get-tuple-element.19), channel_id=1, source_target_pairs={{0,3},{1,0},{2,1},{3,2},{4,7},{5,4},{6,5},{7,6},{8,11},{9,8},{10,9... | collective-permute-start | bytes 1032200 | tf_op jit(solution)/shard_map/ppermute | solution.py:410
  10.6 0.0 copy-done.4
  10.7 2.6 %collective-permute-done.refs_1_ = f32[3,8,32,128]{3,2,1,0:T(8,128)S(1)} collective-permute-done((f32[3,8,32,128]{3,2,1,0:T(8,128)}, f32[3,8,32,128]{3,2,1,0:T(8,128)S(1)}, u32[]{:S(2)}, u32[]{:S(2)}) %collective-permute-start) | collective-permute-done | bytes 393248 | tf_op jit(solution)/shard_map/ppermute | solution.py:410
  13.3 0.4 %whole.1 = (f32[3,8,64,128]{3,2,1,0:T(8,128)S(1)}, f32[3,3,32,128]{3,2,1,0:T(8,128)S(1)}, f32[3,3,32,128]{3,2,1,0:T(8,128)S(1)}, f32[4,1536]{1,0:T(4,128)S(1)}, f32[4,1536]{1,0:T(4,128)S(1)}) custom-call(f32[3,8,32,128]{3,2,1,0:T(8,128)S(1)} %copy-done.3, f32[3,8,32,128]{3,2,1,0:T(8,128)S(1)} %collective-permute-done.refs_1_, ...), custom_call_target="tpu_custom_call" | custom-call | flops 100000000 | bytes 2629632 | tf_op jit(solution)/shard_map/whole/pallas_call | solution.py:433
  13.7 2.0 %collective-permute-start.3 = (f32[3,3,32,128]{3,2,1,0:T(8,128)S(1)}, f32[3,3,32,128]{3,2,1,0:T(8,128)S(1)}, u32[]{:S(2)}, u32[]{:S(2)}) collective-permute-start(f32[3,3,32,128]{3,2,1,0:T(8,128)S(1)} %get-tuple-element.20), channel_id=1, source_target_pairs={{0,1},{1,2},{2,3},{3,0},{4,5},{5,6},{6,7},{7,4},{8,9},{9,10},{10,1... | collective-permute-start | bytes 442376 | tf_op jit(solution)/shard_map/ppermute | solution.py:410
  15.8 2.2 %collective-permute-start.4 = (f32[3,3,32,128]{3,2,1,0:T(8,128)S(1)}, f32[3,3,32,128]{3,2,1,0:T(8,128)S(1)}, u32[]{:S(2)}, u32[]{:S(2)}) collective-permute-start(f32[3,3,32,128]{3,2,1,0:T(8,128)S(1)} %get-tuple-element.21), channel_id=1, source_target_pairs={{0,3},{1,0},{2,1},{3,2},{4,7},{5,4},{6,5},{7,6},{8,11},{9,8},{10,9... | collective-permute-start | bytes 442376 | tf_op jit(solution)/shard_map/ppermute | solution.py:410
  18.0 1.8 %spread.1 = (f32[2,3,8,64,128]{4,3,2,1,0:T(8,128)S(1)}, f32[8,3072]{1,0:T(8,128)S(1)}) custom-call(f32[2,3,8,64,128]{4,3,2,1,0:T(8,128)S(1)} %copy-done.1, f32[1392,128]{1,0:T(8,128)S(1)} %tables.1.refs_2_.refs_1_.refs_10_.refs_4_.refs_5_), custom_call_target="tpu_custom_call" | custom-call | flops 1000000000 | bytes 3956736 | tf_op jit(solution)/shard_map/spread/pallas_call | solution.py:433
  19.8 0.1 collective-permute-start.5
  19.9 0.0 collective-permute-done.1.refs_2_
  19.9 3.9 %collective-permute-start.6 = (f32[4,1536]{1,0:T(4,128)S(1)}, f32[4,1536]{1,0:T(4,128)S(1)}, u32[]{:S(2)}, u32[]{:S(2)}) collective-permute-start(f32[4,1536]{1,0:T(4,128)S(1)} %get-tuple-element.23), channel_id=1, source_target_pairs={{4,8},{12,16},{20,24},{28,32},{36,40},{44,48},{52,56},{60,0},{8,4}... | collective-permute-start | bytes 73736 | tf_op jit(solution)/shard_map/ppermute | solution.py:416
  23.8 1.8 %flow.1.refs_1_ = f32[3,8,64,128]{3,2,1,0:T(8,128)S(1)} custom-call(f32[3,8,64,128]{3,2,1,0:T(8,128)S(1)} %get-tuple-element.17.refs_0_, f32[1392,128]{1,0:T(8,128)S(1)} %tables.1.refs_2_.refs_1_.refs_10_.refs_4_.refs_5_), custom_call_target="tpu_custom_call" | custom-call | flops 1000000000 | bytes 2285568 | tf_op jit(solution)/shard_map/flow/pallas_call | solution.py:433
  25.6 0.0 collective-permute-done.2.refs_3_
  25.6 0.0 collective-permute-done.5.refs_6_
  25.6 0.0 collective-permute-done.6.refs_7_
  25.6 0.0 collective-permute-done.3.refs_4_
  25.6 0.0 collective-permute-done.4.refs_5_
  25.6 1.9 %step.1 = (f32[3,8,32,128]{3,2,1,0:T(8,128)}, f32[2,3,8,64,128]{4,3,2,1,0:T(8,128)S(1)}, f32[2,2,3,64,128]{4,3,2,1,0:T(8,128)S(1)}, f32[2,2,3,64,128]{4,3,2,1,0:...) custom-call(f32[3,8,64,128]{3,2,1,0:T(8,128)S(1)} %get-tuple-element.17.refs_0_, ...), custom_call_target="tpu_custom_call" | custom-call | flops 1000000000 | bytes 7839744 | tf_op jit(solution)/shard_map/step/pallas_call | solution.py:433
  27.5 0.0 collective-permute-start.7
  27.5 3.2 %collective-permute-start.8 = (f32[2,2,3,64,128]{4,3,2,1,0:T(8,128)S(1)}, f32[2,2,3,64,128]{4,3,2,1,0:T(8,128)S(1)}, u32[]{:S(2)}, u32[]{:S(2)}) collective-permute-start(f32[2,2,3,64,128]{4,3,2,1,0:T(8,128)S(1)} %get-tuple-element.29), channel_id=1, source_target_pairs={{0,3},{1,0},{2,1},{3,2},{4,7},{5,4},{6,5},{7,6},{8,11},{9,8},{10,9... | collective-permute-start | bytes 1179656 | tf_op jit(solution)/shard_map/ppermute | solution.py:410
  30.8 0.0 collective-permute-start.9
  30.8 3.0 %collective-permute-start.10 = (f32[4,3072]{1,0:T(4,128)S(1)}, f32[4,3072]{1,0:T(4,128)S(1)}, u32[]{:S(2)}, u32[]{:S(2)}) collective-permute-start(f32[4,3072]{1,0:T(4,128)S(1)} %get-tuple-element.31), channel_id=1, source_target_pairs={{4,8},{12,16},{20,24},{28,32},{36,40},{44,48},{52,56},{60,0},{8,4}... | collective-permute-start | bytes 147464 | tf_op jit(solution)/shard_map/ppermute | solution.py:416
  33.7 1.4 %curl.1.refs_0_ = f32[2,3,8,64,128]{4,3,2,1,0:T(8,128)S(1)} custom-call(f32[2,3,8,64,128]{4,3,2,1,0:T(8,128)S(1)} %get-tuple-element.26.refs_0_, f32[2,3,8,64,128]{4,3,2,1,0:T(8,128)S(1)} %get-tuple-element.27.refs_1_, f32[672,128]{1,0:T(8,128)S(1)} %collective-permute-done.1.refs_2_, f32[672,128]{1,0:T(8,128)S(1)} %collective-permute-done.2.refs_3_, ...), custom_call_target="tpu_custom_call" | custom-call | flops 1000000000 | bytes 6119424 | tf_op jit(solution)/shard_map/curl/pallas_call | solution.py:433
  35.2 0.0 collective-permute-done.9.refs_3_
  35.2 1.2 %collective-permute-done.10.refs_4_ = f32[4,3072]{1,0:T(4,128)S(1)} collective-permute-done((f32[4,3072]{1,0:T(4,128)S(1)}, f32[4,3072]{1,0:T(4,128)S(1)}, u32[]{:S(2)}, u32[]{:S(2)}) %collective-permute-start.10) | collective-permute-done | bytes 49184 | tf_op jit(solution)/shard_map/ppermute | solution.py:416
  36.4 1.4 %collective-permute-done.7.refs_1_ = f32[2,2,3,64,128]{4,3,2,1,0:T(8,128)S(1)} collective-permute-done((f32[2,2,3,64,128]{4,3,2,1,0:T(8,128)S(1)}, f32[2,2,3,64,128]{4,3,2,1,0:T(8,128)S(1)}, u32[]{:S(2)}, u32[]{:S(2)}) %collective-permute-start.7) | collective-permute-done | bytes 393248 | tf_op jit(solution)/shard_map/ppermute | solution.py:410
  37.8 0.0 collective-permute-done.8.refs_2_
  37.8 1.5 %finish.1 = f32[2,3,8,64,128]{4,3,2,1,0:T(8,128)} custom-call(f32[2,3,8,64,128]{4,3,2,1,0:T(8,128)S(1)} %curl.1.refs_0_, f32[2,2,3,64,128]{4,3,2,1,0:T(8,128)S(1)} %collective-permute-done.7.refs_1_, f32[2,2,3,64,128]{4,3,2,1,0:T(8,128)S(1)} %collective-permute-done.8.refs_2_, f32[4,3072]{1,0:T(4,128)S(1)} %collective-permute-done.9.refs_3_, ...), custom_call_target="tpu_custom_call" | custom-call | flops 1000000000 | bytes 4743168 | tf_op jit(solution)/shard_map/finish/pallas_call | solution.py:433
  (8 shorter events, 0.1 us)
Async XLA Ops:
  0.6 12.7 %collective-permute-start = (f32[3,8,32,128]{3,2,1,0:T(8,128)}, f32[3,8,32,128]{3,2,1,0:T(8,128)S(1)}, u32[]{:S(2)}, u32[]{:S(2)}) collective-permute-start(f32[3,8,32,128]{3,2,1,0:T(8,128)} %own_ref.1), channel_id=1, source_target_pairs={{0,64},{64,0},{1,65},{65,1},{2,66},{66,2},{3,67},{67,3},{4,68},{68... | collective-permute-start | bytes 1179656 | tf_op jit(solution)/shard_map/ppermute | solution.py:410
  4.0 1.4 %copy-start = (f32[2,3,8,64,128]{4,3,2,1,0:T(8,128)S(1)}, f32[2,3,8,64,128]{4,3,2,1,0:T(8,128)}, u32[]{:S(2)}) copy-start(f32[2,3,8,64,128]{4,3,2,1,0:T(8,128)} %refs_8_.1) | copy-start | bytes 4718596
  5.4 1.0 %copy-start.2 = (f32[3,8,32,128]{3,2,1,0:T(8,128)S(1)}, f32[3,8,32,128]{3,2,1,0:T(8,128)}, u32[]{:S(2)}) copy-start(f32[3,8,32,128]{3,2,1,0:T(8,128)} %own_ref.1) | copy-start | bytes 1179652
  6.4 4.3 %copy-start.4 = (f32[1392,128]{1,0:T(8,128)S(1)}, f32[1392,128]{1,0:T(8,128)}, u32[]{:S(2)}) copy-start(f32[1392,128]{1,0:T(8,128)} %constant.2.clone.source) | copy-start | bytes 2138116
  6.4 6.9 %copy-start.3 = (f32[3,8,32,128]{3,2,1,0:T(8,128)S(1)}, f32[3,8,32,128]{3,2,1,0:T(8,128)}, u32[]{:S(2)}) copy-start(f32[3,8,32,128]{3,2,1,0:T(8,128)} %own_ref.1) | copy-start | bytes 1179652
  6.4 11.5 %copy-start.1 = (f32[2,3,8,64,128]{4,3,2,1,0:T(8,128)S(1)}, f32[2,3,8,64,128]{4,3,2,1,0:T(8,128)}, u32[]{:S(2)}) copy-start(f32[2,3,8,64,128]{4,3,2,1,0:T(8,128)} %refs_8_.1) | copy-start | bytes 4718596
  6.5 13.4 %collective-permute-start.1 = (f32[672,128]{1,0:T(8,128)S(1)}, f32[672,128]{1,0:T(8,128)S(1)}, u32[]{:S(2)}, u32[]{:S(2)}) collective-permute-start(f32[672,128]{1,0:T(8,128)S(1)} %get-tuple-element.18), channel_id=1, source_target_pairs={{0,1},{1,2},{2,3},{3,0},{4,5},{5,6},{6,7},{7,4},{8,9},{9,10},{10,1... | collective-permute-start | bytes 1032200 | tf_op jit(solution)/shard_map/ppermute | solution.py:410
  8.4 17.1 %collective-permute-start.2 = (f32[672,128]{1,0:T(8,128)S(1)}, f32[672,128]{1,0:T(8,128)S(1)}, u32[]{:S(2)}, u32[]{:S(2)}) collective-permute-start(f32[672,128]{1,0:T(8,128)S(1)} %get-tuple-element.19), channel_id=1, source_target_pairs={{0,3},{1,0},{2,1},{3,2},{4,7},{5,4},{6,5},{7,6},{8,11},{9,8},{10,9... | collective-permute-start | bytes 1032200 | tf_op jit(solution)/shard_map/ppermute | solution.py:410
  13.7 11.9 %collective-permute-start.3 = (f32[3,3,32,128]{3,2,1,0:T(8,128)S(1)}, f32[3,3,32,128]{3,2,1,0:T(8,128)S(1)}, u32[]{:S(2)}, u32[]{:S(2)}) collective-permute-start(f32[3,3,32,128]{3,2,1,0:T(8,128)S(1)} %get-tuple-element.20), channel_id=1, source_target_pairs={{0,1},{1,2},{2,3},{3,0},{4,5},{5,6},{6,7},{7,4},{8,9},{9,10},{10,1... | collective-permute-start | bytes 442376 | tf_op jit(solution)/shard_map/ppermute | solution.py:410
  15.8 9.8 %collective-permute-start.4 = (f32[3,3,32,128]{3,2,1,0:T(8,128)S(1)}, f32[3,3,32,128]{3,2,1,0:T(8,128)S(1)}, u32[]{:S(2)}, u32[]{:S(2)}) collective-permute-start(f32[3,3,32,128]{3,2,1,0:T(8,128)S(1)} %get-tuple-element.21), channel_id=1, source_target_pairs={{0,3},{1,0},{2,1},{3,2},{4,7},{5,4},{6,5},{7,6},{8,11},{9,8},{10,9... | collective-permute-start | bytes 442376 | tf_op jit(solution)/shard_map/ppermute | solution.py:410
  19.8 5.8 %collective-permute-start.5 = (f32[4,1536]{1,0:T(4,128)S(1)}, f32[4,1536]{1,0:T(4,128)S(1)}, u32[]{:S(2)}, u32[]{:S(2)}) collective-permute-start(f32[4,1536]{1,0:T(4,128)S(1)} %get-tuple-element.22), channel_id=1, source_target_pairs={{0,4},{8,12},{16,20},{24,28},{32,36},{40,44},{48,52},{56,60},{4,0}... | collective-permute-start | bytes 73736 | tf_op jit(solution)/shard_map/ppermute | solution.py:416
  19.9 5.7 %collective-permute-start.6 = (f32[4,1536]{1,0:T(4,128)S(1)}, f32[4,1536]{1,0:T(4,128)S(1)}, u32[]{:S(2)}, u32[]{:S(2)}) collective-permute-start(f32[4,1536]{1,0:T(4,128)S(1)} %get-tuple-element.23), channel_id=1, source_target_pairs={{4,8},{12,16},{20,24},{28,32},{36,40},{44,48},{52,56},{60,0},{8,4}... | collective-permute-start | bytes 73736 | tf_op jit(solution)/shard_map/ppermute | solution.py:416
  27.5 10.3 %collective-permute-start.7 = (f32[2,2,3,64,128]{4,3,2,1,0:T(8,128)S(1)}, f32[2,2,3,64,128]{4,3,2,1,0:T(8,128)S(1)}, u32[]{:S(2)}, u32[]{:S(2)}) collective-permute-start(f32[2,2,3,64,128]{4,3,2,1,0:T(8,128)S(1)} %get-tuple-element.28), channel_id=1, source_target_pairs={{0,1},{1,2},{2,3},{3,0},{4,5},{5,6},{6,7},{7,4},{8,9},{9,10},{10,1... | collective-permute-start | bytes 1179656 | tf_op jit(solution)/shard_map/ppermute | solution.py:410
  27.5 10.3 %collective-permute-start.8 = (f32[2,2,3,64,128]{4,3,2,1,0:T(8,128)S(1)}, f32[2,2,3,64,128]{4,3,2,1,0:T(8,128)S(1)}, u32[]{:S(2)}, u32[]{:S(2)}) collective-permute-start(f32[2,2,3,64,128]{4,3,2,1,0:T(8,128)S(1)} %get-tuple-element.29), channel_id=1, source_target_pairs={{0,3},{1,0},{2,1},{3,2},{4,7},{5,4},{6,5},{7,6},{8,11},{9,8},{10,9... | collective-permute-start | bytes 1179656 | tf_op jit(solution)/shard_map/ppermute | solution.py:410
  30.8 4.4 %collective-permute-start.9 = (f32[4,3072]{1,0:T(4,128)S(1)}, f32[4,3072]{1,0:T(4,128)S(1)}, u32[]{:S(2)}, u32[]{:S(2)}) collective-permute-start(f32[4,3072]{1,0:T(4,128)S(1)} %get-tuple-element.30), channel_id=1, source_target_pairs={{0,4},{8,12},{16,20},{24,28},{32,36},{40,44},{48,52},{56,60},{4,0}... | collective-permute-start | bytes 147464 | tf_op jit(solution)/shard_map/ppermute | solution.py:416
  30.8 5.6 %collective-permute-start.10 = (f32[4,3072]{1,0:T(4,128)S(1)}, f32[4,3072]{1,0:T(4,128)S(1)}, u32[]{:S(2)}, u32[]{:S(2)}) collective-permute-start(f32[4,3072]{1,0:T(4,128)S(1)} %get-tuple-element.31), channel_id=1, source_target_pairs={{4,8},{12,16},{20,24},{28,32},{36,40},{44,48},{52,56},{60,0},{8,4}... | collective-permute-start | bytes 147464 | tf_op jit(solution)/shard_map/ppermute | solution.py:416

commit v4 on v3

--- a/solution.py
+++ b/solution.py
@@ -17,6 +17,7 @@
 ROOT = math.sqrt(5.0 / 9.0)
 DECAY = -(1.0 - ROOT) / (2.0 / 3.0)
 VMEM_LIMIT = 12 * 1024 * 1024
+FACES_LIMIT = 62 * 1024 * 1024 + 512 * 1024
 F32 = jnp.float32
 BF16 = jnp.bfloat16
 
@@ -208,15 +209,23 @@
     return tests, flow, first + 9 * half
 
 
-def faces_kernel(tests_ref, own_ref, low_ref, high_ref):
-    nx, ny = tests_ref.shape[2:4]
+def faces_kernel(tests_ref, own_ref, low_ref, high_ref, sems):
+    nx, ny, n = tests_ref.shape[2:5]
     half = own_ref.shape[2]
     tests, flow, _ = early_rows(tests_ref.shape, half)
+    problems = tests_ref.shape[0]
+    copies = []
     for out, start in ((low_ref, 0), (high_ref, nx - 3)):
-        for (p, h), at in tests.items():
-            out[at : at + ny] = tests_ref[p, 0, start + h]
-        for (c, h), at in flow.items():
-            out[at : at + half] = own_ref[c, start + h]
+        for p in range(problems):
+            at = tests[p, 0]
+            copies.append((tests_ref.at[p, 0, start : start + 3], out.at[at : at + 3 * ny].reshape(3, ny, n)))
+        at = flow[0, 0]
+        copies.append((own_ref.at[:, start : start + 3], out.at[at : at + 9 * half].reshape(3, 3, half, n)))
+    copies = [pltpu.make_async_copy(source, out, sems.at[k]) for k, (source, out) in enumerate(copies)]
+    for copy in copies:
+        copy.start()
+    for copy in copies:
+        copy.wait()
 
 
 def spread_kernel(places, tests_ref, tables_ref, out_ref, sent_ref, pad):
@@ -245,7 +254,7 @@
                 out_ref[p, c, i] = value
 
 
-def whole_kernel(places, own_ref, other_ref, tables_ref, whole_ref, low_ref, high_ref, inner_ref, outer_ref):
+def whole_kernel(places, own_ref, other_ref, tables_ref, _, whole_ref, low_ref, high_ref, inner_ref, outer_ref):
     _, nx, half, n = own_ref.shape
     section = lax.axis_index("sec")
     whole_ref[:, :, pl.ds(pl.multiple_of(section * half, half), half)] = own_ref[...]
@@ -289,8 +298,8 @@
 
 
 def step_kernel(
-    places, whole_ref, acc_ref, low_early, high_early, low_other, high_other, inner_in, outer_in, tests_ref, sent_ref,
-    tables_ref, next_ref, cross_ref, low_out, high_out, inner_out, outer_out, moved_ref, grad_z, lap_z, low_ref, high_ref,
+    places, whole_ref, acc_ref, low_early, high_early, low_other, high_other, inner_in, outer_in, tests_ref,
+    tables_ref, moved_ref, cross_ref, low_out, high_out, grad_z, lap_z, low_ref, high_ref,
 ):
     _, nx, ny, n = whole_ref.shape
     half = ny // 2
@@ -323,7 +332,6 @@
                 advect = advect + own[0] * grad_x
             moved = acc_ref[c, i] + STEP * (VISC * lap - advect)
             moved_ref[c, i] = moved
-            next_ref[c, i] = moved_ref[c, i, mine]
             centred.append(0.5 * (own[c] + moved))
         cx, cy, cz = centred
         for p in range(problems):
@@ -342,6 +350,11 @@
                     third = third + (bend * tests_ref[p, 2, j] - slope * cross_ref[p, 0, j])
                 out[p, 0, m] = second
                 out[p, 1, m] = third
+
+
+def sums_kernel(places, cross_ref, sent_ref, tables_ref, inner_out, outer_out):
+    problems, _, nx, ny, n = cross_ref.shape
+    tables = Tables(tables_ref, places)
     lay = tables.get("lay_cross").astype(BF16)
     lines = nx * ny
     even = in_chip()
@@ -385,22 +398,49 @@
                 out_ref[p, c, i] = value[c]
 
 
-def finish_kernel(places, part_ref, low_ref, high_ref, inner_in, outer_in, tables_ref, out_ref, held, sems):
+def land_kernel(
+    places, part_ref, inner_in, outer_in, tables_ref, moved_ref, out_ref, edge_ref, next_ref, held, sems
+):
     problems, _, nx, ny, n = part_ref.shape
     land = Tables(tables_ref, places).get("land").astype(BF16)
     raw = taken_in(inner_in, outer_in)
     lines = nx * ny
-    copies = []
+    half = ny // 2
+    mine = pl.ds(pl.multiple_of(lax.axis_index("sec") * half, half), half)
+    copies = [pltpu.make_async_copy(moved_ref.at[:, :, mine], next_ref, sems.at[3 * problems])]
+    copies[0].start()
     for p in range(problems):
         for c in range(3):
             at = (3 * p + c) * lines
             held[p, c] = part_ref[p, c] + lines_in(raw[:, at : at + lines], land).reshape(nx, ny, n)
+            whole = pl.ds(0, nx) if c == 0 else pl.ds(3, nx - 6)
+            copies.append(pltpu.make_async_copy(held.at[p, c, whole], out_ref.at[p, c, whole], sems.at[3 * p + c]))
+            copies[-1].start()
             if c > 0:
-                held[p, c, 0:3] += low_ref[p, c - 1]
-                for m in range(3):
-                    held[p, c, nx - 1 - m] += high_ref[p, c - 1, m]
-            copies.append(pltpu.make_async_copy(held.at[p, c], out_ref.at[p, c], sems.at[3 * p + c]))
-            copies[-1].start()
+                edge_ref[p, c - 1, 0:3] = held[p, c, 0:3]
+                edge_ref[p, c - 1, 3:6] = held[p, c, nx - 3 : nx]
+    for copy in copies:
+        copy.wait()
+
+
+def finish_kernel(edge_ref, low_ref, high_ref, _, out_ref, held, sems):
+    problems = edge_ref.shape[0]
+    nx = out_ref.shape[2]
+    copies = []
+    for p in range(problems):
+        for c in range(2):
+            held[p, c, 0:3] = edge_ref[p, c, 0:3] + low_ref[p, c]
+            for m in range(3):
+                held[p, c, 5 - m] = edge_ref[p, c, 5 - m] + high_ref[p, c, m]
+            for side, start in ((0, 0), (1, nx - 3)):
+                copies.append(
+                    pltpu.make_async_copy(
+                        held.at[p, c, pl.ds(3 * side, 3)],
+                        out_ref.at[p, c + 1, pl.ds(start, 3)],
+                        sems.at[4 * p + 2 * c + side],
+                    )
+                )
+                copies[-1].start()
     for copy in copies:
         copy.wait()
 
@@ -421,22 +461,24 @@
     problems, _, _, ny, _ = tests.shape
     lines = nx * ny
     constants, places = make_tables(n, nx * lax.axis_size("gx"), ny, n * lax.axis_size("gz"))
-    params = pltpu.CompilerParams(vmem_limit_bytes=VMEM_LIMIT)
     vmem = pl.BlockSpec(memory_space=pltpu.VMEM)
 
     def shape(*dims):
         return jax.ShapeDtypeStruct(dims, F32)
 
-    def run(kernel, name, args, outs, scratch=(), flops=10**8, out_specs=None, bind=True):
+    def run(kernel, name, args, outs, scratch=(), flops=10**8, out_specs=None, bind=True, in_space=pltpu.VMEM, limit=VMEM_LIMIT, alias=None):
         body = kernel if not bind else (lambda *refs: kernel(places, *refs))
         moved = 4 * sum(math.prod(a.shape) for a in (*args, *outs))
         return pl.pallas_call(
             body,
-            in_specs=[vmem] * len(args),
+            in_specs=[
+                pl.BlockSpec(memory_space=pl.ANY if k in (alias or {}) else in_space) for k in range(len(args))
+            ],
+            input_output_aliases=alias or {},
             out_specs=[vmem] * len(outs) if out_specs is None else out_specs,
             out_shape=list(outs),
             scratch_shapes=list(scratch),
-            compiler_params=params,
+            compiler_params=pltpu.CompilerParams(vmem_limit_bytes=limit),
             cost_estimate=pl.CostEstimate(flops=flops, bytes_accessed=moved, transcendentals=0),
             name=name,
         )(*args)
@@ -446,7 +488,10 @@
     other = shifted(velocity, "sec", 1)
     (tables,) = run(tables_kernel, "tables", [jnp.asarray(constants)], [shape(*constants.shape)], bind=False)
     rows = early_rows(tests_shape, half)[2]
-    low, high = run(faces_kernel, "faces", [tests, velocity], [shape(rows, n)] * 2, bind=False)
+    low, high = run(
+        faces_kernel, "faces", [tests, velocity], [shape(rows, n)] * 2,
+        [pltpu.SemaphoreType.DMA((2 * problems + 2,))], bind=False, in_space=pl.ANY, limit=FACES_LIMIT,
+    )
     early = [shifted(high, "gx", 1), shifted(low, "gx", -1)]
     part, sent = run(
         spread_kernel, "spread", [tests, tables],
@@ -454,7 +499,7 @@
         [pltpu.VMEM((3, ny + 16, n), F32)], flops=10**9,
     )
     whole, low, high, inner, outer = run(
-        whole_kernel, "whole", [velocity, other, tables],
+        whole_kernel, "whole", [velocity, other, tables, sent],
         [shape(*whole_shape)] + [shape(3, 3, half, n)] * 2 + [shape(4, 3 * lines)] * 2,
     )
     from_low = shifted(high, "gx", 1)
@@ -466,28 +511,34 @@
         [pltpu.VMEM((3, ny + 16, n), F32), pltpu.VMEM(whole_shape, F32), pltpu.VMEM(whole_shape, F32)],
         flops=10**9,
     )
-    velocity_next, cross, low, high, inner, outer = run(
-        step_kernel, "step", [whole, acc, *early, from_low, from_high, inner, outer, tests, sent, tables],
-        [
-            shape(3, nx, half, n), shape(*tests_shape), shape(problems, 2, 3, ny, n), shape(problems, 2, 3, ny, n),
-            shape(4, problems * 3 * lines), shape(4, problems * 3 * lines),
-        ],
-        [pltpu.VMEM(whole_shape, F32)] * 3 + [pltpu.VMEM((3, 3, ny, n), F32)] * 2, flops=10**9,
+    moved, cross, low, high = run(
+        step_kernel, "step", [whole, acc, *early, from_low, from_high, inner, outer, tests, tables],
+        [shape(*whole_shape), shape(*tests_shape)] + [shape(problems, 2, 3, ny, n)] * 2,
+        [pltpu.VMEM(whole_shape, F32)] * 2 + [pltpu.VMEM((3, 3, ny, n), F32)] * 2, flops=10**9,
     )
     from_low = shifted(high, "gx", 1)
     from_high = shifted(low, "gx", -1)
+    inner, outer = run(
+        sums_kernel, "sums", [cross, sent, tables], [shape(4, problems * 3 * lines)] * 2,
+    )
     outer = swapped(outer, "gz", 1)
     inner = swapped(inner, "gz", 0)
     (part,) = run(
         curl_kernel, "curl", [part, cross, *early, tables], [shape(*tests_shape)],
         [pltpu.VMEM((2, ny + 16, n), F32)], flops=10**9,
     )
+    any_space = pl.BlockSpec(memory_space=pl.ANY)
+    edge_shape = (problems, 2, 6, ny, n)
+    test_next, edge, velocity_next = run(
+        land_kernel, "land", [part, inner, outer, tables, moved],
+        [shape(*tests_shape), shape(*edge_shape), shape(3, nx, half, n)],
+        [pltpu.VMEM(tests_shape, F32), pltpu.SemaphoreType.DMA((3 * problems + 1,))],
+        out_specs=[any_space, pl.BlockSpec(memory_space=pltpu.VMEM), any_space],
+    )
     (test_next,) = run(
-        finish_kernel, "finish",
-        [part, from_low, from_high, inner, outer, tables],
-        [shape(*tests_shape)],
-        [pltpu.VMEM(tests_shape, F32), pltpu.SemaphoreType.DMA((3 * problems,))],
-        flops=10**9, out_specs=[pl.BlockSpec(memory_space=pl.ANY)],
+        finish_kernel, "finish", [edge, from_low, from_high, test_next], [shape(*tests_shape)],
+        [pltpu.VMEM(edge_shape, F32), pltpu.SemaphoreType.DMA((4 * problems,))],
+        out_specs=[any_space], bind=False, alias={3: 0},
     )
     return velocity_next, test_next
 

time: 40 us -> 37.3 us (0.932)
  waiting for transfers between devices: 5.25 us -> 2.32 us
  Pallas kernels: 8.97 us -> 11.3 us
  local copies, waits for them, and re-layouts: 2.42 us -> 1.42 us
  starting transfers between devices: 21.9 us -> 21 us
    ppermute x7, waiting for transfers between devices: 4.04 us -> 0.59 us  [shifted(): lax.ppermute(block, axis, [(i, (i + distance) % count) for i in range(cou...]
    pallas_call x8 -> x10, Pallas kernels: 8.97 us -> 11.3 us  [run(): pl.pallas_call(body, in_specs=[pl.BlockSpec(memory_space=pl.ANY if k in (...]
    unnamed x10 -> x8, local copies, waits for them, and re-layouts: 2.42 us -> 1.42 us
    ppermute x4, starting transfers between devices: 6.91 us -> 6.21 us  [swapped(): return lax.ppermute(block, axis, pairs + [(b, a) for a, b in pairs])]
    ppermute x4, waiting for transfers between devices: 1.22 us -> 1.72 us  [swapped(): return lax.ppermute(block, axis, pairs + [(b, a) for a, b in pairs])]
  transfers between devices with their start and end apart: 11 -> 11, of which waited for: 3 -> 3; matrix products, arithmetic and copies ran while one was open for 0% -> 0% of each run, Pallas kernels for 14% -> 25%
where the time goes in v4:
time: 37.3 us; the launch traced here: 36.8 us
  starting transfers between devices  21 us (56%)
  Pallas kernels  11.3 us (30%)
  waiting for transfers between devices  2.32 us (6%)
  local copies, waits for them, and re-layouts  1.42 us (4%)
  between operations  0.78 us (2%)
    ppermute x7, starting transfers between devices, shifted(): lax.ppermute(block, axis, [(i, (i + distance) % count) for i in range(cou...  14.8 us
    pallas_call x10, Pallas kernels, run(): pl.pallas_call(body, in_specs=[pl.BlockSpec(memory_space=pl.ANY if k in (...  11.3 us
    ppermute x4, starting transfers between devices, swapped(): return lax.ppermute(block, axis, pairs + [(b, a) for a, b in pairs])  6.21 us
    ppermute x4, waiting for transfers between devices, swapped(): return lax.ppermute(block, axis, pairs + [(b, a) for a, b in pairs])  1.72 us
    unnamed x8, local copies, waits for them, and re-layouts  1.42 us
  transfers between devices with their start and end apart: 11, of which 3 were waited for; matrix products, arithmetic and copies ran while one was open for 0% of the time, Pallas kernels for 25%

profile of v4, /device:TPU:0, one launch (start us, length us, event | category | flops | bytes accessed | tf_op | source)
XLA Modules:
  0.0 36.8 jit_solution(3780547563607347374)
XLA Ops:
  0.6 0.0 copy-start.3
  0.6 3.4 %collective-permute-start = (f32[3,8,32,128]{3,2,1,0:T(8,128)}, f32[3,8,32,128]{3,2,1,0:T(8,128)S(1)}, u32[]{:S(2)}, u32[]{:S(2)}) collective-permute-start(f32[3,8,32,128]{3,2,1,0:T(8,128)} %own_ref.1), channel_id=1, source_target_pairs={{0,64},{64,0},{1,65},{65,1},{2,66},{66,2},{3,67},{67,3},{4,68},{68... | collective-permute-start | bytes 1179656 | tf_op jit(solution)/shard_map/ppermute | solution.py:450
  4.0 2.1 %faces.1 = (f32[672,128]{1,0:T(8,128)}, f32[672,128]{1,0:T(8,128)}) custom-call(f32[2,3,8,64,128]{4,3,2,1,0:T(8,128)} %refs_8_.1, f32[3,8,32,128]{3,2,1,0:T(8,128)} %own_ref.1), custom_call_target="tpu_custom_call" | custom-call | flops 100000000 | bytes 2654208 | tf_op jit(solution)/shard_map/faces/pallas_call | solution.py:472
  6.1 2.0 %collective-permute-start.1 = (f32[672,128]{1,0:T(8,128)}, f32[672,128]{1,0:T(8,128)S(1)}, u32[]{:S(2)}, u32[]{:S(2)}) collective-permute-start(f32[672,128]{1,0:T(8,128)} %get-tuple-element.23), channel_id=1, source_target_pairs={{0,1},{1,2},{2,3},{3,0},{4,5},{5,6},{6,7},{7,4},{8,9},{9,10},{10,1... | collective-permute-start | bytes 1032200 | tf_op jit(solution)/shard_map/ppermute | solution.py:450
  8.1 2.2 %collective-permute-start.2 = (f32[672,128]{1,0:T(8,128)}, f32[672,128]{1,0:T(8,128)S(1)}, u32[]{:S(2)}, u32[]{:S(2)}) collective-permute-start(f32[672,128]{1,0:T(8,128)} %get-tuple-element.24), channel_id=1, source_target_pairs={{0,3},{1,0},{2,1},{3,2},{4,7},{5,4},{6,5},{7,6},{8,11},{9,8},{10,9... | collective-permute-start | bytes 1032200 | tf_op jit(solution)/shard_map/ppermute | solution.py:450
  10.3 0.0 copy-start
  10.3 1.4 %copy-done = f32[2,3,8,64,128]{4,3,2,1,0:T(8,128)S(1)} copy-done((f32[2,3,8,64,128]{4,3,2,1,0:T(8,128)S(1)}, f32[2,3,8,64,128]{4,3,2,1,0:T(8,128)}, u32[]{:S(2)}) %copy-start) | copy-done | bytes 1572888
  11.7 1.8 %spread.1 = (f32[2,3,8,64,128]{4,3,2,1,0:T(8,128)S(1)}, f32[8,3072]{1,0:T(8,128)S(1)}) custom-call(f32[2,3,8,64,128]{4,3,2,1,0:T(8,128)S(1)} %copy-done, f32[1392,128]{1,0:T(8,128)S(1)} %tables.1.refs_1_.refs_2_.refs_9_.refs_4_.refs_3_), custom_call_target="tpu_custom_call" | custom-call | flops 1000000000 | bytes 3956736 | tf_op jit(solution)/shard_map/spread/pallas_call | solution.py:472
  13.6 0.0 collective-permute-done.refs_1_
  13.6 0.4 %whole.1 = (f32[3,8,64,128]{3,2,1,0:T(8,128)S(1)}, f32[3,3,32,128]{3,2,1,0:T(8,128)S(1)}, f32[3,3,32,128]{3,2,1,0:T(8,128)S(1)}, f32[4,1536]{1,0:T(4,128)S(1)}, f32[4,1536]{1,0:T(4,128)S(1)}) custom-call(f32[3,8,32,128]{3,2,1,0:T(8,128)S(1)} %copy-done.2, f32[3,8,32,128]{3,2,1,0:T(8,128)S(1)} %collective-permute-done.refs_1_, ...), custom_call_target="tpu_custom_call" | custom-call | flops 100000000 | bytes 2727936 | tf_op jit(solution)/shard_map/whole/pallas_call | solution.py:472
  14.0 1.8 %collective-permute-start.3 = (f32[3,3,32,128]{3,2,1,0:T(8,128)S(1)}, f32[3,3,32,128]{3,2,1,0:T(8,128)S(1)}, u32[]{:S(2)}, u32[]{:S(2)}) collective-permute-start(f32[3,3,32,128]{3,2,1,0:T(8,128)S(1)} %get-tuple-element.25), channel_id=1, source_target_pairs={{0,1},{1,2},{2,3},{3,0},{4,5},{5,6},{6,7},{7,4},{8,9},{9,10},{10,1... | collective-permute-start | bytes 442376 | tf_op jit(solution)/shard_map/ppermute | solution.py:450
  15.8 2.2 %collective-permute-start.4 = (f32[3,3,32,128]{3,2,1,0:T(8,128)S(1)}, f32[3,3,32,128]{3,2,1,0:T(8,128)S(1)}, u32[]{:S(2)}, u32[]{:S(2)}) collective-permute-start(f32[3,3,32,128]{3,2,1,0:T(8,128)S(1)} %get-tuple-element.26), channel_id=1, source_target_pairs={{0,3},{1,0},{2,1},{3,2},{4,7},{5,4},{6,5},{7,6},{8,11},{9,8},{10,9... | collective-permute-start | bytes 442376 | tf_op jit(solution)/shard_map/ppermute | solution.py:450
  18.0 0.0 collective-permute-start.5
  18.0 0.6 %collective-permute-done.1.refs_2_ = f32[672,128]{1,0:T(8,128)S(1)} collective-permute-done((f32[672,128]{1,0:T(8,128)}, f32[672,128]{1,0:T(8,128)S(1)}, u32[]{:S(2)}, u32[]{:S(2)}) %collective-permute-start.1) | collective-permute-done | bytes 344096 | tf_op jit(solution)/shard_map/ppermute | solution.py:450
  18.6 3.3 %collective-permute-start.6 = (f32[4,1536]{1,0:T(4,128)S(1)}, f32[4,1536]{1,0:T(4,128)S(1)}, u32[]{:S(2)}, u32[]{:S(2)}) collective-permute-start(f32[4,1536]{1,0:T(4,128)S(1)} %get-tuple-element.28), channel_id=1, source_target_pairs={{4,8},{12,16},{20,24},{28,32},{36,40},{44,48},{52,56},{60,0},{8,4}... | collective-permute-start | bytes 73736 | tf_op jit(solution)/shard_map/ppermute | solution.py:456
  21.9 1.8 %flow.1.refs_1_ = f32[3,8,64,128]{3,2,1,0:T(8,128)S(1)} custom-call(f32[3,8,64,128]{3,2,1,0:T(8,128)S(1)} %get-tuple-element.22.refs_0_, f32[1392,128]{1,0:T(8,128)S(1)} %tables.1.refs_1_.refs_2_.refs_9_.refs_4_.refs_3_), custom_call_target="tpu_custom_call" | custom-call | flops 1000000000 | bytes 2285568 | tf_op jit(solution)/shard_map/flow/pallas_call | solution.py:472
  23.7 0.0 collective-permute-done.2.refs_3_
  23.7 0.0 collective-permute-done.5.refs_6_
  23.7 0.2 collective-permute-done.6.refs_7_
  23.9 1.2 %step.1 = (f32[3,8,64,128]{3,2,1,0:T(8,128)S(1)}, f32[2,3,8,64,128]{4,3,2,1,0:T(8,128)S(1)}, f32[2,2,3,64,128]{4,3,2,1,0:T(8,128)S(1)}, f32[2,2,3,64,128]{4,3,2,1,0:T(8,128)S(1)}) custom-call(f32[3,8,64,128]{3,2,1,0:T(8,128)S(1)} %get-tuple-element.22.refs_0_, f32[3,8,64,128]{3,2,1,0:T(8,128)S(1)} %flow.1.refs_1_, ...), custom_call_target="tpu_custom_call" | custom-call | flops 1000000000 | bytes 8036352 | tf_op jit(solution)/shard_map/step/pallas_call | solution.py:472
  25.1 0.1 collective-permute-start.9
  25.2 3.2 %collective-permute-start.10 = (f32[2,2,3,64,128]{4,3,2,1,0:T(8,128)S(1)}, f32[2,2,3,64,128]{4,3,2,1,0:T(8,128)S(1)}, u32[]{:S(2)}, u32[]{:S(2)}) collective-permute-start(f32[2,2,3,64,128]{4,3,2,1,0:T(8,128)S(1)} %get-tuple-element.36), channel_id=1, source_target_pairs={{0,3},{1,0},{2,1},{3,2},{4,7},{5,4},{6,5},{7,6},{8,11},{9,8},{10,9... | collective-permute-start | bytes 1179656 | tf_op jit(solution)/shard_map/ppermute | solution.py:450
  28.4 0.4 %sums.1 = (f32[4,3072]{1,0:T(4,128)S(1)}, f32[4,3072]{1,0:T(4,128)S(1)}) custom-call(f32[2,3,8,64,128]{4,3,2,1,0:T(8,128)S(1)} %get-tuple-element.29.refs_1_.refs_0_, f32[8,3072]{1,0:T(8,128)S(1)} %get-tuple-element.21.refs_3_.refs_1_, f32[1392,128]{1,0:T(8,128)S(1)} %tables.1.refs_1_.refs_2_.refs_9_.refs_4_.refs_3_), custom_call_target="tpu_custom_call" | custom-call | flops 100000000 | bytes 2482176 | tf_op jit(solution)/shard_map/sums/pallas_call | solution.py:472
  28.8 0.1 collective-permute-start.7
  28.9 2.8 %collective-permute-start.8 = (f32[4,3072]{1,0:T(4,128)S(1)}, f32[4,3072]{1,0:T(4,128)S(1)}, u32[]{:S(2)}, u32[]{:S(2)}) collective-permute-start(f32[4,3072]{1,0:T(4,128)S(1)} %get-tuple-element.31), channel_id=1, source_target_pairs={{4,8},{12,16},{20,24},{28,32},{36,40},{44,48},{52,56},{60,0},{8,4}... | collective-permute-start | bytes 147464 | tf_op jit(solution)/shard_map/ppermute | solution.py:456
  31.7 1.4 %curl.1.refs_0_ = f32[2,3,8,64,128]{4,3,2,1,0:T(8,128)S(1)} custom-call(f32[2,3,8,64,128]{4,3,2,1,0:T(8,128)S(1)} %get-tuple-element.20.refs_0_, f32[2,3,8,64,128]{4,3,2,1,0:T(8,128)S(1)} %get-tuple-element.29.refs_1_.refs_0_, f32[672,128]{1,0:T(8,128)S(1)} %collective-permute-done.1.refs_2_, f32[672,128]{1,0:T(8,128)S(1)} %collective-permute-done.2.refs_3_, ...), custom_call_target="tpu_custom_call" | custom-call | flops 1000000000 | bytes 6119424 | tf_op jit(solution)/shard_map/curl/pallas_call | solution.py:472
  33.1 0.0 collective-permute-done.7.refs_1_
  33.1 1.5 %collective-permute-done.8.refs_2_ = f32[4,3072]{1,0:T(4,128)S(1)} collective-permute-done((f32[4,3072]{1,0:T(4,128)S(1)}, f32[4,3072]{1,0:T(4,128)S(1)}, u32[]{:S(2)}, u32[]{:S(2)}) %collective-permute-start.8) | collective-permute-done | bytes 49184 | tf_op jit(solution)/shard_map/ppermute | solution.py:456
  34.6 1.2 %land.1 = (f32[2,3,8,64,128]{4,3,2,1,0:T(8,128)}, f32[2,2,6,64,128]{4,3,2,1,0:T(8,128)S(1)}, f32[3,8,32,128]{3,2,1,0:T(8,128)}) custom-call(f32[2,3,8,64,128]{4,3,2,1,0:T(8,128)S(1)} %curl.1.refs_0_, f32[4,3072]{1,0:T(4,128)S(1)} %collective-permute-done.7.refs_1_, f32[4,3072]{1,0:T(4,128)S(1)} %collective-permute-done.8.refs_2_, ...), custom_call_target="tpu_custom_call" | custom-call | flops 100000000 | bytes 5922816 | tf_op jit(solution)/shard_map/land/pallas_call | solution.py:472
  35.8 0.0 collective-permute-done.9.low_ref
  35.9 0.0 collective-permute-done.10.high_ref
  35.9 1.0 %finish.1 = f32[2,3,8,64,128]{4,3,2,1,0:T(8,128)} custom-call(f32[2,2,6,64,128]{4,3,2,1,0:T(8,128)S(1)} %get-tuple-element.34.edge_ref, f32[2,2,3,64,128]{4,3,2,1,0:T(8,128)S(1)} %collective-permute-done.9.low_ref, f32[2,2,3,64,128]{4,3,2,1,0:T(8,128)S(1)} %collective-permute-done.10.high_ref, ...), custom_call_target="tpu_custom_call", output_to_operand_aliasing={{}: (3, {})} | custom-call | flops 100000000 | bytes 4718592 | tf_op jit(solution)/shard_map/finish/pallas_call | solution.py:472
  (8 shorter events, 0.1 us)
Async XLA Ops:
  0.6 9.6 %copy-start.3 = (f32[1392,128]{1,0:T(8,128)S(1)}, f32[1392,128]{1,0:T(8,128)}, u32[]{:S(2)}) copy-start(f32[1392,128]{1,0:T(8,128)} %constant.2.clone.source) | copy-start | bytes 2138116
  0.6 12.9 %collective-permute-start = (f32[3,8,32,128]{3,2,1,0:T(8,128)}, f32[3,8,32,128]{3,2,1,0:T(8,128)S(1)}, u32[]{:S(2)}, u32[]{:S(2)}) collective-permute-start(f32[3,8,32,128]{3,2,1,0:T(8,128)} %own_ref.1), channel_id=1, source_target_pairs={{0,64},{64,0},{1,65},{65,1},{2,66},{66,2},{3,67},{67,3},{4,68},{68... | collective-permute-start | bytes 1179656 | tf_op jit(solution)/shard_map/ppermute | solution.py:450
  6.1 12.5 %collective-permute-start.1 = (f32[672,128]{1,0:T(8,128)}, f32[672,128]{1,0:T(8,128)S(1)}, u32[]{:S(2)}, u32[]{:S(2)}) collective-permute-start(f32[672,128]{1,0:T(8,128)} %get-tuple-element.23), channel_id=1, source_target_pairs={{0,1},{1,2},{2,3},{3,0},{4,5},{5,6},{6,7},{7,4},{8,9},{9,10},{10,1... | collective-permute-start | bytes 1032200 | tf_op jit(solution)/shard_map/ppermute | solution.py:450
  8.1 15.6 %collective-permute-start.2 = (f32[672,128]{1,0:T(8,128)}, f32[672,128]{1,0:T(8,128)S(1)}, u32[]{:S(2)}, u32[]{:S(2)}) collective-permute-start(f32[672,128]{1,0:T(8,128)} %get-tuple-element.24), channel_id=1, source_target_pairs={{0,3},{1,0},{2,1},{3,2},{4,7},{5,4},{6,5},{7,6},{8,11},{9,8},{10,9... | collective-permute-start | bytes 1032200 | tf_op jit(solution)/shard_map/ppermute | solution.py:450
  10.3 1.4 %copy-start = (f32[2,3,8,64,128]{4,3,2,1,0:T(8,128)S(1)}, f32[2,3,8,64,128]{4,3,2,1,0:T(8,128)}, u32[]{:S(2)}) copy-start(f32[2,3,8,64,128]{4,3,2,1,0:T(8,128)} %refs_8_.1) | copy-start | bytes 4718596
  11.7 1.8 %copy-start.2 = (f32[3,8,32,128]{3,2,1,0:T(8,128)S(1)}, f32[3,8,32,128]{3,2,1,0:T(8,128)}, u32[]{:S(2)}) copy-start(f32[3,8,32,128]{3,2,1,0:T(8,128)} %own_ref.1) | copy-start | bytes 1179652
  14.0 9.9 %collective-permute-start.3 = (f32[3,3,32,128]{3,2,1,0:T(8,128)S(1)}, f32[3,3,32,128]{3,2,1,0:T(8,128)S(1)}, u32[]{:S(2)}, u32[]{:S(2)}) collective-permute-start(f32[3,3,32,128]{3,2,1,0:T(8,128)S(1)} %get-tuple-element.25), channel_id=1, source_target_pairs={{0,1},{1,2},{2,3},{3,0},{4,5},{5,6},{6,7},{7,4},{8,9},{9,10},{10,1... | collective-permute-start | bytes 442376 | tf_op jit(solution)/shard_map/ppermute | solution.py:450
  15.8 8.2 %collective-permute-start.4 = (f32[3,3,32,128]{3,2,1,0:T(8,128)S(1)}, f32[3,3,32,128]{3,2,1,0:T(8,128)S(1)}, u32[]{:S(2)}, u32[]{:S(2)}) collective-permute-start(f32[3,3,32,128]{3,2,1,0:T(8,128)S(1)} %get-tuple-element.26), channel_id=1, source_target_pairs={{0,3},{1,0},{2,1},{3,2},{4,7},{5,4},{6,5},{7,6},{8,11},{9,8},{10,9... | collective-permute-start | bytes 442376 | tf_op jit(solution)/shard_map/ppermute | solution.py:450
  18.0 5.7 %collective-permute-start.5 = (f32[4,1536]{1,0:T(4,128)S(1)}, f32[4,1536]{1,0:T(4,128)S(1)}, u32[]{:S(2)}, u32[]{:S(2)}) collective-permute-start(f32[4,1536]{1,0:T(4,128)S(1)} %get-tuple-element.27), channel_id=1, source_target_pairs={{0,4},{8,12},{16,20},{24,28},{32,36},{40,44},{48,52},{56,60},{4,0}... | collective-permute-start | bytes 73736 | tf_op jit(solution)/shard_map/ppermute | solution.py:456
  18.6 5.4 %collective-permute-start.6 = (f32[4,1536]{1,0:T(4,128)S(1)}, f32[4,1536]{1,0:T(4,128)S(1)}, u32[]{:S(2)}, u32[]{:S(2)}) collective-permute-start(f32[4,1536]{1,0:T(4,128)S(1)} %get-tuple-element.28), channel_id=1, source_target_pairs={{4,8},{12,16},{20,24},{28,32},{36,40},{44,48},{52,56},{60,0},{8,4}... | collective-permute-start | bytes 73736 | tf_op jit(solution)/shard_map/ppermute | solution.py:456
  21.9 2.1 %copy-start.1 = (f32[2,3,8,64,128]{4,3,2,1,0:T(8,128)S(1)}, f32[2,3,8,64,128]{4,3,2,1,0:T(8,128)}, u32[]{:S(2)}) copy-start(f32[2,3,8,64,128]{4,3,2,1,0:T(8,128)} %refs_8_.1) | copy-start | bytes 4718596
  25.1 10.7 %collective-permute-start.9 = (f32[2,2,3,64,128]{4,3,2,1,0:T(8,128)S(1)}, f32[2,2,3,64,128]{4,3,2,1,0:T(8,128)S(1)}, u32[]{:S(2)}, u32[]{:S(2)}) collective-permute-start(f32[2,2,3,64,128]{4,3,2,1,0:T(8,128)S(1)} %get-tuple-element.35), channel_id=1, source_target_pairs={{0,1},{1,2},{2,3},{3,0},{4,5},{5,6},{6,7},{7,4},{8,9},{9,10},{10,1... | collective-permute-start | bytes 1179656 | tf_op jit(solution)/shard_map/ppermute | solution.py:450
  25.2 10.7 %collective-permute-start.10 = (f32[2,2,3,64,128]{4,3,2,1,0:T(8,128)S(1)}, f32[2,2,3,64,128]{4,3,2,1,0:T(8,128)S(1)}, u32[]{:S(2)}, u32[]{:S(2)}) collective-permute-start(f32[2,2,3,64,128]{4,3,2,1,0:T(8,128)S(1)} %get-tuple-element.36), channel_id=1, source_target_pairs={{0,3},{1,0},{2,1},{3,2},{4,7},{5,4},{6,5},{7,6},{8,11},{9,8},{10,9... | collective-permute-start | bytes 1179656 | tf_op jit(solution)/shard_map/ppermute | solution.py:450
  28.8 4.3 %collective-permute-start.7 = (f32[4,3072]{1,0:T(4,128)S(1)}, f32[4,3072]{1,0:T(4,128)S(1)}, u32[]{:S(2)}, u32[]{:S(2)}) collective-permute-start(f32[4,3072]{1,0:T(4,128)S(1)} %get-tuple-element.30), channel_id=1, source_target_pairs={{0,4},{8,12},{16,20},{24,28},{32,36},{40,44},{48,52},{56,60},{4,0}... | collective-permute-start | bytes 147464 | tf_op jit(solution)/shard_map/ppermute | solution.py:456
  28.9 5.7 %collective-permute-start.8 = (f32[4,3072]{1,0:T(4,128)S(1)}, f32[4,3072]{1,0:T(4,128)S(1)}, u32[]{:S(2)}, u32[]{:S(2)}) collective-permute-start(f32[4,3072]{1,0:T(4,128)S(1)} %get-tuple-element.31), channel_id=1, source_target_pairs={{4,8},{12,16},{20,24},{28,32},{36,40},{44,48},{52,56},{60,0},{8,4}... | collective-permute-start | bytes 147464 | tf_op jit(solution)/shard_map/ppermute | solution.py:456

commit v5 on v2

--- a/solution.py
+++ b/solution.py
@@ -16,7 +16,7 @@
 MID = -490.0 / 180.0
 ROOT = math.sqrt(5.0 / 9.0)
 DECAY = -(1.0 - ROOT) / (2.0 / 3.0)
-VMEM_LIMIT = 48 * 1024 * 1024
+VMEM_LIMIT = 12 * 1024 * 1024
 F32 = jnp.float32
 BF16 = jnp.bfloat16
 
@@ -200,10 +200,15 @@
     out[...] = source[...]
 
 
-def faces_kernel(tests_ref, low_ref, high_ref):
-    nx = tests_ref.shape[2]
-    low_ref[...] = tests_ref[:, :, 0:3]
-    high_ref[...] = tests_ref[:, :, nx - 3 : nx]
+def faces_kernel(ref, low_ref, high_ref):
+    nx = ref.shape[-3]
+    low_ref[...] = ref[..., 0:3, :, :]
+    high_ref[...] = ref[..., nx - 3 : nx, :, :]
+
+
+def pack_kernel(first, second, out):
+    out[0] = first[...]
+    out[1] = second[...]
 
 
 def spread_kernel(places, tests_ref, tables_ref, out_ref, sent_ref, pad):
@@ -232,13 +237,11 @@
                 out_ref[p, c, i] = value
 
 
-def whole_kernel(places, own_ref, other_ref, tables_ref, whole_ref, low_ref, high_ref, inner_ref, outer_ref):
+def whole_kernel(places, own_ref, other_ref, tables_ref, whole_ref, inner_ref, outer_ref):
     _, nx, half, n = own_ref.shape
     section = lax.axis_index("sec")
     whole_ref[:, :, pl.ds(pl.multiple_of(section * half, half), half)] = own_ref[...]
     whole_ref[:, :, pl.ds(pl.multiple_of((1 - section) * half, half), half)] = other_ref[...]
-    low_ref[...] = whole_ref[:, 0:3]
-    high_ref[...] = whole_ref[:, nx - 3 : nx]
     pick = Tables(tables_ref, places).get("pick").astype(BF16)
     hand_out(lines_out(whole_ref[...].reshape(-1, n), pick), inner_ref, outer_ref)
 
@@ -275,18 +278,28 @@
             acc_ref[c, i] = own[c] + STEP * (VISC * lap - advect + drive[c])
 
 
+def local_kernel(places, whole_ref, tests_ref, tables_ref, acc_ref, part_ref, sent_ref, pad, grad_z, lap_z):
+    flow_kernel(places, whole_ref, tables_ref, acc_ref, pad, grad_z, lap_z)
+    spread_kernel(places, tests_ref, tables_ref, part_ref, sent_ref, pad)
+
+
 def step_kernel(
-    places, whole_ref, acc_ref, low_ref, high_ref, inner_in, outer_in, tests_ref, sent_ref, tables_ref,
-    next_ref, cross_ref, low_out, high_out, inner_out, outer_out, moved_ref, grad_z, lap_z,
+    places, whole_ref, acc_ref, low_own, high_own, other_faces, inner_in, outer_in, tests_ref,
+    tables_ref, moved_ref, cross_ref, low_out, high_out, grad_z, lap_z, low_ref, high_ref,
 ):
     _, nx, ny, n = whole_ref.shape
     half = ny // 2
     problems = tests_ref.shape[0]
+    section = lax.axis_index("sec")
+    mine = pl.ds(pl.multiple_of(section * half, half), half)
+    theirs = pl.ds(pl.multiple_of((1 - section) * half, half), half)
+    for side, (face, faces_own) in enumerate(((low_ref, low_own), (high_ref, high_own))):
+        face[:, :, mine] = faces_own[...]
+        face[:, :, theirs] = other_faces[side]
     tables = Tables(tables_ref, places)
     raw = taken_in(inner_in, outer_in)
     grad_z[...] = lines_in(raw, tables.get("spread_first").astype(BF16)).reshape(grad_z.shape)
     lap_z[...] = lines_in(raw, tables.get("spread_second").astype(BF16)).reshape(lap_z.shape)
-    mine = pl.ds(pl.multiple_of(lax.axis_index("sec") * half, half), half)
     waves = [wave_parts(tables, p, places["wave"][1] // 2) for p in range(problems)]
     for i in range(nx):
         own = [whole_ref[c, i] for c in range(3)]
@@ -304,7 +317,6 @@
                 advect = advect + own[0] * grad_x
             moved = acc_ref[c, i] + STEP * (VISC * lap - advect)
             moved_ref[c, i] = moved
-            next_ref[c, i] = moved_ref[c, i, mine]
             centred.append(0.5 * (own[c] + moved))
             if i < 3:
                 low_out[c, i] = centred[c]
@@ -316,6 +328,11 @@
             cross_ref[p, 0, i] = cx * tz - cz * tx
             cross_ref[p, 1, i] = cy * tz - cz * ty
             cross_ref[p, 2, i] = cx * ty - cy * tx
+
+
+def sums_kernel(places, cross_ref, sent_ref, tables_ref, inner_out, outer_out):
+    problems, _, nx, ny, n = cross_ref.shape
+    tables = Tables(tables_ref, places)
     lay = tables.get("lay_cross").astype(BF16)
     lines = nx * ny
     even = in_chip()
@@ -359,30 +376,32 @@
 
 
 def finish_kernel(
-    places, part_ref, t_low_ref, t_high_ref, c_low_ref, c_high_ref, inner_in, outer_in, tables_ref,
-    out_ref, held, cross, sems,
+    places, part_ref, inner_in, outer_in, t_low, t_high, c_low, c_high, moved_ref, tables_ref,
+    out_ref, next_ref, held, cross, sems,
 ):
     problems, _, nx, ny, n = part_ref.shape
     tables = Tables(tables_ref, places)
     land = tables.get("land").astype(BF16)
     raw = taken_in(inner_in, outer_in)
     lines = nx * ny
-    copies = []
+    half = ny // 2
+    mine = pl.ds(pl.multiple_of(lax.axis_index("sec") * half, half), half)
+    copies = [pltpu.make_async_copy(moved_ref.at[:, :, mine], next_ref, sems.at[3 * problems])]
+    copies[0].start()
     for p in range(problems):
-        wave_x, wave_y = wave_parts(tables, p, places["wave"][1] // 2)
         for c in range(3):
             at = (3 * p + c) * lines
             held[p, c] = part_ref[p, c] + lines_in(raw[:, at : at + lines], land).reshape(nx, ny, n)
             if c == 0:
-                copies.append(pltpu.make_async_copy(held.at[p, c], out_ref.at[p, c], sems.at[3 * p + c]))
+                copies.append(pltpu.make_async_copy(held.at[p, c], out_ref.at[p, c], sems.at[3 * p]))
                 copies[-1].start()
-        for side, (t_ref, c_ref) in enumerate(((t_low_ref, c_low_ref), (t_high_ref, c_high_ref))):
+        wave_x, wave_y = wave_parts(tables, p, places["wave"][1] // 2)
+        for side, (t_ref, c_ref, sign) in enumerate(((t_low, c_low, -STEP), (t_high, c_high, STEP))):
             for h in range(3):
                 cx, cy, cz = c_ref[0, h], c_ref[1, h], c_ref[2, h]
                 tx, ty, tz = t_ref[p, 0, h] + wave_x, t_ref[p, 1, h] + wave_y, t_ref[p, 2, h]
                 cross[0, h] = cz * tx - cx * tz
                 cross[1, h] = cx * ty - cy * tx
-            sign = -STEP if side == 0 else STEP
             for m in range(3):
                 i = m if side == 0 else nx - 1 - m
                 second, third = held[p, 1, i], held[p, 2, i]
@@ -415,7 +434,6 @@
     problems, _, _, ny, _ = tests.shape
     lines = nx * ny
     constants, places = make_tables(n, nx * lax.axis_size("gx"), ny, n * lax.axis_size("gz"))
-    params = pltpu.CompilerParams(vmem_limit_bytes=VMEM_LIMIT)
     vmem = pl.BlockSpec(memory_space=pltpu.VMEM)
 
     def shape(*dims):
@@ -430,7 +448,7 @@
             out_specs=[vmem] * len(outs) if out_specs is None else out_specs,
             out_shape=list(outs),
             scratch_shapes=list(scratch),
-            compiler_params=params,
+            compiler_params=pltpu.CompilerParams(vmem_limit_bytes=VMEM_LIMIT),
             cost_estimate=pl.CostEstimate(flops=flops, bytes_accessed=moved, transcendentals=0),
             name=name,
         )(*args)
@@ -439,52 +457,49 @@
     tests_shape = (problems, 3, nx, ny, n)
     other = shifted(velocity, "sec", 1)
     (tables,) = run(tables_kernel, "tables", [jnp.asarray(constants)], [shape(*constants.shape)], bind=False)
-    t_low, t_high = run(faces_kernel, "faces", [tests], [shape(problems, 3, 3, ny, n)] * 2, bind=False)
-    t_from_low = shifted(t_high, "gx", 1)
-    t_from_high = shifted(t_low, "gx", -1)
-    part, sent = run(
-        spread_kernel, "spread", [tests, tables],
-        [shape(*tests_shape), shape(8, problems * 3 * lines)],
-        [pltpu.VMEM((3, ny + 16, n), F32)], flops=10**9,
+    v_low, v_high = run(faces_kernel, "flow_faces", [velocity], [shape(3, 3, half, n)] * 2, bind=False)
+    v_own = [shifted(v_high, "gx", 1), shifted(v_low, "gx", -1)]
+    t_low, t_high = run(faces_kernel, "test_faces", [tests], [shape(problems, 3, 3, ny, n)] * 2, bind=False)
+    t_faces = [shifted(t_high, "gx", 1), shifted(t_low, "gx", -1)]
+    (packed,) = run(pack_kernel, "pack", v_own, [shape(2, 3, 3, half, n)], bind=False)
+    v_other = shifted(packed, "sec", 1)
+    whole, inner, outer = run(
+        whole_kernel, "whole", [velocity, other, tables],
+        [shape(*whole_shape)] + [shape(4, 3 * lines)] * 2,
     )
-    whole, low, high, inner, outer = run(
-        whole_kernel, "whole", [velocity, other, tables],
-        [shape(*whole_shape), shape(3, 3, ny, n), shape(3, 3, ny, n), shape(4, 3 * lines), shape(4, 3 * lines)],
+    outer = swapped(outer, "gz", 1)
+    inner = swapped(inner, "gz", 0)
+    acc, part, sent = run(
+        local_kernel, "local", [whole, tests, tables],
+        [shape(*whole_shape), shape(*tests_shape), shape(8, problems * 3 * lines)],
+        [pltpu.VMEM((3, ny + 16, n), F32), pltpu.VMEM(whole_shape, F32), pltpu.VMEM(whole_shape, F32)],
+        flops=4 * 10**9,
+    )
+    moved, cross, low, high = run(
+        step_kernel, "step", [whole, acc, *v_own, v_other, inner, outer, tests, tables],
+        [shape(*whole_shape), shape(*tests_shape)] + [shape(3, 3, ny, n)] * 2,
+        [pltpu.VMEM(whole_shape, F32)] * 2 + [pltpu.VMEM((3, 3, ny, n), F32)] * 2, flops=10**9,
     )
     from_low = shifted(high, "gx", 1)
     from_high = shifted(low, "gx", -1)
-    outer = swapped(outer, "gz", 1)
-    inner = swapped(inner, "gz", 0)
-    (acc,) = run(
-        flow_kernel, "flow", [whole, tables], [shape(*whole_shape)],
-        [pltpu.VMEM((3, ny + 16, n), F32), pltpu.VMEM(whole_shape, F32), pltpu.VMEM(whole_shape, F32)],
-        flops=10**9,
+    inner, outer = run(
+        sums_kernel, "sums", [cross, sent, tables], [shape(4, problems * 3 * lines)] * 2,
     )
-    velocity_next, cross, low, high, inner, outer = run(
-        step_kernel, "step", [whole, acc, from_low, from_high, inner, outer, tests, sent, tables],
-        [
-            shape(3, nx, half, n), shape(*tests_shape), shape(3, 3, ny, n), shape(3, 3, ny, n),
-            shape(4, problems * 3 * lines), shape(4, problems * 3 * lines),
-        ],
-        [pltpu.VMEM(whole_shape, F32)] * 3, flops=10**9,
-    )
-    from_low = shifted(high, "gx", 1)
-    from_high = shifted(low, "gx", -1)
     outer = swapped(outer, "gz", 1)
     inner = swapped(inner, "gz", 0)
     (part,) = run(
-        curl_kernel, "curl", [part, cross, t_from_low, t_from_high, tables], [shape(*tests_shape)],
+        curl_kernel, "curl", [part, cross, *t_faces, tables], [shape(*tests_shape)],
         [pltpu.VMEM((2, ny + 16, n), F32)], flops=10**9,
     )
-    (test_next,) = run(
+    test_next, velocity_next = run(
         finish_kernel, "finish",
-        [part, t_from_low, t_from_high, from_low, from_high, inner, outer, tables],
-        [shape(*tests_shape)],
+        [part, inner, outer, *t_faces, from_low, from_high, moved, tables],
+        [shape(*tests_shape), shape(3, nx, half, n)],
         [
             pltpu.VMEM(tests_shape, F32), pltpu.VMEM((2, 3, ny, n), F32),
-            pltpu.SemaphoreType.DMA((3 * problems,)),
+            pltpu.SemaphoreType.DMA((3 * problems + 1,)),
         ],
-        flops=10**9, out_specs=[pl.BlockSpec(memory_space=pl.ANY)],
+        out_specs=[pl.BlockSpec(memory_space=pl.ANY)] * 2,
     )
     return velocity_next, test_next
 

time: 44 us -> 36 us (0.82)
  waiting for transfers between devices: 8.35 us -> 2.03 us
  Pallas kernels: 11.6 us -> 8.85 us
  starting transfers between devices: 20.6 us -> 21.5 us
    ppermute x7 -> x8, waiting for transfers between devices: 7.2 us -> 0.89 us  [shifted(): lax.ppermute(block, axis, [(i, (i + distance) % count) for i in range(cou...]
    pallas_call x8 -> x10, Pallas kernels: 11.6 us -> 8.85 us  [run(): pl.pallas_call(body, in_specs=[vmem] * len(args), out_specs=[vmem] * len(...]
    ppermute x4, starting transfers between devices: 5.57 us -> 6.99 us  [swapped(): return lax.ppermute(block, axis, pairs + [(b, a) for a, b in pairs])]
    ppermute x7 -> x8, starting transfers between devices: 15 us -> 14.5 us  [shifted(): lax.ppermute(block, axis, [(i, (i + distance) % count) for i in range(cou...]
  transfers between devices with their start and end apart: 11 -> 12, of which waited for: 4 -> 2; matrix products, arithmetic and copies ran while one was open for 0% -> 0% of each run, Pallas kernels for 23% -> 20%
where the time goes in v5:
time: 36 us; the launch traced here: 35.6 us
  starting transfers between devices  21.5 us (60%)
  Pallas kernels  8.85 us (25%)
  local copies, waits for them, and re-layouts  2.45 us (7%)
  waiting for transfers between devices  2.03 us (6%)
  between operations  0.77 us (2%)
    ppermute x8, starting transfers between devices, shifted(): lax.ppermute(block, axis, [(i, (i + distance) % count) for i in range(cou...  14.5 us
    pallas_call x10, Pallas kernels, run(): pl.pallas_call(body, in_specs=[vmem] * len(args), out_specs=[vmem] * len(...  8.85 us
    ppermute x4, starting transfers between devices, swapped(): return lax.ppermute(block, axis, pairs + [(b, a) for a, b in pairs])  6.99 us
    unnamed x10, local copies, waits for them, and re-layouts  2.45 us
    ppermute x4, waiting for transfers between devices, swapped(): return lax.ppermute(block, axis, pairs + [(b, a) for a, b in pairs])  1.13 us
    ppermute x8, waiting for transfers between devices, shifted(): lax.ppermute(block, axis, [(i, (i + distance) % count) for i in range(cou...  0.89 us
  transfers between devices with their start and end apart: 12, of which 2 were waited for; matrix products, arithmetic and copies ran while one was open for 0% of the time, Pallas kernels for 20%

profile of v5, /device:TPU:0, one launch (start us, length us, event | category | flops | bytes accessed | tf_op | source)
XLA Modules:
  0.0 35.6 jit_solution(6018114798151137337)
XLA Ops:
  0.6 3.4 %collective-permute-start = (f32[3,8,32,128]{3,2,1,0:T(8,128)}, f32[3,8,32,128]{3,2,1,0:T(8,128)S(1)}, u32[]{:S(2)}, u32[]{:S(2)}) collective-permute-start(f32[3,8,32,128]{3,2,1,0:T(8,128)} %ref.2), channel_id=1, source_target_pairs={{0,64},{64,0},{1,65},{65,1},{2,66},{66,2},{3,67},{67,3},{4,68},{68... | collective-permute-start | bytes 1179656 | tf_op jit(solution)/shard_map/ppermute | solution.py:423
  4.0 1.0 %copy-done.2 = f32[3,8,32,128]{3,2,1,0:T(8,128)S(1)} copy-done((f32[3,8,32,128]{3,2,1,0:T(8,128)S(1)}, f32[3,8,32,128]{3,2,1,0:T(8,128)}, u32[]{:S(2)}) %copy-start.2) | copy-done | bytes 393240
  5.0 2.0 %collective-permute-start.1 = (f32[3,3,32,128]{3,2,1,0:T(8,128)S(1)}, f32[3,3,32,128]{3,2,1,0:T(8,128)S(1)}, u32[]{:S(2)}, u32[]{:S(2)}) collective-permute-start(f32[3,3,32,128]{3,2,1,0:T(8,128)S(1)} %get-tuple-element.23), channel_id=1, source_target_pairs={{0,1},{1,2},{2,3},{3,0},{4,5},{5,6},{6,7},{7,4},{8,9},{9,10},{10,1... | collective-permute-start | bytes 442376 | tf_op jit(solution)/shard_map/ppermute | solution.py:423
  7.0 2.2 %collective-permute-start.2 = (f32[3,3,32,128]{3,2,1,0:T(8,128)S(1)}, f32[3,3,32,128]{3,2,1,0:T(8,128)S(1)}, u32[]{:S(2)}, u32[]{:S(2)}) collective-permute-start(f32[3,3,32,128]{3,2,1,0:T(8,128)S(1)} %get-tuple-element.24), channel_id=1, source_target_pairs={{0,3},{1,0},{2,1},{3,2},{4,7},{5,4},{6,5},{7,6},{8,11},{9,8},{10,9... | collective-permute-start | bytes 442376 | tf_op jit(solution)/shard_map/ppermute | solution.py:423
  9.2 1.4 %copy-done = f32[2,3,8,64,128]{4,3,2,1,0:T(8,128)S(1)} copy-done((f32[2,3,8,64,128]{4,3,2,1,0:T(8,128)S(1)}, f32[2,3,8,64,128]{4,3,2,1,0:T(8,128)}, u32[]{:S(2)}) %copy-start) | copy-done | bytes 1572888
  10.6 0.1 test_faces.1
  10.7 0.1 collective-permute-start.6
  10.8 0.0 copy-start.1
  10.8 3.2 %collective-permute-start.7 = (f32[2,3,3,64,128]{4,3,2,1,0:T(8,128)S(1)}, f32[2,3,3,64,128]{4,3,2,1,0:T(8,128)S(1)}, u32[]{:S(2)}, u32[]{:S(2)}) collective-permute-start(f32[2,3,3,64,128]{4,3,2,1,0:T(8,128)S(1)} %get-tuple-element.29), channel_id=1, source_target_pairs={{0,3},{1,0},{2,1},{3,2},{4,7},{5,4},{6,5},{7,6},{8,11},{9,8},{10,9... | collective-permute-start | bytes 1769480 | tf_op jit(solution)/shard_map/ppermute | solution.py:423
  14.1 0.0 collective-permute-done.1.first.refs_2_
  14.1 0.0 collective-permute-done.2.second.refs_3_
  14.1 0.4 %collective-permute-start.3 = (f32[2,3,3,32,128]{4,3,2,1,0:T(8,128)S(1)}, f32[2,3,3,32,128]{4,3,2,1,0:T(8,128)S(1)}, u32[]{:S(2)}, u32[]{:S(2)}) collective-permute-start(f32[2,3,3,32,128]{4,3,2,1,0:T(8,128)S(1)} %pack.1), channel_id=1, source_target_pairs={{0,64},{64,0},{1,65},{65,1},{2,66},{66,2},{3,67},{67,3},{4,68},{68... | collective-permute-start | bytes 884744 | tf_op jit(solution)/shard_map/ppermute | solution.py:423
  14.5 0.0 collective-permute-done.refs_1_
  14.6 0.4 %whole.1 = (f32[3,8,64,128]{3,2,1,0:T(8,128)S(1)}, f32[4,1536]{1,0:T(4,128)S(1)}, f32[4,1536]{1,0:T(4,128)S(1)}) custom-call(f32[3,8,32,128]{3,2,1,0:T(8,128)S(1)} %copy-done.3, f32[3,8,32,128]{3,2,1,0:T(8,128)S(1)} %collective-permute-done.refs_1_, f32[1392,128]{1,0:T(8,128)S(1)} %tables.1.refs_2_.refs_8_.refs_4_), custom_call_target="tpu_custom_call" | custom-call | flops 100000000 | bytes 2334720 | tf_op jit(solution)/shard_map/whole/pallas_call | solution.py:445
  14.9 0.1 collective-permute-start.4
  15.0 3.9 %collective-permute-start.5 = (f32[4,1536]{1,0:T(4,128)S(1)}, f32[4,1536]{1,0:T(4,128)S(1)}, u32[]{:S(2)}, u32[]{:S(2)}) collective-permute-start(f32[4,1536]{1,0:T(4,128)S(1)} %get-tuple-element.26), channel_id=1, source_target_pairs={{4,8},{12,16},{20,24},{28,32},{36,40},{44,48},{52,56},{60,0},{8,4}... | collective-permute-start | bytes 73736 | tf_op jit(solution)/shard_map/ppermute | solution.py:429
  18.9 3.8 %local.1 = (f32[3,8,64,128]{3,2,1,0:T(8,128)S(1)}, f32[2,3,8,64,128]{4,3,2,1,0:T(8,128)S(1)}, f32[8,3072]{1,0:T(8,128)S(1)}) custom-call(f32[3,8,64,128]{3,2,1,0:T(8,128)S(1)} %get-tuple-element.20.refs_0_, f32[2,3,8,64,128]{4,3,2,1,0:T(8,128)S(1)} %copy-done.1, f32[1392,128]{1,0:T(8,128)S(1)} %tables.1.refs_2_.refs_8_.refs_4_), custom_call_target="tpu_custom_call" | custom-call | flops 4000000000 | bytes 5529600 | tf_op jit(solution)/shard_map/local/pallas_call | solution.py:445
  22.7 0.0 collective-permute-done.4.refs_5_
  22.7 0.0 collective-permute-done.5.refs_6_
  22.7 0.9 %collective-permute-done.3.refs_4_ = f32[2,3,3,32,128]{4,3,2,1,0:T(8,128)S(1)} collective-permute-done((f32[2,3,3,32,128]{4,3,2,1,0:T(8,128)S(1)}, f32[2,3,3,32,128]{4,3,2,1,0:T(8,128)S(1)}, u32[]{:S(2)}, u32[]{:S(2)}) %collective-permute-start.3) | collective-permute-done | bytes 294944 | tf_op jit(solution)/shard_map/ppermute | solution.py:423
  23.6 0.9 %step.1 = (f32[3,8,64,128]{3,2,1,0:T(8,128)S(1)}, f32[2,3,8,64,128]{4,3,2,1,0:T(8,128)S(1)}, f32[3,3,64,128]{3,2,1,0:T(8,128)S(1)}, f32[3,3,64,128]{3,2,1,0:T(8,128)S(1)}) custom-call(f32[3,8,64,128]{3,2,1,0:T(8,128)S(1)} %get-tuple-element.20.refs_0_, f32[3,8,64,128]{3,2,1,0:T(8,128)S(1)} %get-tuple-element.22.refs_1_, ...), custom_call_target="tpu_custom_call" | custom-call | flops 1000000000 | bytes 7446528 | tf_op jit(solution)/shard_map/step/pallas_call | solution.py:445
  24.6 0.1 collective-permute-start.10
  24.6 3.2 %collective-permute-start.11 = (f32[3,3,64,128]{3,2,1,0:T(8,128)S(1)}, f32[3,3,64,128]{3,2,1,0:T(8,128)S(1)}, u32[]{:S(2)}, u32[]{:S(2)}) collective-permute-start(f32[3,3,64,128]{3,2,1,0:T(8,128)S(1)} %get-tuple-element.34), channel_id=1, source_target_pairs={{0,3},{1,0},{2,1},{3,2},{4,7},{5,4},{6,5},{7,6},{8,11},{9,8},{10,9... | collective-permute-start | bytes 884744 | tf_op jit(solution)/shard_map/ppermute | solution.py:423
  27.9 0.4 %sums.1 = (f32[4,3072]{1,0:T(4,128)S(1)}, f32[4,3072]{1,0:T(4,128)S(1)}) custom-call(f32[2,3,8,64,128]{4,3,2,1,0:T(8,128)S(1)} %get-tuple-element.27.refs_1_.refs_0_, f32[8,3072]{1,0:T(8,128)S(1)} %get-tuple-element.30.refs_1_, f32[1392,128]{1,0:T(8,128)S(1)} %tables.1.refs_2_.refs_8_.refs_4_), custom_call_target="tpu_custom_call" | custom-call | flops 100000000 | bytes 2482176 | tf_op jit(solution)/shard_map/sums/pallas_call | solution.py:445
  28.2 0.1 collective-permute-start.8
  28.3 0.0 collective-permute-done.6.refs_2_.refs_3_
  28.3 3.0 %collective-permute-start.9 = (f32[4,3072]{1,0:T(4,128)S(1)}, f32[4,3072]{1,0:T(4,128)S(1)}, u32[]{:S(2)}, u32[]{:S(2)}) collective-permute-start(f32[4,3072]{1,0:T(4,128)S(1)} %get-tuple-element.32), channel_id=1, source_target_pairs={{4,8},{12,16},{20,24},{28,32},{36,40},{44,48},{52,56},{60,0},{8,4}... | collective-permute-start | bytes 147464 | tf_op jit(solution)/shard_map/ppermute | solution.py:429
  31.3 0.0 collective-permute-done.7.refs_3_.refs_4_
  31.3 1.6 %curl.1.refs_0_ = f32[2,3,8,64,128]{4,3,2,1,0:T(8,128)S(1)} custom-call(f32[2,3,8,64,128]{4,3,2,1,0:T(8,128)S(1)} %get-tuple-element.21.refs_0_, f32[2,3,8,64,128]{4,3,2,1,0:T(8,128)S(1)} %get-tuple-element.27.refs_1_.refs_0_, f32[2,3,3,64,128]{4,3,2,1,0:T(8,128)S(1)} %collective-permute-done.6.refs_2_.refs_3_, ...), custom_call_target="tpu_custom_call" | custom-call | flops 1000000000 | bytes 6610944 | tf_op jit(solution)/shard_map/curl/pallas_call | solution.py:445
  32.9 0.0 collective-permute-done.8.refs_1_
  32.9 1.1 %collective-permute-done.9.refs_2_ = f32[4,3072]{1,0:T(4,128)S(1)} collective-permute-done((f32[4,3072]{1,0:T(4,128)S(1)}, f32[4,3072]{1,0:T(4,128)S(1)}, u32[]{:S(2)}, u32[]{:S(2)}) %collective-permute-start.9) | collective-permute-done | bytes 49184 | tf_op jit(solution)/shard_map/ppermute | solution.py:429
  34.1 1.6 %finish.1 = (f32[2,3,8,64,128]{4,3,2,1,0:T(8,128)}, f32[3,8,32,128]{3,2,1,0:T(8,128)}) custom-call(f32[2,3,8,64,128]{4,3,2,1,0:T(8,128)S(1)} %curl.1.refs_0_, f32[4,3072]{1,0:T(4,128)S(1)} %collective-permute-done.8.refs_1_, f32[4,3072]{1,0:T(4,128)S(1)} %collective-permute-done.9.refs_2_, f32[2,3,3,64,128]{4,3,2,1,0:T(8,128)S(1)} %collective-permute-done.6.refs_2_.refs_3_, ...), custom_call_target="tpu_custom_call" | custom-call | flops 100000000 | bytes 6905856 | tf_op jit(solution)/shard_map/finish/pallas_call | solution.py:445
  (12 shorter events, 0.1 us)
Async XLA Ops:
  0.6 13.9 %collective-permute-start = (f32[3,8,32,128]{3,2,1,0:T(8,128)}, f32[3,8,32,128]{3,2,1,0:T(8,128)S(1)}, u32[]{:S(2)}, u32[]{:S(2)}) collective-permute-start(f32[3,8,32,128]{3,2,1,0:T(8,128)} %ref.2), channel_id=1, source_target_pairs={{0,64},{64,0},{1,65},{65,1},{2,66},{66,2},{3,67},{67,3},{4,68},{68... | collective-permute-start | bytes 1179656 | tf_op jit(solution)/shard_map/ppermute | solution.py:423
  4.0 1.0 %copy-start.2 = (f32[3,8,32,128]{3,2,1,0:T(8,128)S(1)}, f32[3,8,32,128]{3,2,1,0:T(8,128)}, u32[]{:S(2)}) copy-start(f32[3,8,32,128]{3,2,1,0:T(8,128)} %ref.2) | copy-start | bytes 1179652
  5.0 9.0 %collective-permute-start.1 = (f32[3,3,32,128]{3,2,1,0:T(8,128)S(1)}, f32[3,3,32,128]{3,2,1,0:T(8,128)S(1)}, u32[]{:S(2)}, u32[]{:S(2)}) collective-permute-start(f32[3,3,32,128]{3,2,1,0:T(8,128)S(1)} %get-tuple-element.23), channel_id=1, source_target_pairs={{0,1},{1,2},{2,3},{3,0},{4,5},{5,6},{6,7},{7,4},{8,9},{9,10},{10,1... | collective-permute-start | bytes 442376 | tf_op jit(solution)/shard_map/ppermute | solution.py:423
  7.0 7.1 %collective-permute-start.2 = (f32[3,3,32,128]{3,2,1,0:T(8,128)S(1)}, f32[3,3,32,128]{3,2,1,0:T(8,128)S(1)}, u32[]{:S(2)}, u32[]{:S(2)}) collective-permute-start(f32[3,3,32,128]{3,2,1,0:T(8,128)S(1)} %get-tuple-element.24), channel_id=1, source_target_pairs={{0,3},{1,0},{2,1},{3,2},{4,7},{5,4},{6,5},{7,6},{8,11},{9,8},{10,9... | collective-permute-start | bytes 442376 | tf_op jit(solution)/shard_map/ppermute | solution.py:423
  9.2 1.4 %copy-start = (f32[2,3,8,64,128]{4,3,2,1,0:T(8,128)S(1)}, f32[2,3,8,64,128]{4,3,2,1,0:T(8,128)}, u32[]{:S(2)}) copy-start(f32[2,3,8,64,128]{4,3,2,1,0:T(8,128)} %ref.3) | copy-start | bytes 4718596
  10.6 3.4 %copy-start.4 = (f32[1392,128]{1,0:T(8,128)S(1)}, f32[1392,128]{1,0:T(8,128)}, u32[]{:S(2)}) copy-start(f32[1392,128]{1,0:T(8,128)} %constant.2.clone.source) | copy-start | bytes 2138116
  10.6 3.9 %copy-start.3 = (f32[3,8,32,128]{3,2,1,0:T(8,128)S(1)}, f32[3,8,32,128]{3,2,1,0:T(8,128)}, u32[]{:S(2)}) copy-start(f32[3,8,32,128]{3,2,1,0:T(8,128)} %ref.2) | copy-start | bytes 1179652
  10.7 17.6 %collective-permute-start.6 = (f32[2,3,3,64,128]{4,3,2,1,0:T(8,128)S(1)}, f32[2,3,3,64,128]{4,3,2,1,0:T(8,128)S(1)}, u32[]{:S(2)}, u32[]{:S(2)}) collective-permute-start(f32[2,3,3,64,128]{4,3,2,1,0:T(8,128)S(1)} %get-tuple-element.28), channel_id=1, source_target_pairs={{0,1},{1,2},{2,3},{3,0},{4,5},{5,6},{6,7},{7,4},{8,9},{9,10},{10,1... | collective-permute-start | bytes 1769480 | tf_op jit(solution)/shard_map/ppermute | solution.py:423
  10.8 8.1 %copy-start.1 = (f32[2,3,8,64,128]{4,3,2,1,0:T(8,128)S(1)}, f32[2,3,8,64,128]{4,3,2,1,0:T(8,128)}, u32[]{:S(2)}) copy-start(f32[2,3,8,64,128]{4,3,2,1,0:T(8,128)} %ref.3) | copy-start | bytes 4718596
  10.8 20.5 %collective-permute-start.7 = (f32[2,3,3,64,128]{4,3,2,1,0:T(8,128)S(1)}, f32[2,3,3,64,128]{4,3,2,1,0:T(8,128)S(1)}, u32[]{:S(2)}, u32[]{:S(2)}) collective-permute-start(f32[2,3,3,64,128]{4,3,2,1,0:T(8,128)S(1)} %get-tuple-element.29), channel_id=1, source_target_pairs={{0,3},{1,0},{2,1},{3,2},{4,7},{5,4},{6,5},{7,6},{8,11},{9,8},{10,9... | collective-permute-start | bytes 1769480 | tf_op jit(solution)/shard_map/ppermute | solution.py:423
  14.1 9.5 %collective-permute-start.3 = (f32[2,3,3,32,128]{4,3,2,1,0:T(8,128)S(1)}, f32[2,3,3,32,128]{4,3,2,1,0:T(8,128)S(1)}, u32[]{:S(2)}, u32[]{:S(2)}) collective-permute-start(f32[2,3,3,32,128]{4,3,2,1,0:T(8,128)S(1)} %pack.1), channel_id=1, source_target_pairs={{0,64},{64,0},{1,65},{65,1},{2,66},{66,2},{3,67},{67,3},{4,68},{68... | collective-permute-start | bytes 884744 | tf_op jit(solution)/shard_map/ppermute | solution.py:423
  14.9 7.8 %collective-permute-start.4 = (f32[4,1536]{1,0:T(4,128)S(1)}, f32[4,1536]{1,0:T(4,128)S(1)}, u32[]{:S(2)}, u32[]{:S(2)}) collective-permute-start(f32[4,1536]{1,0:T(4,128)S(1)} %get-tuple-element.25), channel_id=1, source_target_pairs={{0,4},{8,12},{16,20},{24,28},{32,36},{40,44},{48,52},{56,60},{4,0}... | collective-permute-start | bytes 73736 | tf_op jit(solution)/shard_map/ppermute | solution.py:429
  15.0 7.7 %collective-permute-start.5 = (f32[4,1536]{1,0:T(4,128)S(1)}, f32[4,1536]{1,0:T(4,128)S(1)}, u32[]{:S(2)}, u32[]{:S(2)}) collective-permute-start(f32[4,1536]{1,0:T(4,128)S(1)} %get-tuple-element.26), channel_id=1, source_target_pairs={{4,8},{12,16},{20,24},{28,32},{36,40},{44,48},{52,56},{60,0},{8,4}... | collective-permute-start | bytes 73736 | tf_op jit(solution)/shard_map/ppermute | solution.py:429
  24.6 9.5 %collective-permute-start.10 = (f32[3,3,64,128]{3,2,1,0:T(8,128)S(1)}, f32[3,3,64,128]{3,2,1,0:T(8,128)S(1)}, u32[]{:S(2)}, u32[]{:S(2)}) collective-permute-start(f32[3,3,64,128]{3,2,1,0:T(8,128)S(1)} %get-tuple-element.33), channel_id=1, source_target_pairs={{0,1},{1,2},{2,3},{3,0},{4,5},{5,6},{6,7},{7,4},{8,9},{9,10},{10,1... | collective-permute-start | bytes 884744 | tf_op jit(solution)/shard_map/ppermute | solution.py:423
  24.6 9.4 %collective-permute-start.11 = (f32[3,3,64,128]{3,2,1,0:T(8,128)S(1)}, f32[3,3,64,128]{3,2,1,0:T(8,128)S(1)}, u32[]{:S(2)}, u32[]{:S(2)}) collective-permute-start(f32[3,3,64,128]{3,2,1,0:T(8,128)S(1)} %get-tuple-element.34), channel_id=1, source_target_pairs={{0,3},{1,0},{2,1},{3,2},{4,7},{5,4},{6,5},{7,6},{8,11},{9,8},{10,9... | collective-permute-start | bytes 884744 | tf_op jit(solution)/shard_map/ppermute | solution.py:423
  28.2 4.7 %collective-permute-start.8 = (f32[4,3072]{1,0:T(4,128)S(1)}, f32[4,3072]{1,0:T(4,128)S(1)}, u32[]{:S(2)}, u32[]{:S(2)}) collective-permute-start(f32[4,3072]{1,0:T(4,128)S(1)} %get-tuple-element.31), channel_id=1, source_target_pairs={{0,4},{8,12},{16,20},{24,28},{32,36},{40,44},{48,52},{56,60},{4,0}... | collective-permute-start | bytes 147464 | tf_op jit(solution)/shard_map/ppermute | solution.py:429
  28.3 5.7 %collective-permute-start.9 = (f32[4,3072]{1,0:T(4,128)S(1)}, f32[4,3072]{1,0:T(4,128)S(1)}, u32[]{:S(2)}, u32[]{:S(2)}) collective-permute-start(f32[4,3072]{1,0:T(4,128)S(1)} %get-tuple-element.32), channel_id=1, source_target_pairs={{4,8},{12,16},{20,24},{28,32},{36,40},{44,48},{52,56},{60,0},{8,4}... | collective-permute-start | bytes 147464 | tf_op jit(solution)/shard_map/ppermute | solution.py:429

commit v6 on v5

--- a/solution.py
+++ b/solution.py
@@ -347,8 +347,12 @@
             outer_out[:, start:stop] = jnp.where(even, sent[4:8], sent[0:4])
 
 
-def curl_kernel(places, part_ref, cross_ref, low_ref, high_ref, tables_ref, out_ref, pad):
+def curl_kernel(places, part_ref, cross_ref, low_ref, high_ref, moved_ref, tables_ref, out_ref, next_ref, pad, sem):
     problems, _, nx, ny, n = part_ref.shape
+    half = ny // 2
+    mine = pl.ds(pl.multiple_of(lax.axis_index("sec") * half, half), half)
+    copy = pltpu.make_async_copy(moved_ref.at[:, :, mine], next_ref, sem)
+    copy.start()
     tables = Tables(tables_ref, places)
     high, low = tables.pair("test_first")
     for p in range(problems):
@@ -373,28 +377,31 @@
                             value[c] = value[c] + (STEP * DIFF * second) * face[p, c, h]
             for c in range(3):
                 out_ref[p, c, i] = value[c]
+    copy.wait()
 
 
 def finish_kernel(
-    places, part_ref, inner_in, outer_in, t_low, t_high, c_low, c_high, moved_ref, tables_ref,
-    out_ref, next_ref, held, cross, sems,
+    places, part_ref, inner_in, outer_in, t_low, t_high, c_low, c_high, tables_ref,
+    out_ref, held, cross, sems,
 ):
     problems, _, nx, ny, n = part_ref.shape
     tables = Tables(tables_ref, places)
     land = tables.get("land").astype(BF16)
     raw = taken_in(inner_in, outer_in)
     lines = nx * ny
-    half = ny // 2
-    mine = pl.ds(pl.multiple_of(lax.axis_index("sec") * half, half), half)
-    copies = [pltpu.make_async_copy(moved_ref.at[:, :, mine], next_ref, sems.at[3 * problems])]
-    copies[0].start()
+    copies = []
+
+    def landed(p, c):
+        at = (3 * p + c) * lines
+        held[p, c] = part_ref[p, c] + lines_in(raw[:, at : at + lines], land).reshape(nx, ny, n)
+
+    def leave(p, c):
+        copies.append(pltpu.make_async_copy(held.at[p, c], out_ref.at[p, c], sems.at[3 * p + c]))
+        copies[-1].start()
+
     for p in range(problems):
-        for c in range(3):
-            at = (3 * p + c) * lines
-            held[p, c] = part_ref[p, c] + lines_in(raw[:, at : at + lines], land).reshape(nx, ny, n)
-            if c == 0:
-                copies.append(pltpu.make_async_copy(held.at[p, c], out_ref.at[p, c], sems.at[3 * p]))
-                copies[-1].start()
+        landed(p, 1)
+        landed(p, 2)
         wave_x, wave_y = wave_parts(tables, p, places["wave"][1] // 2)
         for side, (t_ref, c_ref, sign) in enumerate(((t_low, c_low, -STEP), (t_high, c_high, STEP))):
             for h in range(3):
@@ -411,9 +418,11 @@
                     third = third + (sign * FIRST[d - 1]) * cross[0, h]
                 held[p, 1, i] = second
                 held[p, 2, i] = third
-        for c in (1, 2):
-            copies.append(pltpu.make_async_copy(held.at[p, c], out_ref.at[p, c], sems.at[3 * p + c]))
-            copies[-1].start()
+        leave(p, 1)
+        leave(p, 2)
+    for p in range(problems):
+        landed(p, 0)
+        leave(p, 0)
     for copy in copies:
         copy.wait()
 
@@ -487,19 +496,20 @@
     )
     outer = swapped(outer, "gz", 1)
     inner = swapped(inner, "gz", 0)
-    (part,) = run(
-        curl_kernel, "curl", [part, cross, *t_faces, tables], [shape(*tests_shape)],
-        [pltpu.VMEM((2, ny + 16, n), F32)], flops=10**9,
+    part, velocity_next = run(
+        curl_kernel, "curl", [part, cross, *t_faces, moved, tables], [shape(*tests_shape), shape(3, nx, half, n)],
+        [pltpu.VMEM((2, ny + 16, n), F32), pltpu.SemaphoreType.DMA], flops=10**9,
+        out_specs=[vmem, pl.BlockSpec(memory_space=pl.ANY)],
     )
-    test_next, velocity_next = run(
+    (test_next,) = run(
         finish_kernel, "finish",
-        [part, inner, outer, *t_faces, from_low, from_high, moved, tables],
-        [shape(*tests_shape), shape(3, nx, half, n)],
+        [part, inner, outer, *t_faces, from_low, from_high, tables],
+        [shape(*tests_shape)],
         [
             pltpu.VMEM(tests_shape, F32), pltpu.VMEM((2, 3, ny, n), F32),
-            pltpu.SemaphoreType.DMA((3 * problems + 1,)),
+            pltpu.SemaphoreType.DMA((3 * problems,)),
         ],
-        out_specs=[pl.BlockSpec(memory_space=pl.ANY)] * 2,
+        out_specs=[pl.BlockSpec(memory_space=pl.ANY)],
     )
     return velocity_next, test_next
 

time: 36 us -> 36 us (level)
  no operation moved by 1% of the time
where the time goes in v6:
time: 36 us; the launch traced here: 35.6 us
  starting transfers between devices  21.5 us (60%)
  Pallas kernels  8.76 us (24%)
  local copies, waits for them, and re-layouts  2.45 us (7%)
  waiting for transfers between devices  2.09 us (6%)
  between operations  0.77 us (2%)
    ppermute x8, starting transfers between devices, shifted(): lax.ppermute(block, axis, [(i, (i + distance) % count) for i in range(cou...  14.5 us
    pallas_call x10, Pallas kernels, run(): pl.pallas_call(body, in_specs=[vmem] * len(args), out_specs=[vmem] * len(...  8.76 us
    ppermute x4, starting transfers between devices, swapped(): return lax.ppermute(block, axis, pairs + [(b, a) for a, b in pairs])  6.99 us
    unnamed x10, local copies, waits for them, and re-layouts  2.45 us
    ppermute x4, waiting for transfers between devices, swapped(): return lax.ppermute(block, axis, pairs + [(b, a) for a, b in pairs])  1.2 us
    ppermute x8, waiting for transfers between devices, shifted(): lax.ppermute(block, axis, [(i, (i + distance) % count) for i in range(cou...  0.89 us
  transfers between devices with their start and end apart: 12, of which 2 were waited for; matrix products, arithmetic and copies ran while one was open for 0% of the time, Pallas kernels for 20%

profile of v6, /device:TPU:0, one launch (start us, length us, event | category | flops | bytes accessed | tf_op | source)
XLA Modules:
  0.0 35.6 jit_solution(14735681734396343028)
XLA Ops:
  0.6 3.4 %collective-permute-start = (f32[3,8,32,128]{3,2,1,0:T(8,128)}, f32[3,8,32,128]{3,2,1,0:T(8,128)S(1)}, u32[]{:S(2)}, u32[]{:S(2)}) collective-permute-start(f32[3,8,32,128]{3,2,1,0:T(8,128)} %ref.2), channel_id=1, source_target_pairs={{0,64},{64,0},{1,65},{65,1},{2,66},{66,2},{3,67},{67,3},{4,68},{68... | collective-permute-start | bytes 1179656 | tf_op jit(solution)/shard_map/ppermute | solution.py:432
  4.0 1.0 %copy-done.2 = f32[3,8,32,128]{3,2,1,0:T(8,128)S(1)} copy-done((f32[3,8,32,128]{3,2,1,0:T(8,128)S(1)}, f32[3,8,32,128]{3,2,1,0:T(8,128)}, u32[]{:S(2)}) %copy-start.2) | copy-done | bytes 393240
  5.0 2.0 %collective-permute-start.1 = (f32[3,3,32,128]{3,2,1,0:T(8,128)S(1)}, f32[3,3,32,128]{3,2,1,0:T(8,128)S(1)}, u32[]{:S(2)}, u32[]{:S(2)}) collective-permute-start(f32[3,3,32,128]{3,2,1,0:T(8,128)S(1)} %get-tuple-element.23), channel_id=1, source_target_pairs={{0,1},{1,2},{2,3},{3,0},{4,5},{5,6},{6,7},{7,4},{8,9},{9,10},{10,1... | collective-permute-start | bytes 442376 | tf_op jit(solution)/shard_map/ppermute | solution.py:432
  7.0 2.2 %collective-permute-start.2 = (f32[3,3,32,128]{3,2,1,0:T(8,128)S(1)}, f32[3,3,32,128]{3,2,1,0:T(8,128)S(1)}, u32[]{:S(2)}, u32[]{:S(2)}) collective-permute-start(f32[3,3,32,128]{3,2,1,0:T(8,128)S(1)} %get-tuple-element.24), channel_id=1, source_target_pairs={{0,3},{1,0},{2,1},{3,2},{4,7},{5,4},{6,5},{7,6},{8,11},{9,8},{10,9... | collective-permute-start | bytes 442376 | tf_op jit(solution)/shard_map/ppermute | solution.py:432
  9.2 1.4 %copy-done = f32[2,3,8,64,128]{4,3,2,1,0:T(8,128)S(1)} copy-done((f32[2,3,8,64,128]{4,3,2,1,0:T(8,128)S(1)}, f32[2,3,8,64,128]{4,3,2,1,0:T(8,128)}, u32[]{:S(2)}) %copy-start) | copy-done | bytes 1572888
  10.6 0.1 test_faces.1
  10.7 0.1 collective-permute-start.6
  10.8 0.0 copy-start.1
  10.8 3.2 %collective-permute-start.7 = (f32[2,3,3,64,128]{4,3,2,1,0:T(8,128)S(1)}, f32[2,3,3,64,128]{4,3,2,1,0:T(8,128)S(1)}, u32[]{:S(2)}, u32[]{:S(2)}) collective-permute-start(f32[2,3,3,64,128]{4,3,2,1,0:T(8,128)S(1)} %get-tuple-element.29), channel_id=1, source_target_pairs={{0,3},{1,0},{2,1},{3,2},{4,7},{5,4},{6,5},{7,6},{8,11},{9,8},{10,9... | collective-permute-start | bytes 1769480 | tf_op jit(solution)/shard_map/ppermute | solution.py:432
  14.1 0.0 collective-permute-done.1.first.refs_2_
  14.1 0.0 collective-permute-done.2.second.refs_3_
  14.1 0.4 %collective-permute-start.3 = (f32[2,3,3,32,128]{4,3,2,1,0:T(8,128)S(1)}, f32[2,3,3,32,128]{4,3,2,1,0:T(8,128)S(1)}, u32[]{:S(2)}, u32[]{:S(2)}) collective-permute-start(f32[2,3,3,32,128]{4,3,2,1,0:T(8,128)S(1)} %pack.1), channel_id=1, source_target_pairs={{0,64},{64,0},{1,65},{65,1},{2,66},{66,2},{3,67},{67,3},{4,68},{68... | collective-permute-start | bytes 884744 | tf_op jit(solution)/shard_map/ppermute | solution.py:432
  14.6 0.4 %whole.1 = (f32[3,8,64,128]{3,2,1,0:T(8,128)S(1)}, f32[4,1536]{1,0:T(4,128)S(1)}, f32[4,1536]{1,0:T(4,128)S(1)}) custom-call(f32[3,8,32,128]{3,2,1,0:T(8,128)S(1)} %copy-done.3, f32[3,8,32,128]{3,2,1,0:T(8,128)S(1)} %collective-permute-done.refs_1_, f32[1392,128]{1,0:T(8,128)S(1)} %tables.1.refs_2_.refs_8_.refs_5_.refs_7_), custom_call_target="tpu_custom_call" | custom-call | flops 100000000 | bytes 2334720 | tf_op jit(solution)/shard_map/whole/pallas_call | solution.py:454
  15.0 0.1 collective-permute-start.4
  15.0 3.9 %collective-permute-start.5 = (f32[4,1536]{1,0:T(4,128)S(1)}, f32[4,1536]{1,0:T(4,128)S(1)}, u32[]{:S(2)}, u32[]{:S(2)}) collective-permute-start(f32[4,1536]{1,0:T(4,128)S(1)} %get-tuple-element.26), channel_id=1, source_target_pairs={{4,8},{12,16},{20,24},{28,32},{36,40},{44,48},{52,56},{60,0},{8,4}... | collective-permute-start | bytes 73736 | tf_op jit(solution)/shard_map/ppermute | solution.py:438
  18.9 3.8 %local.1 = (f32[3,8,64,128]{3,2,1,0:T(8,128)S(1)}, f32[2,3,8,64,128]{4,3,2,1,0:T(8,128)S(1)}, f32[8,3072]{1,0:T(8,128)S(1)}) custom-call(f32[3,8,64,128]{3,2,1,0:T(8,128)S(1)} %get-tuple-element.20.refs_0_, f32[2,3,8,64,128]{4,3,2,1,0:T(8,128)S(1)} %copy-done.1, f32[1392,128]{1,0:T(8,128)S(1)} %tables.1.refs_2_.refs_8_.refs_5_.refs_7_), custom_call_target="tpu_custom_call" | custom-call | flops 4000000000 | bytes 5529600 | tf_op jit(solution)/shard_map/local/pallas_call | solution.py:454
  22.7 0.0 collective-permute-done.4.refs_5_
  22.7 0.9 %collective-permute-done.3.refs_4_ = f32[2,3,3,32,128]{4,3,2,1,0:T(8,128)S(1)} collective-permute-done((f32[2,3,3,32,128]{4,3,2,1,0:T(8,128)S(1)}, f32[2,3,3,32,128]{4,3,2,1,0:T(8,128)S(1)}, u32[]{:S(2)}, u32[]{:S(2)}) %collective-permute-start.3) | collective-permute-done | bytes 294944 | tf_op jit(solution)/shard_map/ppermute | solution.py:432
  23.6 1.0 %step.1 = (f32[3,8,64,128]{3,2,1,0:T(8,128)S(1)}, f32[2,3,8,64,128]{4,3,2,1,0:T(8,128)S(1)}, f32[3,3,64,128]{3,2,1,0:T(8,128)S(1)}, f32[3,3,64,128]{3,2,1,0:T(8,128)S(1)}) custom-call(f32[3,8,64,128]{3,2,1,0:T(8,128)S(1)} %get-tuple-element.20.refs_0_, f32[3,8,64,128]{3,2,1,0:T(8,128)S(1)} %get-tuple-element.22.refs_1_, ...), custom_call_target="tpu_custom_call" | custom-call | flops 1000000000 | bytes 7446528 | tf_op jit(solution)/shard_map/step/pallas_call | solution.py:454
  24.6 0.1 collective-permute-start.10
  24.7 3.2 %collective-permute-start.11 = (f32[3,3,64,128]{3,2,1,0:T(8,128)S(1)}, f32[3,3,64,128]{3,2,1,0:T(8,128)S(1)}, u32[]{:S(2)}, u32[]{:S(2)}) collective-permute-start(f32[3,3,64,128]{3,2,1,0:T(8,128)S(1)} %get-tuple-element.37), channel_id=1, source_target_pairs={{0,3},{1,0},{2,1},{3,2},{4,7},{5,4},{6,5},{7,6},{8,11},{9,8},{10,9... | collective-permute-start | bytes 884744 | tf_op jit(solution)/shard_map/ppermute | solution.py:432
  27.9 0.4 %sums.1 = (f32[4,3072]{1,0:T(4,128)S(1)}, f32[4,3072]{1,0:T(4,128)S(1)}) custom-call(f32[2,3,8,64,128]{4,3,2,1,0:T(8,128)S(1)} %get-tuple-element.27.refs_1_.refs_0_, f32[8,3072]{1,0:T(8,128)S(1)} %get-tuple-element.33.refs_1_, f32[1392,128]{1,0:T(8,128)S(1)} %tables.1.refs_2_.refs_8_.refs_5_.refs_7_), custom_call_target="tpu_custom_call" | custom-call | flops 100000000 | bytes 2482176 | tf_op jit(solution)/shard_map/sums/pallas_call | solution.py:454
  28.3 0.1 collective-permute-start.8
  28.3 0.0 collective-permute-done.6.refs_2_.refs_3_
  28.4 3.0 %collective-permute-start.9 = (f32[4,3072]{1,0:T(4,128)S(1)}, f32[4,3072]{1,0:T(4,128)S(1)}, u32[]{:S(2)}, u32[]{:S(2)}) collective-permute-start(f32[4,3072]{1,0:T(4,128)S(1)} %get-tuple-element.35), channel_id=1, source_target_pairs={{4,8},{12,16},{20,24},{28,32},{36,40},{44,48},{52,56},{60,0},{8,4}... | collective-permute-start | bytes 147464 | tf_op jit(solution)/shard_map/ppermute | solution.py:438
  31.3 0.0 collective-permute-done.7.refs_3_.refs_4_
  31.3 1.5 %curl.1 = (f32[2,3,8,64,128]{4,3,2,1,0:T(8,128)S(1)}, f32[3,8,32,128]{3,2,1,0:T(8,128)}) custom-call(f32[2,3,8,64,128]{4,3,2,1,0:T(8,128)S(1)} %get-tuple-element.21.refs_0_, f32[2,3,8,64,128]{4,3,2,1,0:T(8,128)S(1)} %get-tuple-element.27.refs_1_.refs_0_, f32[2,3,3,64,128]{4,3,2,1,0:T(8,128)S(1)} %collective-permute-done.6.refs_2_.refs_3_, ...), custom_call_target="tpu_custom_call" | custom-call | flops 1000000000 | bytes 7790592 | tf_op jit(solution)/shard_map/curl/pallas_call | solution.py:454
  32.9 0.0 collective-permute-done.8.refs_1_
  32.9 1.2 %collective-permute-done.9.refs_2_ = f32[4,3072]{1,0:T(4,128)S(1)} collective-permute-done((f32[4,3072]{1,0:T(4,128)S(1)}, f32[4,3072]{1,0:T(4,128)S(1)}, u32[]{:S(2)}, u32[]{:S(2)}) %collective-permute-start.9) | collective-permute-done | bytes 49184 | tf_op jit(solution)/shard_map/ppermute | solution.py:438
  34.1 0.0 collective-permute-done.10.refs_5_
  34.1 0.0 collective-permute-done.11.refs_6_
  34.1 1.5 %finish.1 = f32[2,3,8,64,128]{4,3,2,1,0:T(8,128)} custom-call(f32[2,3,8,64,128]{4,3,2,1,0:T(8,128)S(1)} %get-tuple-element.32.refs_0_, f32[4,3072]{1,0:T(4,128)S(1)} %collective-permute-done.8.refs_1_, f32[4,3072]{1,0:T(4,128)S(1)} %collective-permute-done.9.refs_2_, f32[2,3,3,64,128]{4,3,2,1,0:T(8,128)S(1)} %collective-permute-done.6.refs_2_.refs_3_, ...), custom_call_target="tpu_custom_call" | custom-call | flops 100000000 | bytes 5726208 | tf_op jit(solution)/shard_map/finish/pallas_call | solution.py:454
  (12 shorter events, 0.1 us)
Async XLA Ops:
  0.6 13.9 %collective-permute-start = (f32[3,8,32,128]{3,2,1,0:T(8,128)}, f32[3,8,32,128]{3,2,1,0:T(8,128)S(1)}, u32[]{:S(2)}, u32[]{:S(2)}) collective-permute-start(f32[3,8,32,128]{3,2,1,0:T(8,128)} %ref.2), channel_id=1, source_target_pairs={{0,64},{64,0},{1,65},{65,1},{2,66},{66,2},{3,67},{67,3},{4,68},{68... | collective-permute-start | bytes 1179656 | tf_op jit(solution)/shard_map/ppermute | solution.py:432
  4.0 1.0 %copy-start.2 = (f32[3,8,32,128]{3,2,1,0:T(8,128)S(1)}, f32[3,8,32,128]{3,2,1,0:T(8,128)}, u32[]{:S(2)}) copy-start(f32[3,8,32,128]{3,2,1,0:T(8,128)} %ref.2) | copy-start | bytes 1179652
  5.0 9.0 %collective-permute-start.1 = (f32[3,3,32,128]{3,2,1,0:T(8,128)S(1)}, f32[3,3,32,128]{3,2,1,0:T(8,128)S(1)}, u32[]{:S(2)}, u32[]{:S(2)}) collective-permute-start(f32[3,3,32,128]{3,2,1,0:T(8,128)S(1)} %get-tuple-element.23), channel_id=1, source_target_pairs={{0,1},{1,2},{2,3},{3,0},{4,5},{5,6},{6,7},{7,4},{8,9},{9,10},{10,1... | collective-permute-start | bytes 442376 | tf_op jit(solution)/shard_map/ppermute | solution.py:432
  7.0 7.1 %collective-permute-start.2 = (f32[3,3,32,128]{3,2,1,0:T(8,128)S(1)}, f32[3,3,32,128]{3,2,1,0:T(8,128)S(1)}, u32[]{:S(2)}, u32[]{:S(2)}) collective-permute-start(f32[3,3,32,128]{3,2,1,0:T(8,128)S(1)} %get-tuple-element.24), channel_id=1, source_target_pairs={{0,3},{1,0},{2,1},{3,2},{4,7},{5,4},{6,5},{7,6},{8,11},{9,8},{10,9... | collective-permute-start | bytes 442376 | tf_op jit(solution)/shard_map/ppermute | solution.py:432
  9.2 1.4 %copy-start = (f32[2,3,8,64,128]{4,3,2,1,0:T(8,128)S(1)}, f32[2,3,8,64,128]{4,3,2,1,0:T(8,128)}, u32[]{:S(2)}) copy-start(f32[2,3,8,64,128]{4,3,2,1,0:T(8,128)} %ref.3) | copy-start | bytes 4718596
  10.6 3.4 %copy-start.4 = (f32[1392,128]{1,0:T(8,128)S(1)}, f32[1392,128]{1,0:T(8,128)}, u32[]{:S(2)}) copy-start(f32[1392,128]{1,0:T(8,128)} %constant.2.clone.source) | copy-start | bytes 2138116
  10.6 3.9 %copy-start.3 = (f32[3,8,32,128]{3,2,1,0:T(8,128)S(1)}, f32[3,8,32,128]{3,2,1,0:T(8,128)}, u32[]{:S(2)}) copy-start(f32[3,8,32,128]{3,2,1,0:T(8,128)} %ref.2) | copy-start | bytes 1179652
  10.7 17.6 %collective-permute-start.6 = (f32[2,3,3,64,128]{4,3,2,1,0:T(8,128)S(1)}, f32[2,3,3,64,128]{4,3,2,1,0:T(8,128)S(1)}, u32[]{:S(2)}, u32[]{:S(2)}) collective-permute-start(f32[2,3,3,64,128]{4,3,2,1,0:T(8,128)S(1)} %get-tuple-element.28), channel_id=1, source_target_pairs={{0,1},{1,2},{2,3},{3,0},{4,5},{5,6},{6,7},{7,4},{8,9},{9,10},{10,1... | collective-permute-start | bytes 1769480 | tf_op jit(solution)/shard_map/ppermute | solution.py:432
  10.8 8.1 %copy-start.1 = (f32[2,3,8,64,128]{4,3,2,1,0:T(8,128)S(1)}, f32[2,3,8,64,128]{4,3,2,1,0:T(8,128)}, u32[]{:S(2)}) copy-start(f32[2,3,8,64,128]{4,3,2,1,0:T(8,128)} %ref.3) | copy-start | bytes 4718596
  10.8 20.5 %collective-permute-start.7 = (f32[2,3,3,64,128]{4,3,2,1,0:T(8,128)S(1)}, f32[2,3,3,64,128]{4,3,2,1,0:T(8,128)S(1)}, u32[]{:S(2)}, u32[]{:S(2)}) collective-permute-start(f32[2,3,3,64,128]{4,3,2,1,0:T(8,128)S(1)} %get-tuple-element.29), channel_id=1, source_target_pairs={{0,3},{1,0},{2,1},{3,2},{4,7},{5,4},{6,5},{7,6},{8,11},{9,8},{10,9... | collective-permute-start | bytes 1769480 | tf_op jit(solution)/shard_map/ppermute | solution.py:432
  14.1 9.5 %collective-permute-start.3 = (f32[2,3,3,32,128]{4,3,2,1,0:T(8,128)S(1)}, f32[2,3,3,32,128]{4,3,2,1,0:T(8,128)S(1)}, u32[]{:S(2)}, u32[]{:S(2)}) collective-permute-start(f32[2,3,3,32,128]{4,3,2,1,0:T(8,128)S(1)} %pack.1), channel_id=1, source_target_pairs={{0,64},{64,0},{1,65},{65,1},{2,66},{66,2},{3,67},{67,3},{4,68},{68... | collective-permute-start | bytes 884744 | tf_op jit(solution)/shard_map/ppermute | solution.py:432
  15.0 7.8 %collective-permute-start.4 = (f32[4,1536]{1,0:T(4,128)S(1)}, f32[4,1536]{1,0:T(4,128)S(1)}, u32[]{:S(2)}, u32[]{:S(2)}) collective-permute-start(f32[4,1536]{1,0:T(4,128)S(1)} %get-tuple-element.25), channel_id=1, source_target_pairs={{0,4},{8,12},{16,20},{24,28},{32,36},{40,44},{48,52},{56,60},{4,0}... | collective-permute-start | bytes 73736 | tf_op jit(solution)/shard_map/ppermute | solution.py:438
  15.0 7.7 %collective-permute-start.5 = (f32[4,1536]{1,0:T(4,128)S(1)}, f32[4,1536]{1,0:T(4,128)S(1)}, u32[]{:S(2)}, u32[]{:S(2)}) collective-permute-start(f32[4,1536]{1,0:T(4,128)S(1)} %get-tuple-element.26), channel_id=1, source_target_pairs={{4,8},{12,16},{20,24},{28,32},{36,40},{44,48},{52,56},{60,0},{8,4}... | collective-permute-start | bytes 73736 | tf_op jit(solution)/shard_map/ppermute | solution.py:438
  24.6 9.5 %collective-permute-start.10 = (f32[3,3,64,128]{3,2,1,0:T(8,128)S(1)}, f32[3,3,64,128]{3,2,1,0:T(8,128)S(1)}, u32[]{:S(2)}, u32[]{:S(2)}) collective-permute-start(f32[3,3,64,128]{3,2,1,0:T(8,128)S(1)} %get-tuple-element.36), channel_id=1, source_target_pairs={{0,1},{1,2},{2,3},{3,0},{4,5},{5,6},{6,7},{7,4},{8,9},{9,10},{10,1... | collective-permute-start | bytes 884744 | tf_op jit(solution)/shard_map/ppermute | solution.py:432
  24.7 9.4 %collective-permute-start.11 = (f32[3,3,64,128]{3,2,1,0:T(8,128)S(1)}, f32[3,3,64,128]{3,2,1,0:T(8,128)S(1)}, u32[]{:S(2)}, u32[]{:S(2)}) collective-permute-start(f32[3,3,64,128]{3,2,1,0:T(8,128)S(1)} %get-tuple-element.37), channel_id=1, source_target_pairs={{0,3},{1,0},{2,1},{3,2},{4,7},{5,4},{6,5},{7,6},{8,11},{9,8},{10,9... | collective-permute-start | bytes 884744 | tf_op jit(solution)/shard_map/ppermute | solution.py:432
  28.3 4.6 %collective-permute-start.8 = (f32[4,3072]{1,0:T(4,128)S(1)}, f32[4,3072]{1,0:T(4,128)S(1)}, u32[]{:S(2)}, u32[]{:S(2)}) collective-permute-start(f32[4,3072]{1,0:T(4,128)S(1)} %get-tuple-element.34), channel_id=1, source_target_pairs={{0,4},{8,12},{16,20},{24,28},{32,36},{40,44},{48,52},{56,60},{4,0}... | collective-permute-start | bytes 147464 | tf_op jit(solution)/shard_map/ppermute | solution.py:438
  28.4 5.7 %collective-permute-start.9 = (f32[4,3072]{1,0:T(4,128)S(1)}, f32[4,3072]{1,0:T(4,128)S(1)}, u32[]{:S(2)}, u32[]{:S(2)}) collective-permute-start(f32[4,3072]{1,0:T(4,128)S(1)} %get-tuple-element.35), channel_id=1, source_target_pairs={{4,8},{12,16},{20,24},{28,32},{36,40},{44,48},{52,56},{60,0},{8,4}... | collective-permute-start | bytes 147464 | tf_op jit(solution)/shard_map/ppermute | solution.py:438

commit v7 on v6

--- a/solution.py
+++ b/solution.py
@@ -17,6 +17,7 @@
 ROOT = math.sqrt(5.0 / 9.0)
 DECAY = -(1.0 - ROOT) / (2.0 / 3.0)
 VMEM_LIMIT = 12 * 1024 * 1024
+FACES_LIMIT = int(52.0 * 1024 * 1024)
 F32 = jnp.float32
 BF16 = jnp.bfloat16
 
@@ -204,6 +205,18 @@
     nx = ref.shape[-3]
     low_ref[...] = ref[..., 0:3, :, :]
     high_ref[...] = ref[..., nx - 3 : nx, :, :]
+
+
+def test_faces_kernel(tests_ref, low_ref, high_ref, sems):
+    nx = tests_ref.shape[2]
+    copies = [
+        pltpu.make_async_copy(tests_ref.at[:, :, pl.ds(start, 3)], out, sems.at[k])
+        for k, (start, out) in enumerate(((0, low_ref), (nx - 3, high_ref)))
+    ]
+    for copy in copies:
+        copy.start()
+    for copy in copies:
+        copy.wait()
 
 
 def pack_kernel(first, second, out):
@@ -448,16 +461,16 @@
     def shape(*dims):
         return jax.ShapeDtypeStruct(dims, F32)
 
-    def run(kernel, name, args, outs, scratch=(), flops=10**8, out_specs=None, bind=True):
+    def run(kernel, name, args, outs, scratch=(), flops=10**8, out_specs=None, bind=True, in_space=pltpu.VMEM, limit=VMEM_LIMIT):
         body = kernel if not bind else (lambda *refs: kernel(places, *refs))
         moved = 4 * sum(math.prod(a.shape) for a in (*args, *outs))
         return pl.pallas_call(
             body,
-            in_specs=[vmem] * len(args),
+            in_specs=[pl.BlockSpec(memory_space=in_space)] * len(args),
             out_specs=[vmem] * len(outs) if out_specs is None else out_specs,
             out_shape=list(outs),
             scratch_shapes=list(scratch),
-            compiler_params=pltpu.CompilerParams(vmem_limit_bytes=VMEM_LIMIT),
+            compiler_params=pltpu.CompilerParams(vmem_limit_bytes=limit),
             cost_estimate=pl.CostEstimate(flops=flops, bytes_accessed=moved, transcendentals=0),
             name=name,
         )(*args)
@@ -468,7 +481,10 @@
     (tables,) = run(tables_kernel, "tables", [jnp.asarray(constants)], [shape(*constants.shape)], bind=False)
     v_low, v_high = run(faces_kernel, "flow_faces", [velocity], [shape(3, 3, half, n)] * 2, bind=False)
     v_own = [shifted(v_high, "gx", 1), shifted(v_low, "gx", -1)]
-    t_low, t_high = run(faces_kernel, "test_faces", [tests], [shape(problems, 3, 3, ny, n)] * 2, bind=False)
+    t_low, t_high = run(
+        test_faces_kernel, "test_faces", [tests], [shape(problems, 3, 3, ny, n)] * 2,
+        [pltpu.SemaphoreType.DMA((2,))], bind=False, in_space=pl.ANY, limit=FACES_LIMIT,
+    )
     t_faces = [shifted(t_high, "gx", 1), shifted(t_low, "gx", -1)]
     (packed,) = run(pack_kernel, "pack", v_own, [shape(2, 3, 3, half, n)], bind=False)
     v_other = shifted(packed, "sec", 1)

time: 36 us -> 35.8 us (level)
  local copies, waits for them, and re-layouts: 2.45 us -> 1.04 us
  Pallas kernels: 8.76 us -> 9.93 us
    unnamed x10 -> x8, local copies, waits for them, and re-layouts: 2.45 us -> 1.04 us
    pallas_call x10, Pallas kernels: 8.76 us -> 9.93 us  [run(): pl.pallas_call(body, in_specs=[pl.BlockSpec(memory_space=in_space)] * len...]
  transfers between devices with their start and end apart: 12 -> 12, of which waited for: 2 -> 2; matrix products, arithmetic and copies ran while one was open for 0% -> 0% of each run, Pallas kernels for 20% -> 24%
where the time goes in v7:
time: 35.8 us; the launch traced here: 35.4 us
  starting transfers between devices  21.6 us (60%)
  Pallas kernels  9.93 us (28%)
  waiting for transfers between devices  2.09 us (6%)
  local copies, waits for them, and re-layouts  1.04 us (3%)
  between operations  0.76 us (2%)
    ppermute x8, starting transfers between devices, shifted(): lax.ppermute(block, axis, [(i, (i + distance) % count) for i in range(cou...  14.6 us
    pallas_call x10, Pallas kernels, run(): pl.pallas_call(body, in_specs=[pl.BlockSpec(memory_space=in_space)] * len...  9.93 us
    ppermute x4, starting transfers between devices, swapped(): return lax.ppermute(block, axis, pairs + [(b, a) for a, b in pairs])  6.99 us
    ppermute x4, waiting for transfers between devices, swapped(): return lax.ppermute(block, axis, pairs + [(b, a) for a, b in pairs])  1.2 us
    unnamed x8, local copies, waits for them, and re-layouts  1.04 us
    ppermute x8, waiting for transfers between devices, shifted(): lax.ppermute(block, axis, [(i, (i + distance) % count) for i in range(cou...  0.89 us
  transfers between devices with their start and end apart: 12, of which 2 were waited for; matrix products, arithmetic and copies ran while one was open for 0% of the time, Pallas kernels for 24%

profile of v7, /device:TPU:0, one launch (start us, length us, event | category | flops | bytes accessed | tf_op | source)
XLA Modules:
  0.0 35.4 jit_solution(5040421971010490667)
XLA Ops:
  0.6 3.4 %collective-permute-start = (f32[3,8,32,128]{3,2,1,0:T(8,128)}, f32[3,8,32,128]{3,2,1,0:T(8,128)S(1)}, u32[]{:S(2)}, u32[]{:S(2)}) collective-permute-start(f32[3,8,32,128]{3,2,1,0:T(8,128)} %ref.1), channel_id=1, source_target_pairs={{0,64},{64,0},{1,65},{65,1},{2,66},{66,2},{3,67},{67,3},{4,68},{68... | collective-permute-start | bytes 1179656 | tf_op jit(solution)/shard_map/ppermute | solution.py:445
  4.0 1.0 %copy-done.1 = f32[3,8,32,128]{3,2,1,0:T(8,128)S(1)} copy-done((f32[3,8,32,128]{3,2,1,0:T(8,128)S(1)}, f32[3,8,32,128]{3,2,1,0:T(8,128)}, u32[]{:S(2)}) %copy-start.1) | copy-done | bytes 393240
  5.0 2.0 %collective-permute-start.1 = (f32[3,3,32,128]{3,2,1,0:T(8,128)S(1)}, f32[3,3,32,128]{3,2,1,0:T(8,128)S(1)}, u32[]{:S(2)}, u32[]{:S(2)}) collective-permute-start(f32[3,3,32,128]{3,2,1,0:T(8,128)S(1)} %get-tuple-element.23), channel_id=1, source_target_pairs={{0,1},{1,2},{2,3},{3,0},{4,5},{5,6},{6,7},{7,4},{8,9},{9,10},{10,1... | collective-permute-start | bytes 442376 | tf_op jit(solution)/shard_map/ppermute | solution.py:445
  7.0 2.2 %collective-permute-start.2 = (f32[3,3,32,128]{3,2,1,0:T(8,128)S(1)}, f32[3,3,32,128]{3,2,1,0:T(8,128)S(1)}, u32[]{:S(2)}, u32[]{:S(2)}) collective-permute-start(f32[3,3,32,128]{3,2,1,0:T(8,128)S(1)} %get-tuple-element.24), channel_id=1, source_target_pairs={{0,3},{1,0},{2,1},{3,2},{4,7},{5,4},{6,5},{7,6},{8,11},{9,8},{10,9... | collective-permute-start | bytes 442376 | tf_op jit(solution)/shard_map/ppermute | solution.py:445
  9.2 1.3 %test_faces.1 = (f32[2,3,3,64,128]{4,3,2,1,0:T(8,128)S(1)}, f32[2,3,3,64,128]{4,3,2,1,0:T(8,128)S(1)}) custom-call(f32[2,3,8,64,128]{4,3,2,1,0:T(8,128)} %tests_ref.1), custom_call_target="tpu_custom_call" | custom-call | flops 100000000 | bytes 2752512 | tf_op jit(solution)/shard_map/test_faces/pallas_call | solution.py:467
  10.5 0.1 collective-permute-start.6
  10.6 0.0 copy-start
  10.6 3.2 %collective-permute-start.7 = (f32[2,3,3,64,128]{4,3,2,1,0:T(8,128)S(1)}, f32[2,3,3,64,128]{4,3,2,1,0:T(8,128)S(1)}, u32[]{:S(2)}, u32[]{:S(2)}) collective-permute-start(f32[2,3,3,64,128]{4,3,2,1,0:T(8,128)S(1)} %get-tuple-element.29), channel_id=1, source_target_pairs={{0,3},{1,0},{2,1},{3,2},{4,7},{5,4},{6,5},{7,6},{8,11},{9,8},{10,9... | collective-permute-start | bytes 1769480 | tf_op jit(solution)/shard_map/ppermute | solution.py:445
  13.9 0.0 collective-permute-done.1.first.refs_2_
  13.9 0.0 collective-permute-done.2.second.refs_3_
  13.9 0.4 %collective-permute-start.3 = (f32[2,3,3,32,128]{4,3,2,1,0:T(8,128)S(1)}, f32[2,3,3,32,128]{4,3,2,1,0:T(8,128)S(1)}, u32[]{:S(2)}, u32[]{:S(2)}) collective-permute-start(f32[2,3,3,32,128]{4,3,2,1,0:T(8,128)S(1)} %pack.1), channel_id=1, source_target_pairs={{0,64},{64,0},{1,65},{65,1},{2,66},{66,2},{3,67},{67,3},{4,68},{68... | collective-permute-start | bytes 884744 | tf_op jit(solution)/shard_map/ppermute | solution.py:445
  14.3 0.0 collective-permute-done.refs_1_
  14.3 0.4 %whole.1 = (f32[3,8,64,128]{3,2,1,0:T(8,128)S(1)}, f32[4,1536]{1,0:T(4,128)S(1)}, f32[4,1536]{1,0:T(4,128)S(1)}) custom-call(f32[3,8,32,128]{3,2,1,0:T(8,128)S(1)} %copy-done.2, f32[3,8,32,128]{3,2,1,0:T(8,128)S(1)} %collective-permute-done.refs_1_, f32[1392,128]{1,0:T(8,128)S(1)} %tables.1.refs_2_.refs_8_.refs_5_.refs_7_), custom_call_target="tpu_custom_call" | custom-call | flops 100000000 | bytes 2334720 | tf_op jit(solution)/shard_map/whole/pallas_call | solution.py:467
  14.7 0.1 collective-permute-start.4
  14.8 3.9 %collective-permute-start.5 = (f32[4,1536]{1,0:T(4,128)S(1)}, f32[4,1536]{1,0:T(4,128)S(1)}, u32[]{:S(2)}, u32[]{:S(2)}) collective-permute-start(f32[4,1536]{1,0:T(4,128)S(1)} %get-tuple-element.26), channel_id=1, source_target_pairs={{4,8},{12,16},{20,24},{28,32},{36,40},{44,48},{52,56},{60,0},{8,4}... | collective-permute-start | bytes 73736 | tf_op jit(solution)/shard_map/ppermute | solution.py:451
  18.7 3.8 %local.1 = (f32[3,8,64,128]{3,2,1,0:T(8,128)S(1)}, f32[2,3,8,64,128]{4,3,2,1,0:T(8,128)S(1)}, f32[8,3072]{1,0:T(8,128)S(1)}) custom-call(f32[3,8,64,128]{3,2,1,0:T(8,128)S(1)} %get-tuple-element.20.refs_0_, f32[2,3,8,64,128]{4,3,2,1,0:T(8,128)S(1)} %copy-done, f32[1392,128]{1,0:T(8,128)S(1)} %tables.1.refs_2_.refs_8_.refs_5_.refs_7_), custom_call_target="tpu_custom_call" | custom-call | flops 4000000000 | bytes 5529600 | tf_op jit(solution)/shard_map/local/pallas_call | solution.py:467
  22.5 0.0 collective-permute-done.4.refs_5_
  22.5 0.9 %collective-permute-done.3.refs_4_ = f32[2,3,3,32,128]{4,3,2,1,0:T(8,128)S(1)} collective-permute-done((f32[2,3,3,32,128]{4,3,2,1,0:T(8,128)S(1)}, f32[2,3,3,32,128]{4,3,2,1,0:T(8,128)S(1)}, u32[]{:S(2)}, u32[]{:S(2)}) %collective-permute-start.3) | collective-permute-done | bytes 294944 | tf_op jit(solution)/shard_map/ppermute | solution.py:445
  23.4 1.0 %step.1 = (f32[3,8,64,128]{3,2,1,0:T(8,128)S(1)}, f32[2,3,8,64,128]{4,3,2,1,0:T(8,128)S(1)}, f32[3,3,64,128]{3,2,1,0:T(8,128)S(1)}, f32[3,3,64,128]{3,2,1,0:T(8,128)S(1)}) custom-call(f32[3,8,64,128]{3,2,1,0:T(8,128)S(1)} %get-tuple-element.20.refs_0_, f32[3,8,64,128]{3,2,1,0:T(8,128)S(1)} %get-tuple-element.22.refs_1_, ...), custom_call_target="tpu_custom_call" | custom-call | flops 1000000000 | bytes 7446528 | tf_op jit(solution)/shard_map/step/pallas_call | solution.py:467
  24.4 0.2 collective-permute-start.10
  24.5 3.1 %collective-permute-start.11 = (f32[3,3,64,128]{3,2,1,0:T(8,128)S(1)}, f32[3,3,64,128]{3,2,1,0:T(8,128)S(1)}, u32[]{:S(2)}, u32[]{:S(2)}) collective-permute-start(f32[3,3,64,128]{3,2,1,0:T(8,128)S(1)} %get-tuple-element.37), channel_id=1, source_target_pairs={{0,3},{1,0},{2,1},{3,2},{4,7},{5,4},{6,5},{7,6},{8,11},{9,8},{10,9... | collective-permute-start | bytes 884744 | tf_op jit(solution)/shard_map/ppermute | solution.py:445
  27.7 0.4 %sums.1 = (f32[4,3072]{1,0:T(4,128)S(1)}, f32[4,3072]{1,0:T(4,128)S(1)}) custom-call(f32[2,3,8,64,128]{4,3,2,1,0:T(8,128)S(1)} %get-tuple-element.27.refs_1_.refs_0_, f32[8,3072]{1,0:T(8,128)S(1)} %get-tuple-element.33.refs_1_, f32[1392,128]{1,0:T(8,128)S(1)} %tables.1.refs_2_.refs_8_.refs_5_.refs_7_), custom_call_target="tpu_custom_call" | custom-call | flops 100000000 | bytes 2482176 | tf_op jit(solution)/shard_map/sums/pallas_call | solution.py:467
  28.0 0.1 collective-permute-start.8
  28.1 0.0 collective-permute-done.6.refs_2_.refs_3_
  28.1 3.0 %collective-permute-start.9 = (f32[4,3072]{1,0:T(4,128)S(1)}, f32[4,3072]{1,0:T(4,128)S(1)}, u32[]{:S(2)}, u32[]{:S(2)}) collective-permute-start(f32[4,3072]{1,0:T(4,128)S(1)} %get-tuple-element.35), channel_id=1, source_target_pairs={{4,8},{12,16},{20,24},{28,32},{36,40},{44,48},{52,56},{60,0},{8,4}... | collective-permute-start | bytes 147464 | tf_op jit(solution)/shard_map/ppermute | solution.py:451
  31.1 0.0 collective-permute-done.7.refs_3_.refs_4_
  31.1 1.5 %curl.1 = (f32[2,3,8,64,128]{4,3,2,1,0:T(8,128)S(1)}, f32[3,8,32,128]{3,2,1,0:T(8,128)}) custom-call(f32[2,3,8,64,128]{4,3,2,1,0:T(8,128)S(1)} %get-tuple-element.21.refs_0_, f32[2,3,8,64,128]{4,3,2,1,0:T(8,128)S(1)} %get-tuple-element.27.refs_1_.refs_0_, f32[2,3,3,64,128]{4,3,2,1,0:T(8,128)S(1)} %collective-permute-done.6.refs_2_.refs_3_, ...), custom_call_target="tpu_custom_call" | custom-call | flops 1000000000 | bytes 7790592 | tf_op jit(solution)/shard_map/curl/pallas_call | solution.py:467
  32.6 0.0 collective-permute-done.8.refs_1_
  32.7 1.2 %collective-permute-done.9.refs_2_ = f32[4,3072]{1,0:T(4,128)S(1)} collective-permute-done((f32[4,3072]{1,0:T(4,128)S(1)}, f32[4,3072]{1,0:T(4,128)S(1)}, u32[]{:S(2)}, u32[]{:S(2)}) %collective-permute-start.9) | collective-permute-done | bytes 49184 | tf_op jit(solution)/shard_map/ppermute | solution.py:451
  33.8 0.0 collective-permute-done.10.refs_5_
  33.9 0.0 collective-permute-done.11.refs_6_
  33.9 1.5 %finish.1 = f32[2,3,8,64,128]{4,3,2,1,0:T(8,128)} custom-call(f32[2,3,8,64,128]{4,3,2,1,0:T(8,128)S(1)} %get-tuple-element.32.refs_0_, f32[4,3072]{1,0:T(4,128)S(1)} %collective-permute-done.8.refs_1_, f32[4,3072]{1,0:T(4,128)S(1)} %collective-permute-done.9.refs_2_, f32[2,3,3,64,128]{4,3,2,1,0:T(8,128)S(1)} %collective-permute-done.6.refs_2_.refs_3_, ...), custom_call_target="tpu_custom_call" | custom-call | flops 100000000 | bytes 5726208 | tf_op jit(solution)/shard_map/finish/pallas_call | solution.py:467
  (10 shorter events, 0.1 us)
Async XLA Ops:
  0.6 13.7 %collective-permute-start = (f32[3,8,32,128]{3,2,1,0:T(8,128)}, f32[3,8,32,128]{3,2,1,0:T(8,128)S(1)}, u32[]{:S(2)}, u32[]{:S(2)}) collective-permute-start(f32[3,8,32,128]{3,2,1,0:T(8,128)} %ref.1), channel_id=1, source_target_pairs={{0,64},{64,0},{1,65},{65,1},{2,66},{66,2},{3,67},{67,3},{4,68},{68... | collective-permute-start | bytes 1179656 | tf_op jit(solution)/shard_map/ppermute | solution.py:445
  4.0 1.0 %copy-start.1 = (f32[3,8,32,128]{3,2,1,0:T(8,128)S(1)}, f32[3,8,32,128]{3,2,1,0:T(8,128)}, u32[]{:S(2)}) copy-start(f32[3,8,32,128]{3,2,1,0:T(8,128)} %ref.1) | copy-start | bytes 1179652
  5.0 8.8 %copy-start.3 = (f32[1392,128]{1,0:T(8,128)S(1)}, f32[1392,128]{1,0:T(8,128)}, u32[]{:S(2)}) copy-start(f32[1392,128]{1,0:T(8,128)} %constant.2.clone.source) | copy-start | bytes 2138116
  5.0 8.8 %collective-permute-start.1 = (f32[3,3,32,128]{3,2,1,0:T(8,128)S(1)}, f32[3,3,32,128]{3,2,1,0:T(8,128)S(1)}, u32[]{:S(2)}, u32[]{:S(2)}) collective-permute-start(f32[3,3,32,128]{3,2,1,0:T(8,128)S(1)} %get-tuple-element.23), channel_id=1, source_target_pairs={{0,1},{1,2},{2,3},{3,0},{4,5},{5,6},{6,7},{7,4},{8,9},{9,10},{10,1... | collective-permute-start | bytes 442376 | tf_op jit(solution)/shard_map/ppermute | solution.py:445
  7.0 7.3 %copy-start.2 = (f32[3,8,32,128]{3,2,1,0:T(8,128)S(1)}, f32[3,8,32,128]{3,2,1,0:T(8,128)}, u32[]{:S(2)}) copy-start(f32[3,8,32,128]{3,2,1,0:T(8,128)} %ref.1) | copy-start | bytes 1179652
  7.0 6.9 %collective-permute-start.2 = (f32[3,3,32,128]{3,2,1,0:T(8,128)S(1)}, f32[3,3,32,128]{3,2,1,0:T(8,128)S(1)}, u32[]{:S(2)}, u32[]{:S(2)}) collective-permute-start(f32[3,3,32,128]{3,2,1,0:T(8,128)S(1)} %get-tuple-element.24), channel_id=1, source_target_pairs={{0,3},{1,0},{2,1},{3,2},{4,7},{5,4},{6,5},{7,6},{8,11},{9,8},{10,9... | collective-permute-start | bytes 442376 | tf_op jit(solution)/shard_map/ppermute | solution.py:445
  10.5 17.6 %collective-permute-start.6 = (f32[2,3,3,64,128]{4,3,2,1,0:T(8,128)S(1)}, f32[2,3,3,64,128]{4,3,2,1,0:T(8,128)S(1)}, u32[]{:S(2)}, u32[]{:S(2)}) collective-permute-start(f32[2,3,3,64,128]{4,3,2,1,0:T(8,128)S(1)} %get-tuple-element.28), channel_id=1, source_target_pairs={{0,1},{1,2},{2,3},{3,0},{4,5},{5,6},{6,7},{7,4},{8,9},{9,10},{10,1... | collective-permute-start | bytes 1769480 | tf_op jit(solution)/shard_map/ppermute | solution.py:445
  10.6 8.1 %copy-start = (f32[2,3,8,64,128]{4,3,2,1,0:T(8,128)S(1)}, f32[2,3,8,64,128]{4,3,2,1,0:T(8,128)}, u32[]{:S(2)}) copy-start(f32[2,3,8,64,128]{4,3,2,1,0:T(8,128)} %tests_ref.1) | copy-start | bytes 4718596
  10.6 20.5 %collective-permute-start.7 = (f32[2,3,3,64,128]{4,3,2,1,0:T(8,128)S(1)}, f32[2,3,3,64,128]{4,3,2,1,0:T(8,128)S(1)}, u32[]{:S(2)}, u32[]{:S(2)}) collective-permute-start(f32[2,3,3,64,128]{4,3,2,1,0:T(8,128)S(1)} %get-tuple-element.29), channel_id=1, source_target_pairs={{0,3},{1,0},{2,1},{3,2},{4,7},{5,4},{6,5},{7,6},{8,11},{9,8},{10,9... | collective-permute-start | bytes 1769480 | tf_op jit(solution)/shard_map/ppermute | solution.py:445
  13.9 9.5 %collective-permute-start.3 = (f32[2,3,3,32,128]{4,3,2,1,0:T(8,128)S(1)}, f32[2,3,3,32,128]{4,3,2,1,0:T(8,128)S(1)}, u32[]{:S(2)}, u32[]{:S(2)}) collective-permute-start(f32[2,3,3,32,128]{4,3,2,1,0:T(8,128)S(1)} %pack.1), channel_id=1, source_target_pairs={{0,64},{64,0},{1,65},{65,1},{2,66},{66,2},{3,67},{67,3},{4,68},{68... | collective-permute-start | bytes 884744 | tf_op jit(solution)/shard_map/ppermute | solution.py:445
  14.7 7.8 %collective-permute-start.4 = (f32[4,1536]{1,0:T(4,128)S(1)}, f32[4,1536]{1,0:T(4,128)S(1)}, u32[]{:S(2)}, u32[]{:S(2)}) collective-permute-start(f32[4,1536]{1,0:T(4,128)S(1)} %get-tuple-element.25), channel_id=1, source_target_pairs={{0,4},{8,12},{16,20},{24,28},{32,36},{40,44},{48,52},{56,60},{4,0}... | collective-permute-start | bytes 73736 | tf_op jit(solution)/shard_map/ppermute | solution.py:451
  14.8 7.7 %collective-permute-start.5 = (f32[4,1536]{1,0:T(4,128)S(1)}, f32[4,1536]{1,0:T(4,128)S(1)}, u32[]{:S(2)}, u32[]{:S(2)}) collective-permute-start(f32[4,1536]{1,0:T(4,128)S(1)} %get-tuple-element.26), channel_id=1, source_target_pairs={{4,8},{12,16},{20,24},{28,32},{36,40},{44,48},{52,56},{60,0},{8,4}... | collective-permute-start | bytes 73736 | tf_op jit(solution)/shard_map/ppermute | solution.py:451
  24.4 9.5 %collective-permute-start.10 = (f32[3,3,64,128]{3,2,1,0:T(8,128)S(1)}, f32[3,3,64,128]{3,2,1,0:T(8,128)S(1)}, u32[]{:S(2)}, u32[]{:S(2)}) collective-permute-start(f32[3,3,64,128]{3,2,1,0:T(8,128)S(1)} %get-tuple-element.36), channel_id=1, source_target_pairs={{0,1},{1,2},{2,3},{3,0},{4,5},{5,6},{6,7},{7,4},{8,9},{9,10},{10,1... | collective-permute-start | bytes 884744 | tf_op jit(solution)/shard_map/ppermute | solution.py:445
  24.5 9.3 %collective-permute-start.11 = (f32[3,3,64,128]{3,2,1,0:T(8,128)S(1)}, f32[3,3,64,128]{3,2,1,0:T(8,128)S(1)}, u32[]{:S(2)}, u32[]{:S(2)}) collective-permute-start(f32[3,3,64,128]{3,2,1,0:T(8,128)S(1)} %get-tuple-element.37), channel_id=1, source_target_pairs={{0,3},{1,0},{2,1},{3,2},{4,7},{5,4},{6,5},{7,6},{8,11},{9,8},{10,9... | collective-permute-start | bytes 884744 | tf_op jit(solution)/shard_map/ppermute | solution.py:445
  28.0 4.6 %collective-permute-start.8 = (f32[4,3072]{1,0:T(4,128)S(1)}, f32[4,3072]{1,0:T(4,128)S(1)}, u32[]{:S(2)}, u32[]{:S(2)}) collective-permute-start(f32[4,3072]{1,0:T(4,128)S(1)} %get-tuple-element.34), channel_id=1, source_target_pairs={{0,4},{8,12},{16,20},{24,28},{32,36},{40,44},{48,52},{56,60},{4,0}... | collective-permute-start | bytes 147464 | tf_op jit(solution)/shard_map/ppermute | solution.py:451
  28.1 5.7 %collective-permute-start.9 = (f32[4,3072]{1,0:T(4,128)S(1)}, f32[4,3072]{1,0:T(4,128)S(1)}, u32[]{:S(2)}, u32[]{:S(2)}) collective-permute-start(f32[4,3072]{1,0:T(4,128)S(1)} %get-tuple-element.35), channel_id=1, source_target_pairs={{4,8},{12,16},{20,24},{28,32},{36,40},{44,48},{52,56},{60,0},{8,4}... | collective-permute-start | bytes 147464 | tf_op jit(solution)/shard_map/ppermute | solution.py:451

commit v8 on v7

--- a/solution.py
+++ b/solution.py
@@ -408,8 +408,8 @@
         at = (3 * p + c) * lines
         held[p, c] = part_ref[p, c] + lines_in(raw[:, at : at + lines], land).reshape(nx, ny, n)
 
-    def leave(p, c):
-        copies.append(pltpu.make_async_copy(held.at[p, c], out_ref.at[p, c], sems.at[3 * p + c]))
+    def leave(*place):
+        copies.append(pltpu.make_async_copy(held.at[place], out_ref.at[place], sems.at[len(copies)]))
         copies[-1].start()
 
     for p in range(problems):
@@ -431,11 +431,10 @@
                     third = third + (sign * FIRST[d - 1]) * cross[0, h]
                 held[p, 1, i] = second
                 held[p, 2, i] = third
-        leave(p, 1)
-        leave(p, 2)
+        leave(p, pl.ds(1, 2))
     for p in range(problems):
         landed(p, 0)
-        leave(p, 0)
+    leave(pl.ds(0, problems), 0)
     for copy in copies:
         copy.wait()
 

time: 35.8 us -> 35.8 us (level)
  no operation moved by 1% of the time
where the time goes in v8:
time: 35.8 us; the launch traced here: 35.4 us
  starting transfers between devices  21.6 us (60%)
  Pallas kernels  9.94 us (28%)
  waiting for transfers between devices  2.09 us (6%)
  local copies, waits for them, and re-layouts  1.04 us (3%)
  between operations  0.76 us (2%)
    ppermute x8, starting transfers between devices, shifted(): lax.ppermute(block, axis, [(i, (i + distance) % count) for i in range(cou...  14.6 us
    pallas_call x10, Pallas kernels, run(): pl.pallas_call(body, in_specs=[pl.BlockSpec(memory_space=in_space)] * len...  9.94 us
    ppermute x4, starting transfers between devices, swapped(): return lax.ppermute(block, axis, pairs + [(b, a) for a, b in pairs])  6.99 us
    ppermute x4, waiting for transfers between devices, swapped(): return lax.ppermute(block, axis, pairs + [(b, a) for a, b in pairs])  1.2 us
    unnamed x8, local copies, waits for them, and re-layouts  1.04 us
    ppermute x8, waiting for transfers between devices, shifted(): lax.ppermute(block, axis, [(i, (i + distance) % count) for i in range(cou...  0.89 us
  transfers between devices with their start and end apart: 12, of which 2 were waited for; matrix products, arithmetic and copies ran while one was open for 0% of the time, Pallas kernels for 24%

profile of v8, /device:TPU:0, one launch (start us, length us, event | category | flops | bytes accessed | tf_op | source)
XLA Modules:
  0.0 35.4 jit_solution(5916560912760904260)
XLA Ops:
  0.6 3.4 %collective-permute-start = (f32[3,8,32,128]{3,2,1,0:T(8,128)}, f32[3,8,32,128]{3,2,1,0:T(8,128)S(1)}, u32[]{:S(2)}, u32[]{:S(2)}) collective-permute-start(f32[3,8,32,128]{3,2,1,0:T(8,128)} %ref.1), channel_id=1, source_target_pairs={{0,64},{64,0},{1,65},{65,1},{2,66},{66,2},{3,67},{67,3},{4,68},{68... | collective-permute-start | bytes 1179656 | tf_op jit(solution)/shard_map/ppermute | solution.py:444
  4.0 1.0 %copy-done.1 = f32[3,8,32,128]{3,2,1,0:T(8,128)S(1)} copy-done((f32[3,8,32,128]{3,2,1,0:T(8,128)S(1)}, f32[3,8,32,128]{3,2,1,0:T(8,128)}, u32[]{:S(2)}) %copy-start.1) | copy-done | bytes 393240
  5.0 2.0 %collective-permute-start.1 = (f32[3,3,32,128]{3,2,1,0:T(8,128)S(1)}, f32[3,3,32,128]{3,2,1,0:T(8,128)S(1)}, u32[]{:S(2)}, u32[]{:S(2)}) collective-permute-start(f32[3,3,32,128]{3,2,1,0:T(8,128)S(1)} %get-tuple-element.23), channel_id=1, source_target_pairs={{0,1},{1,2},{2,3},{3,0},{4,5},{5,6},{6,7},{7,4},{8,9},{9,10},{10,1... | collective-permute-start | bytes 442376 | tf_op jit(solution)/shard_map/ppermute | solution.py:444
  7.0 2.2 %collective-permute-start.2 = (f32[3,3,32,128]{3,2,1,0:T(8,128)S(1)}, f32[3,3,32,128]{3,2,1,0:T(8,128)S(1)}, u32[]{:S(2)}, u32[]{:S(2)}) collective-permute-start(f32[3,3,32,128]{3,2,1,0:T(8,128)S(1)} %get-tuple-element.24), channel_id=1, source_target_pairs={{0,3},{1,0},{2,1},{3,2},{4,7},{5,4},{6,5},{7,6},{8,11},{9,8},{10,9... | collective-permute-start | bytes 442376 | tf_op jit(solution)/shard_map/ppermute | solution.py:444
  9.2 1.3 %test_faces.1 = (f32[2,3,3,64,128]{4,3,2,1,0:T(8,128)S(1)}, f32[2,3,3,64,128]{4,3,2,1,0:T(8,128)S(1)}) custom-call(f32[2,3,8,64,128]{4,3,2,1,0:T(8,128)} %tests_ref.1), custom_call_target="tpu_custom_call" | custom-call | flops 100000000 | bytes 2752512 | tf_op jit(solution)/shard_map/test_faces/pallas_call | solution.py:466
  10.5 0.1 collective-permute-start.6
  10.6 0.0 copy-start
  10.6 3.2 %collective-permute-start.7 = (f32[2,3,3,64,128]{4,3,2,1,0:T(8,128)S(1)}, f32[2,3,3,64,128]{4,3,2,1,0:T(8,128)S(1)}, u32[]{:S(2)}, u32[]{:S(2)}) collective-permute-start(f32[2,3,3,64,128]{4,3,2,1,0:T(8,128)S(1)} %get-tuple-element.29), channel_id=1, source_target_pairs={{0,3},{1,0},{2,1},{3,2},{4,7},{5,4},{6,5},{7,6},{8,11},{9,8},{10,9... | collective-permute-start | bytes 1769480 | tf_op jit(solution)/shard_map/ppermute | solution.py:444
  13.9 0.0 collective-permute-done.1.first.refs_2_
  13.9 0.0 collective-permute-done.2.second.refs_3_
  13.9 0.4 %collective-permute-start.3 = (f32[2,3,3,32,128]{4,3,2,1,0:T(8,128)S(1)}, f32[2,3,3,32,128]{4,3,2,1,0:T(8,128)S(1)}, u32[]{:S(2)}, u32[]{:S(2)}) collective-permute-start(f32[2,3,3,32,128]{4,3,2,1,0:T(8,128)S(1)} %pack.1), channel_id=1, source_target_pairs={{0,64},{64,0},{1,65},{65,1},{2,66},{66,2},{3,67},{67,3},{4,68},{68... | collective-permute-start | bytes 884744 | tf_op jit(solution)/shard_map/ppermute | solution.py:444
  14.3 0.0 collective-permute-done.refs_1_
  14.3 0.4 %whole.1 = (f32[3,8,64,128]{3,2,1,0:T(8,128)S(1)}, f32[4,1536]{1,0:T(4,128)S(1)}, f32[4,1536]{1,0:T(4,128)S(1)}) custom-call(f32[3,8,32,128]{3,2,1,0:T(8,128)S(1)} %copy-done.2, f32[3,8,32,128]{3,2,1,0:T(8,128)S(1)} %collective-permute-done.refs_1_, f32[1392,128]{1,0:T(8,128)S(1)} %tables.1.refs_2_.refs_8_.refs_5_.refs_7_), custom_call_target="tpu_custom_call" | custom-call | flops 100000000 | bytes 2334720 | tf_op jit(solution)/shard_map/whole/pallas_call | solution.py:466
  14.7 0.1 collective-permute-start.4
  14.8 3.9 %collective-permute-start.5 = (f32[4,1536]{1,0:T(4,128)S(1)}, f32[4,1536]{1,0:T(4,128)S(1)}, u32[]{:S(2)}, u32[]{:S(2)}) collective-permute-start(f32[4,1536]{1,0:T(4,128)S(1)} %get-tuple-element.26), channel_id=1, source_target_pairs={{4,8},{12,16},{20,24},{28,32},{36,40},{44,48},{52,56},{60,0},{8,4}... | collective-permute-start | bytes 73736 | tf_op jit(solution)/shard_map/ppermute | solution.py:450
  18.7 3.8 %local.1 = (f32[3,8,64,128]{3,2,1,0:T(8,128)S(1)}, f32[2,3,8,64,128]{4,3,2,1,0:T(8,128)S(1)}, f32[8,3072]{1,0:T(8,128)S(1)}) custom-call(f32[3,8,64,128]{3,2,1,0:T(8,128)S(1)} %get-tuple-element.20.refs_0_, f32[2,3,8,64,128]{4,3,2,1,0:T(8,128)S(1)} %copy-done, f32[1392,128]{1,0:T(8,128)S(1)} %tables.1.refs_2_.refs_8_.refs_5_.refs_7_), custom_call_target="tpu_custom_call" | custom-call | flops 4000000000 | bytes 5529600 | tf_op jit(solution)/shard_map/local/pallas_call | solution.py:466
  22.5 0.0 collective-permute-done.4.refs_5_
  22.5 0.9 %collective-permute-done.3.refs_4_ = f32[2,3,3,32,128]{4,3,2,1,0:T(8,128)S(1)} collective-permute-done((f32[2,3,3,32,128]{4,3,2,1,0:T(8,128)S(1)}, f32[2,3,3,32,128]{4,3,2,1,0:T(8,128)S(1)}, u32[]{:S(2)}, u32[]{:S(2)}) %collective-permute-start.3) | collective-permute-done | bytes 294944 | tf_op jit(solution)/shard_map/ppermute | solution.py:444
  23.4 1.0 %step.1 = (f32[3,8,64,128]{3,2,1,0:T(8,128)S(1)}, f32[2,3,8,64,128]{4,3,2,1,0:T(8,128)S(1)}, f32[3,3,64,128]{3,2,1,0:T(8,128)S(1)}, f32[3,3,64,128]{3,2,1,0:T(8,128)S(1)}) custom-call(f32[3,8,64,128]{3,2,1,0:T(8,128)S(1)} %get-tuple-element.20.refs_0_, f32[3,8,64,128]{3,2,1,0:T(8,128)S(1)} %get-tuple-element.22.refs_1_, ...), custom_call_target="tpu_custom_call" | custom-call | flops 1000000000 | bytes 7446528 | tf_op jit(solution)/shard_map/step/pallas_call | solution.py:466
  24.4 0.2 collective-permute-start.10
  24.5 3.1 %collective-permute-start.11 = (f32[3,3,64,128]{3,2,1,0:T(8,128)S(1)}, f32[3,3,64,128]{3,2,1,0:T(8,128)S(1)}, u32[]{:S(2)}, u32[]{:S(2)}) collective-permute-start(f32[3,3,64,128]{3,2,1,0:T(8,128)S(1)} %get-tuple-element.37), channel_id=1, source_target_pairs={{0,3},{1,0},{2,1},{3,2},{4,7},{5,4},{6,5},{7,6},{8,11},{9,8},{10,9... | collective-permute-start | bytes 884744 | tf_op jit(solution)/shard_map/ppermute | solution.py:444
  27.7 0.4 %sums.1 = (f32[4,3072]{1,0:T(4,128)S(1)}, f32[4,3072]{1,0:T(4,128)S(1)}) custom-call(f32[2,3,8,64,128]{4,3,2,1,0:T(8,128)S(1)} %get-tuple-element.27.refs_1_.refs_0_, f32[8,3072]{1,0:T(8,128)S(1)} %get-tuple-element.33.refs_1_, f32[1392,128]{1,0:T(8,128)S(1)} %tables.1.refs_2_.refs_8_.refs_5_.refs_7_), custom_call_target="tpu_custom_call" | custom-call | flops 100000000 | bytes 2482176 | tf_op jit(solution)/shard_map/sums/pallas_call | solution.py:466
  28.0 0.1 collective-permute-start.8
  28.1 0.0 collective-permute-done.6.refs_2_.refs_3_
  28.1 3.0 %collective-permute-start.9 = (f32[4,3072]{1,0:T(4,128)S(1)}, f32[4,3072]{1,0:T(4,128)S(1)}, u32[]{:S(2)}, u32[]{:S(2)}) collective-permute-start(f32[4,3072]{1,0:T(4,128)S(1)} %get-tuple-element.35), channel_id=1, source_target_pairs={{4,8},{12,16},{20,24},{28,32},{36,40},{44,48},{52,56},{60,0},{8,4}... | collective-permute-start | bytes 147464 | tf_op jit(solution)/shard_map/ppermute | solution.py:450
  31.1 0.0 collective-permute-done.7.refs_3_.refs_4_
  31.1 1.5 %curl.1 = (f32[2,3,8,64,128]{4,3,2,1,0:T(8,128)S(1)}, f32[3,8,32,128]{3,2,1,0:T(8,128)}) custom-call(f32[2,3,8,64,128]{4,3,2,1,0:T(8,128)S(1)} %get-tuple-element.21.refs_0_, f32[2,3,8,64,128]{4,3,2,1,0:T(8,128)S(1)} %get-tuple-element.27.refs_1_.refs_0_, f32[2,3,3,64,128]{4,3,2,1,0:T(8,128)S(1)} %collective-permute-done.6.refs_2_.refs_3_, ...), custom_call_target="tpu_custom_call" | custom-call | flops 1000000000 | bytes 7790592 | tf_op jit(solution)/shard_map/curl/pallas_call | solution.py:466
  32.6 0.0 collective-permute-done.8.refs_1_
  32.7 1.2 %collective-permute-done.9.refs_2_ = f32[4,3072]{1,0:T(4,128)S(1)} collective-permute-done((f32[4,3072]{1,0:T(4,128)S(1)}, f32[4,3072]{1,0:T(4,128)S(1)}, u32[]{:S(2)}, u32[]{:S(2)}) %collective-permute-start.9) | collective-permute-done | bytes 49184 | tf_op jit(solution)/shard_map/ppermute | solution.py:450
  33.8 0.0 collective-permute-done.10.refs_5_
  33.9 0.0 collective-permute-done.11.refs_6_
  33.9 1.5 %finish.1 = f32[2,3,8,64,128]{4,3,2,1,0:T(8,128)} custom-call(f32[2,3,8,64,128]{4,3,2,1,0:T(8,128)S(1)} %get-tuple-element.32.refs_0_, f32[4,3072]{1,0:T(4,128)S(1)} %collective-permute-done.8.refs_1_, f32[4,3072]{1,0:T(4,128)S(1)} %collective-permute-done.9.refs_2_, f32[2,3,3,64,128]{4,3,2,1,0:T(8,128)S(1)} %collective-permute-done.6.refs_2_.refs_3_, ...), custom_call_target="tpu_custom_call" | custom-call | flops 100000000 | bytes 5726208 | tf_op jit(solution)/shard_map/finish/pallas_call | solution.py:466
  (10 shorter events, 0.1 us)
Async XLA Ops:
  0.6 13.7 %collective-permute-start = (f32[3,8,32,128]{3,2,1,0:T(8,128)}, f32[3,8,32,128]{3,2,1,0:T(8,128)S(1)}, u32[]{:S(2)}, u32[]{:S(2)}) collective-permute-start(f32[3,8,32,128]{3,2,1,0:T(8,128)} %ref.1), channel_id=1, source_target_pairs={{0,64},{64,0},{1,65},{65,1},{2,66},{66,2},{3,67},{67,3},{4,68},{68... | collective-permute-start | bytes 1179656 | tf_op jit(solution)/shard_map/ppermute | solution.py:444
  4.0 1.0 %copy-start.1 = (f32[3,8,32,128]{3,2,1,0:T(8,128)S(1)}, f32[3,8,32,128]{3,2,1,0:T(8,128)}, u32[]{:S(2)}) copy-start(f32[3,8,32,128]{3,2,1,0:T(8,128)} %ref.1) | copy-start | bytes 1179652
  5.0 8.8 %copy-start.3 = (f32[1392,128]{1,0:T(8,128)S(1)}, f32[1392,128]{1,0:T(8,128)}, u32[]{:S(2)}) copy-start(f32[1392,128]{1,0:T(8,128)} %constant.2.clone.source) | copy-start | bytes 2138116
  5.0 8.8 %collective-permute-start.1 = (f32[3,3,32,128]{3,2,1,0:T(8,128)S(1)}, f32[3,3,32,128]{3,2,1,0:T(8,128)S(1)}, u32[]{:S(2)}, u32[]{:S(2)}) collective-permute-start(f32[3,3,32,128]{3,2,1,0:T(8,128)S(1)} %get-tuple-element.23), channel_id=1, source_target_pairs={{0,1},{1,2},{2,3},{3,0},{4,5},{5,6},{6,7},{7,4},{8,9},{9,10},{10,1... | collective-permute-start | bytes 442376 | tf_op jit(solution)/shard_map/ppermute | solution.py:444
  7.0 7.3 %copy-start.2 = (f32[3,8,32,128]{3,2,1,0:T(8,128)S(1)}, f32[3,8,32,128]{3,2,1,0:T(8,128)}, u32[]{:S(2)}) copy-start(f32[3,8,32,128]{3,2,1,0:T(8,128)} %ref.1) | copy-start | bytes 1179652
  7.0 6.9 %collective-permute-start.2 = (f32[3,3,32,128]{3,2,1,0:T(8,128)S(1)}, f32[3,3,32,128]{3,2,1,0:T(8,128)S(1)}, u32[]{:S(2)}, u32[]{:S(2)}) collective-permute-start(f32[3,3,32,128]{3,2,1,0:T(8,128)S(1)} %get-tuple-element.24), channel_id=1, source_target_pairs={{0,3},{1,0},{2,1},{3,2},{4,7},{5,4},{6,5},{7,6},{8,11},{9,8},{10,9... | collective-permute-start | bytes 442376 | tf_op jit(solution)/shard_map/ppermute | solution.py:444
  10.5 17.6 %collective-permute-start.6 = (f32[2,3,3,64,128]{4,3,2,1,0:T(8,128)S(1)}, f32[2,3,3,64,128]{4,3,2,1,0:T(8,128)S(1)}, u32[]{:S(2)}, u32[]{:S(2)}) collective-permute-start(f32[2,3,3,64,128]{4,3,2,1,0:T(8,128)S(1)} %get-tuple-element.28), channel_id=1, source_target_pairs={{0,1},{1,2},{2,3},{3,0},{4,5},{5,6},{6,7},{7,4},{8,9},{9,10},{10,1... | collective-permute-start | bytes 1769480 | tf_op jit(solution)/shard_map/ppermute | solution.py:444
  10.6 8.1 %copy-start = (f32[2,3,8,64,128]{4,3,2,1,0:T(8,128)S(1)}, f32[2,3,8,64,128]{4,3,2,1,0:T(8,128)}, u32[]{:S(2)}) copy-start(f32[2,3,8,64,128]{4,3,2,1,0:T(8,128)} %tests_ref.1) | copy-start | bytes 4718596
  10.6 20.5 %collective-permute-start.7 = (f32[2,3,3,64,128]{4,3,2,1,0:T(8,128)S(1)}, f32[2,3,3,64,128]{4,3,2,1,0:T(8,128)S(1)}, u32[]{:S(2)}, u32[]{:S(2)}) collective-permute-start(f32[2,3,3,64,128]{4,3,2,1,0:T(8,128)S(1)} %get-tuple-element.29), channel_id=1, source_target_pairs={{0,3},{1,0},{2,1},{3,2},{4,7},{5,4},{6,5},{7,6},{8,11},{9,8},{10,9... | collective-permute-start | bytes 1769480 | tf_op jit(solution)/shard_map/ppermute | solution.py:444
  13.9 9.5 %collective-permute-start.3 = (f32[2,3,3,32,128]{4,3,2,1,0:T(8,128)S(1)}, f32[2,3,3,32,128]{4,3,2,1,0:T(8,128)S(1)}, u32[]{:S(2)}, u32[]{:S(2)}) collective-permute-start(f32[2,3,3,32,128]{4,3,2,1,0:T(8,128)S(1)} %pack.1), channel_id=1, source_target_pairs={{0,64},{64,0},{1,65},{65,1},{2,66},{66,2},{3,67},{67,3},{4,68},{68... | collective-permute-start | bytes 884744 | tf_op jit(solution)/shard_map/ppermute | solution.py:444
  14.7 7.8 %collective-permute-start.4 = (f32[4,1536]{1,0:T(4,128)S(1)}, f32[4,1536]{1,0:T(4,128)S(1)}, u32[]{:S(2)}, u32[]{:S(2)}) collective-permute-start(f32[4,1536]{1,0:T(4,128)S(1)} %get-tuple-element.25), channel_id=1, source_target_pairs={{0,4},{8,12},{16,20},{24,28},{32,36},{40,44},{48,52},{56,60},{4,0}... | collective-permute-start | bytes 73736 | tf_op jit(solution)/shard_map/ppermute | solution.py:450
  14.8 7.7 %collective-permute-start.5 = (f32[4,1536]{1,0:T(4,128)S(1)}, f32[4,1536]{1,0:T(4,128)S(1)}, u32[]{:S(2)}, u32[]{:S(2)}) collective-permute-start(f32[4,1536]{1,0:T(4,128)S(1)} %get-tuple-element.26), channel_id=1, source_target_pairs={{4,8},{12,16},{20,24},{28,32},{36,40},{44,48},{52,56},{60,0},{8,4}... | collective-permute-start | bytes 73736 | tf_op jit(solution)/shard_map/ppermute | solution.py:450
  24.4 9.5 %collective-permute-start.10 = (f32[3,3,64,128]{3,2,1,0:T(8,128)S(1)}, f32[3,3,64,128]{3,2,1,0:T(8,128)S(1)}, u32[]{:S(2)}, u32[]{:S(2)}) collective-permute-start(f32[3,3,64,128]{3,2,1,0:T(8,128)S(1)} %get-tuple-element.36), channel_id=1, source_target_pairs={{0,1},{1,2},{2,3},{3,0},{4,5},{5,6},{6,7},{7,4},{8,9},{9,10},{10,1... | collective-permute-start | bytes 884744 | tf_op jit(solution)/shard_map/ppermute | solution.py:444
  24.5 9.3 %collective-permute-start.11 = (f32[3,3,64,128]{3,2,1,0:T(8,128)S(1)}, f32[3,3,64,128]{3,2,1,0:T(8,128)S(1)}, u32[]{:S(2)}, u32[]{:S(2)}) collective-permute-start(f32[3,3,64,128]{3,2,1,0:T(8,128)S(1)} %get-tuple-element.37), channel_id=1, source_target_pairs={{0,3},{1,0},{2,1},{3,2},{4,7},{5,4},{6,5},{7,6},{8,11},{9,8},{10,9... | collective-permute-start | bytes 884744 | tf_op jit(solution)/shard_map/ppermute | solution.py:444
  28.0 4.6 %collective-permute-start.8 = (f32[4,3072]{1,0:T(4,128)S(1)}, f32[4,3072]{1,0:T(4,128)S(1)}, u32[]{:S(2)}, u32[]{:S(2)}) collective-permute-start(f32[4,3072]{1,0:T(4,128)S(1)} %get-tuple-element.34), channel_id=1, source_target_pairs={{0,4},{8,12},{16,20},{24,28},{32,36},{40,44},{48,52},{56,60},{4,0}... | collective-permute-start | bytes 147464 | tf_op jit(solution)/shard_map/ppermute | solution.py:450
  28.1 5.7 %collective-permute-start.9 = (f32[4,3072]{1,0:T(4,128)S(1)}, f32[4,3072]{1,0:T(4,128)S(1)}, u32[]{:S(2)}, u32[]{:S(2)}) collective-permute-start(f32[4,3072]{1,0:T(4,128)S(1)} %get-tuple-element.35), channel_id=1, source_target_pairs={{4,8},{12,16},{20,24},{28,32},{36,40},{44,48},{52,56},{60,0},{8,4}... | collective-permute-start | bytes 147464 | tf_op jit(solution)/shard_map/ppermute | solution.py:450

commit v9 on v7

--- a/solution.py
+++ b/solution.py
@@ -195,10 +195,6 @@
     pad[k, 0:8] = values[ny - 8 : ny]
     pad[k, 8 : 8 + ny] = values
     pad[k, 8 + ny : 16 + ny] = values[0:8]
-
-
-def tables_kernel(source, out):
-    out[...] = source[...]
 
 
 def faces_kernel(ref, low_ref, high_ref):
@@ -478,7 +474,7 @@
     whole_shape = (3, nx, ny, n)
     tests_shape = (problems, 3, nx, ny, n)
     other = shifted(velocity, "sec", 1)
-    (tables,) = run(tables_kernel, "tables", [jnp.asarray(constants)], [shape(*constants.shape)], bind=False)
+    tables = jnp.asarray(constants)
     v_low, v_high = run(faces_kernel, "flow_faces", [velocity], [shape(3, 3, half, n)] * 2, bind=False)
     v_own = [shifted(v_high, "gx", 1), shifted(v_low, "gx", -1)]
     t_low, t_high = run(

time: 35.8 us -> 35.7 us (level)
  waiting for transfers between devices: 2.09 us -> 1.42 us
  Pallas kernels: 9.93 us -> 10.5 us
    pallas_call x10 -> x9, Pallas kernels: 9.93 us -> 10.5 us  [run(): pl.pallas_call(body, in_specs=[pl.BlockSpec(memory_space=in_space)] * len...]
    ppermute x8, waiting for transfers between devices: 0.89 us -> 0.5 us  [shifted(): lax.ppermute(block, axis, [(i, (i + distance) % count) for i in range(cou...]
  transfers between devices with their start and end apart: 12 -> 12, of which waited for: 2 -> 2; matrix products, arithmetic and copies ran while one was open for 0% -> 0% of each run, Pallas kernels for 24% -> 26%
where the time goes in v9:
time: 35.7 us; the launch traced here: 35.3 us
  starting transfers between devices  21.6 us (61%)
  Pallas kernels  10.5 us (29%)
  waiting for transfers between devices  1.42 us (4%)
  local copies, waits for them, and re-layouts  1.04 us (3%)
  between operations  0.74 us (2%)
    ppermute x8, starting transfers between devices, shifted(): lax.ppermute(block, axis, [(i, (i + distance) % count) for i in range(cou...  14.6 us
    pallas_call x9, Pallas kernels, run(): pl.pallas_call(body, in_specs=[pl.BlockSpec(memory_space=in_space)] * len...  10.5 us
    ppermute x4, starting transfers between devices, swapped(): return lax.ppermute(block, axis, pairs + [(b, a) for a, b in pairs])  6.99 us
    unnamed x8, local copies, waits for them, and re-layouts  1.04 us
    ppermute x4, waiting for transfers between devices, swapped(): return lax.ppermute(block, axis, pairs + [(b, a) for a, b in pairs])  0.92 us
  transfers between devices with their start and end apart: 12, of which 2 were waited for; matrix products, arithmetic and copies ran while one was open for 0% of the time, Pallas kernels for 26%

profile of v9, /device:TPU:0, one launch (start us, length us, event | category | flops | bytes accessed | tf_op | source)
XLA Modules:
  0.0 35.3 jit_solution(12304382942167286179)
XLA Ops:
  0.6 0.0 copy-start
  0.6 3.4 %collective-permute-start = (f32[3,8,32,128]{3,2,1,0:T(8,128)}, f32[3,8,32,128]{3,2,1,0:T(8,128)S(1)}, u32[]{:S(2)}, u32[]{:S(2)}) collective-permute-start(f32[3,8,32,128]{3,2,1,0:T(8,128)} %ref.1), channel_id=1, source_target_pairs={{0,64},{64,0},{1,65},{65,1},{2,66},{66,2},{3,67},{67,3},{4,68},{68... | collective-permute-start | bytes 1179656 | tf_op jit(solution)/shard_map/ppermute | solution.py:441
  4.0 1.0 %copy-done.2 = f32[3,8,32,128]{3,2,1,0:T(8,128)S(1)} copy-done((f32[3,8,32,128]{3,2,1,0:T(8,128)S(1)}, f32[3,8,32,128]{3,2,1,0:T(8,128)}, u32[]{:S(2)}) %copy-start.2) | copy-done | bytes 393240
  5.1 2.0 %collective-permute-start.1 = (f32[3,3,32,128]{3,2,1,0:T(8,128)S(1)}, f32[3,3,32,128]{3,2,1,0:T(8,128)S(1)}, u32[]{:S(2)}, u32[]{:S(2)}) collective-permute-start(f32[3,3,32,128]{3,2,1,0:T(8,128)S(1)} %get-tuple-element.23), channel_id=1, source_target_pairs={{0,1},{1,2},{2,3},{3,0},{4,5},{5,6},{6,7},{7,4},{8,9},{9,10},{10,1... | collective-permute-start | bytes 442376 | tf_op jit(solution)/shard_map/ppermute | solution.py:441
  7.0 2.2 %collective-permute-start.2 = (f32[3,3,32,128]{3,2,1,0:T(8,128)S(1)}, f32[3,3,32,128]{3,2,1,0:T(8,128)S(1)}, u32[]{:S(2)}, u32[]{:S(2)}) collective-permute-start(f32[3,3,32,128]{3,2,1,0:T(8,128)S(1)} %get-tuple-element.24), channel_id=1, source_target_pairs={{0,3},{1,0},{2,1},{3,2},{4,7},{5,4},{6,5},{7,6},{8,11},{9,8},{10,9... | collective-permute-start | bytes 442376 | tf_op jit(solution)/shard_map/ppermute | solution.py:441
  9.3 1.3 %test_faces.1 = (f32[2,3,3,64,128]{4,3,2,1,0:T(8,128)S(1)}, f32[2,3,3,64,128]{4,3,2,1,0:T(8,128)S(1)}) custom-call(f32[2,3,8,64,128]{4,3,2,1,0:T(8,128)} %tests_ref.1), custom_call_target="tpu_custom_call" | custom-call | flops 100000000 | bytes 2752512 | tf_op jit(solution)/shard_map/test_faces/pallas_call | solution.py:463
  10.5 0.1 collective-permute-start.6
  10.6 3.2 %collective-permute-start.7 = (f32[2,3,3,64,128]{4,3,2,1,0:T(8,128)S(1)}, f32[2,3,3,64,128]{4,3,2,1,0:T(8,128)S(1)}, u32[]{:S(2)}, u32[]{:S(2)}) collective-permute-start(f32[2,3,3,64,128]{4,3,2,1,0:T(8,128)S(1)} %get-tuple-element.29), channel_id=1, source_target_pairs={{0,3},{1,0},{2,1},{3,2},{4,7},{5,4},{6,5},{7,6},{8,11},{9,8},{10,9... | collective-permute-start | bytes 1769480 | tf_op jit(solution)/shard_map/ppermute | solution.py:441
  13.8 0.0 collective-permute-done.1.first.refs_2_
  13.8 0.0 collective-permute-done.2.second.refs_3_
  13.9 0.4 %collective-permute-start.3 = (f32[2,3,3,32,128]{4,3,2,1,0:T(8,128)S(1)}, f32[2,3,3,32,128]{4,3,2,1,0:T(8,128)S(1)}, u32[]{:S(2)}, u32[]{:S(2)}) collective-permute-start(f32[2,3,3,32,128]{4,3,2,1,0:T(8,128)S(1)} %pack.1), channel_id=1, source_target_pairs={{0,64},{64,0},{1,65},{65,1},{2,66},{66,2},{3,67},{67,3},{4,68},{68... | collective-permute-start | bytes 884744 | tf_op jit(solution)/shard_map/ppermute | solution.py:441
  14.3 0.0 collective-permute-done.refs_1_
  14.3 0.4 %whole.1 = (f32[3,8,64,128]{3,2,1,0:T(8,128)S(1)}, f32[4,1536]{1,0:T(4,128)S(1)}, f32[4,1536]{1,0:T(4,128)S(1)}) custom-call(f32[3,8,32,128]{3,2,1,0:T(8,128)S(1)} %copy-done.3, f32[3,8,32,128]{3,2,1,0:T(8,128)S(1)} %collective-permute-done.refs_1_, f32[1392,128]{1,0:T(8,128)S(1)} %copy-done), custom_call_target="tpu_custom_call" | custom-call | flops 100000000 | bytes 2334720 | tf_op jit(solution)/shard_map/whole/pallas_call | solution.py:463
  14.7 0.1 collective-permute-start.4
  14.8 3.9 %collective-permute-start.5 = (f32[4,1536]{1,0:T(4,128)S(1)}, f32[4,1536]{1,0:T(4,128)S(1)}, u32[]{:S(2)}, u32[]{:S(2)}) collective-permute-start(f32[4,1536]{1,0:T(4,128)S(1)} %get-tuple-element.26), channel_id=1, source_target_pairs={{4,8},{12,16},{20,24},{28,32},{36,40},{44,48},{52,56},{60,0},{8,4}... | collective-permute-start | bytes 73736 | tf_op jit(solution)/shard_map/ppermute | solution.py:447
  18.6 4.2 %local.1 = (f32[3,8,64,128]{3,2,1,0:T(8,128)S(1)}, f32[2,3,8,64,128]{4,3,2,1,0:T(8,128)S(1)}, f32[8,3072]{1,0:T(8,128)S(1)}) custom-call(f32[3,8,64,128]{3,2,1,0:T(8,128)S(1)} %get-tuple-element.20.refs_0_, f32[2,3,8,64,128]{4,3,2,1,0:T(8,128)S(1)} %copy-done.1, f32[1392,128]{1,0:T(8,128)S(1)} %copy-done), custom_call_target="tpu_custom_call" | custom-call | flops 4000000000 | bytes 5529600 | tf_op jit(solution)/shard_map/local/pallas_call | solution.py:463
  22.8 0.0 collective-permute-done.4.refs_5_
  22.8 0.0 collective-permute-done.5.refs_6_
  22.9 0.5 %collective-permute-done.3.refs_4_ = f32[2,3,3,32,128]{4,3,2,1,0:T(8,128)S(1)} collective-permute-done((f32[2,3,3,32,128]{4,3,2,1,0:T(8,128)S(1)}, f32[2,3,3,32,128]{4,3,2,1,0:T(8,128)S(1)}, u32[]{:S(2)}, u32[]{:S(2)}) %collective-permute-start.3) | collective-permute-done | bytes 294944 | tf_op jit(solution)/shard_map/ppermute | solution.py:441
  23.3 0.9 %step.1 = (f32[3,8,64,128]{3,2,1,0:T(8,128)S(1)}, f32[2,3,8,64,128]{4,3,2,1,0:T(8,128)S(1)}, f32[3,3,64,128]{3,2,1,0:T(8,128)S(1)}, f32[3,3,64,128]{3,2,1,0:T(8,128)S(1)}) custom-call(f32[3,8,64,128]{3,2,1,0:T(8,128)S(1)} %get-tuple-element.20.refs_0_, f32[3,8,64,128]{3,2,1,0:T(8,128)S(1)} %get-tuple-element.22.refs_1_, ...), custom_call_target="tpu_custom_call" | custom-call | flops 1000000000 | bytes 7446528 | tf_op jit(solution)/shard_map/step/pallas_call | solution.py:463
  24.3 0.6 %collective-permute-start.10 = (f32[3,3,64,128]{3,2,1,0:T(8,128)S(1)}, f32[3,3,64,128]{3,2,1,0:T(8,128)S(1)}, u32[]{:S(2)}, u32[]{:S(2)}) collective-permute-start(f32[3,3,64,128]{3,2,1,0:T(8,128)S(1)} %get-tuple-element.36), channel_id=1, source_target_pairs={{0,1},{1,2},{2,3},{3,0},{4,5},{5,6},{6,7},{7,4},{8,9},{9,10},{10,1... | collective-permute-start | bytes 884744 | tf_op jit(solution)/shard_map/ppermute | solution.py:441
  24.9 2.7 %collective-permute-start.11 = (f32[3,3,64,128]{3,2,1,0:T(8,128)S(1)}, f32[3,3,64,128]{3,2,1,0:T(8,128)S(1)}, u32[]{:S(2)}, u32[]{:S(2)}) collective-permute-start(f32[3,3,64,128]{3,2,1,0:T(8,128)S(1)} %get-tuple-element.37), channel_id=1, source_target_pairs={{0,3},{1,0},{2,1},{3,2},{4,7},{5,4},{6,5},{7,6},{8,11},{9,8},{10,9... | collective-permute-start | bytes 884744 | tf_op jit(solution)/shard_map/ppermute | solution.py:441
  27.6 0.4 %sums.1 = (f32[4,3072]{1,0:T(4,128)S(1)}, f32[4,3072]{1,0:T(4,128)S(1)}) custom-call(f32[2,3,8,64,128]{4,3,2,1,0:T(8,128)S(1)} %get-tuple-element.27.refs_1_.refs_0_, f32[8,3072]{1,0:T(8,128)S(1)} %get-tuple-element.33.refs_1_, f32[1392,128]{1,0:T(8,128)S(1)} %copy-done), custom_call_target="tpu_custom_call" | custom-call | flops 100000000 | bytes 2482176 | tf_op jit(solution)/shard_map/sums/pallas_call | solution.py:463
  28.0 0.1 collective-permute-start.8
  28.1 0.0 collective-permute-done.6.refs_2_.refs_3_
  28.1 3.0 %collective-permute-start.9 = (f32[4,3072]{1,0:T(4,128)S(1)}, f32[4,3072]{1,0:T(4,128)S(1)}, u32[]{:S(2)}, u32[]{:S(2)}) collective-permute-start(f32[4,3072]{1,0:T(4,128)S(1)} %get-tuple-element.35), channel_id=1, source_target_pairs={{4,8},{12,16},{20,24},{28,32},{36,40},{44,48},{52,56},{60,0},{8,4}... | collective-permute-start | bytes 147464 | tf_op jit(solution)/shard_map/ppermute | solution.py:447
  31.0 0.0 collective-permute-done.7.refs_3_.refs_4_
  31.0 1.8 %curl.1 = (f32[2,3,8,64,128]{4,3,2,1,0:T(8,128)S(1)}, f32[3,8,32,128]{3,2,1,0:T(8,128)}) custom-call(f32[2,3,8,64,128]{4,3,2,1,0:T(8,128)S(1)} %get-tuple-element.21.refs_0_, f32[2,3,8,64,128]{4,3,2,1,0:T(8,128)S(1)} %get-tuple-element.27.refs_1_.refs_0_, f32[2,3,3,64,128]{4,3,2,1,0:T(8,128)S(1)} %collective-permute-done.6.refs_2_.refs_3_, ...), custom_call_target="tpu_custom_call" | custom-call | flops 1000000000 | bytes 7790592 | tf_op jit(solution)/shard_map/curl/pallas_call | solution.py:463
  32.8 0.0 collective-permute-done.8.refs_1_
  32.9 0.9 %collective-permute-done.9.refs_2_ = f32[4,3072]{1,0:T(4,128)S(1)} collective-permute-done((f32[4,3072]{1,0:T(4,128)S(1)}, f32[4,3072]{1,0:T(4,128)S(1)}, u32[]{:S(2)}, u32[]{:S(2)}) %collective-permute-start.9) | collective-permute-done | bytes 49184 | tf_op jit(solution)/shard_map/ppermute | solution.py:447
  33.8 0.0 collective-permute-done.10.refs_5_
  33.8 1.5 %finish.1 = f32[2,3,8,64,128]{4,3,2,1,0:T(8,128)} custom-call(f32[2,3,8,64,128]{4,3,2,1,0:T(8,128)S(1)} %get-tuple-element.32.refs_0_, f32[4,3072]{1,0:T(4,128)S(1)} %collective-permute-done.8.refs_1_, f32[4,3072]{1,0:T(4,128)S(1)} %collective-permute-done.9.refs_2_, f32[2,3,3,64,128]{4,3,2,1,0:T(8,128)S(1)} %collective-permute-done.6.refs_2_.refs_3_, ...), custom_call_target="tpu_custom_call" | custom-call | flops 100000000 | bytes 5726208 | tf_op jit(solution)/shard_map/finish/pallas_call | solution.py:463
  (9 shorter events, 0.1 us)
Async XLA Ops:
  0.6 13.7 %copy-start = (f32[1392,128]{1,0:T(8,128)S(1)}, f32[1392,128]{1,0:T(8,128)}, u32[]{:S(2)}) copy-start(f32[1392,128]{1,0:T(8,128)} %constant.2.clone.refs_2_.refs_8_.refs_5_.refs_7_) | copy-start | bytes 2138116
  0.6 13.6 %collective-permute-start = (f32[3,8,32,128]{3,2,1,0:T(8,128)}, f32[3,8,32,128]{3,2,1,0:T(8,128)S(1)}, u32[]{:S(2)}, u32[]{:S(2)}) collective-permute-start(f32[3,8,32,128]{3,2,1,0:T(8,128)} %ref.1), channel_id=1, source_target_pairs={{0,64},{64,0},{1,65},{65,1},{2,66},{66,2},{3,67},{67,3},{4,68},{68... | collective-permute-start | bytes 1179656 | tf_op jit(solution)/shard_map/ppermute | solution.py:441
  4.0 1.0 %copy-start.2 = (f32[3,8,32,128]{3,2,1,0:T(8,128)S(1)}, f32[3,8,32,128]{3,2,1,0:T(8,128)}, u32[]{:S(2)}) copy-start(f32[3,8,32,128]{3,2,1,0:T(8,128)} %ref.1) | copy-start | bytes 1179652
  5.0 9.3 %copy-start.3 = (f32[3,8,32,128]{3,2,1,0:T(8,128)S(1)}, f32[3,8,32,128]{3,2,1,0:T(8,128)}, u32[]{:S(2)}) copy-start(f32[3,8,32,128]{3,2,1,0:T(8,128)} %ref.1) | copy-start | bytes 1179652
  5.1 8.8 %collective-permute-start.1 = (f32[3,3,32,128]{3,2,1,0:T(8,128)S(1)}, f32[3,3,32,128]{3,2,1,0:T(8,128)S(1)}, u32[]{:S(2)}, u32[]{:S(2)}) collective-permute-start(f32[3,3,32,128]{3,2,1,0:T(8,128)S(1)} %get-tuple-element.23), channel_id=1, source_target_pairs={{0,1},{1,2},{2,3},{3,0},{4,5},{5,6},{6,7},{7,4},{8,9},{9,10},{10,1... | collective-permute-start | bytes 442376 | tf_op jit(solution)/shard_map/ppermute | solution.py:441
  7.0 11.6 %copy-start.1 = (f32[2,3,8,64,128]{4,3,2,1,0:T(8,128)S(1)}, f32[2,3,8,64,128]{4,3,2,1,0:T(8,128)}, u32[]{:S(2)}) copy-start(f32[2,3,8,64,128]{4,3,2,1,0:T(8,128)} %tests_ref.1) | copy-start | bytes 4718596
  7.0 6.8 %collective-permute-start.2 = (f32[3,3,32,128]{3,2,1,0:T(8,128)S(1)}, f32[3,3,32,128]{3,2,1,0:T(8,128)S(1)}, u32[]{:S(2)}, u32[]{:S(2)}) collective-permute-start(f32[3,3,32,128]{3,2,1,0:T(8,128)S(1)} %get-tuple-element.24), channel_id=1, source_target_pairs={{0,3},{1,0},{2,1},{3,2},{4,7},{5,4},{6,5},{7,6},{8,11},{9,8},{10,9... | collective-permute-start | bytes 442376 | tf_op jit(solution)/shard_map/ppermute | solution.py:441
  10.5 17.5 %collective-permute-start.6 = (f32[2,3,3,64,128]{4,3,2,1,0:T(8,128)S(1)}, f32[2,3,3,64,128]{4,3,2,1,0:T(8,128)S(1)}, u32[]{:S(2)}, u32[]{:S(2)}) collective-permute-start(f32[2,3,3,64,128]{4,3,2,1,0:T(8,128)S(1)} %get-tuple-element.28), channel_id=1, source_target_pairs={{0,1},{1,2},{2,3},{3,0},{4,5},{5,6},{6,7},{7,4},{8,9},{9,10},{10,1... | collective-permute-start | bytes 1769480 | tf_op jit(solution)/shard_map/ppermute | solution.py:441
  10.6 20.4 %collective-permute-start.7 = (f32[2,3,3,64,128]{4,3,2,1,0:T(8,128)S(1)}, f32[2,3,3,64,128]{4,3,2,1,0:T(8,128)S(1)}, u32[]{:S(2)}, u32[]{:S(2)}) collective-permute-start(f32[2,3,3,64,128]{4,3,2,1,0:T(8,128)S(1)} %get-tuple-element.29), channel_id=1, source_target_pairs={{0,3},{1,0},{2,1},{3,2},{4,7},{5,4},{6,5},{7,6},{8,11},{9,8},{10,9... | collective-permute-start | bytes 1769480 | tf_op jit(solution)/shard_map/ppermute | solution.py:441
  13.9 9.5 %collective-permute-start.3 = (f32[2,3,3,32,128]{4,3,2,1,0:T(8,128)S(1)}, f32[2,3,3,32,128]{4,3,2,1,0:T(8,128)S(1)}, u32[]{:S(2)}, u32[]{:S(2)}) collective-permute-start(f32[2,3,3,32,128]{4,3,2,1,0:T(8,128)S(1)} %pack.1), channel_id=1, source_target_pairs={{0,64},{64,0},{1,65},{65,1},{2,66},{66,2},{3,67},{67,3},{4,68},{68... | collective-permute-start | bytes 884744 | tf_op jit(solution)/shard_map/ppermute | solution.py:441
  14.7 8.2 %collective-permute-start.4 = (f32[4,1536]{1,0:T(4,128)S(1)}, f32[4,1536]{1,0:T(4,128)S(1)}, u32[]{:S(2)}, u32[]{:S(2)}) collective-permute-start(f32[4,1536]{1,0:T(4,128)S(1)} %get-tuple-element.25), channel_id=1, source_target_pairs={{0,4},{8,12},{16,20},{24,28},{32,36},{40,44},{48,52},{56,60},{4,0}... | collective-permute-start | bytes 73736 | tf_op jit(solution)/shard_map/ppermute | solution.py:447
  14.8 8.1 %collective-permute-start.5 = (f32[4,1536]{1,0:T(4,128)S(1)}, f32[4,1536]{1,0:T(4,128)S(1)}, u32[]{:S(2)}, u32[]{:S(2)}) collective-permute-start(f32[4,1536]{1,0:T(4,128)S(1)} %get-tuple-element.26), channel_id=1, source_target_pairs={{4,8},{12,16},{20,24},{28,32},{36,40},{44,48},{52,56},{60,0},{8,4}... | collective-permute-start | bytes 73736 | tf_op jit(solution)/shard_map/ppermute | solution.py:447
  24.3 9.5 %collective-permute-start.10 = (f32[3,3,64,128]{3,2,1,0:T(8,128)S(1)}, f32[3,3,64,128]{3,2,1,0:T(8,128)S(1)}, u32[]{:S(2)}, u32[]{:S(2)}) collective-permute-start(f32[3,3,64,128]{3,2,1,0:T(8,128)S(1)} %get-tuple-element.36), channel_id=1, source_target_pairs={{0,1},{1,2},{2,3},{3,0},{4,5},{5,6},{6,7},{7,4},{8,9},{9,10},{10,1... | collective-permute-start | bytes 884744 | tf_op jit(solution)/shard_map/ppermute | solution.py:441
  24.9 8.9 %collective-permute-start.11 = (f32[3,3,64,128]{3,2,1,0:T(8,128)S(1)}, f32[3,3,64,128]{3,2,1,0:T(8,128)S(1)}, u32[]{:S(2)}, u32[]{:S(2)}) collective-permute-start(f32[3,3,64,128]{3,2,1,0:T(8,128)S(1)} %get-tuple-element.37), channel_id=1, source_target_pairs={{0,3},{1,0},{2,1},{3,2},{4,7},{5,4},{6,5},{7,6},{8,11},{9,8},{10,9... | collective-permute-start | bytes 884744 | tf_op jit(solution)/shard_map/ppermute | solution.py:441
  28.0 4.9 %collective-permute-start.8 = (f32[4,3072]{1,0:T(4,128)S(1)}, f32[4,3072]{1,0:T(4,128)S(1)}, u32[]{:S(2)}, u32[]{:S(2)}) collective-permute-start(f32[4,3072]{1,0:T(4,128)S(1)} %get-tuple-element.34), channel_id=1, source_target_pairs={{0,4},{8,12},{16,20},{24,28},{32,36},{40,44},{48,52},{56,60},{4,0}... | collective-permute-start | bytes 147464 | tf_op jit(solution)/shard_map/ppermute | solution.py:447
  28.1 5.7 %collective-permute-start.9 = (f32[4,3072]{1,0:T(4,128)S(1)}, f32[4,3072]{1,0:T(4,128)S(1)}, u32[]{:S(2)}, u32[]{:S(2)}) collective-permute-start(f32[4,3072]{1,0:T(4,128)S(1)} %get-tuple-element.35), channel_id=1, source_target_pairs={{4,8},{12,16},{20,24},{28,32},{36,40},{44,48},{52,56},{60,0},{8,4}... | collective-permute-start | bytes 147464 | tf_op jit(solution)/shard_map/ppermute | solution.py:447
